TPU v7x, 32 devices: a whole 2x2x4 slice. The times are simulated.
32 devices in a mesh: tract: 2 (over y), sky: 4 (over x, core), band: 4 (over z).
Axes of the slice: x: 2, y: 2, z: 4, core: 2. Of those that a mesh axis runs over, the one named last changes fastest.
Arguments:
- patches: float32 [8, 32, 256, 256], P(('tract', 'band'), 'sky'), parts along dimension 0, may hold values from -6 to 6
- valid_rows: int32 [8, 32], P(('tract', 'band'), 'sky'), parts along dimension 0, may hold values from 64 to 256
- slot_owner: int32 [8, 32, 1], P(('tract', 'band'), 'sky'), parts along dimension 0, may hold values from 0 to 3; in each aligned block of 8 rows (0 to 7, 8 to 15, ..., all dimensions but the last counted through in order) at most 4 rows name the same one
- slot_local: int32 [8, 32], P(('tract', 'band'), 'sky'), parts along dimension 0, may hold values from 0 to 7
- slot_visit: int32 [8, 32], P(('tract', 'band'), 'sky'), parts along dimension 0, may hold values from 0 to 11
- basis_coef: float32 [8, 12, 21], P(('tract', 'band')), parts along dimension 0, may hold values from -1.25 to 1.25
- inv_var: float32 [8, 12], P(('tract', 'band')), parts along dimension 0, may hold values from 0.1 to 1
- kernel_x: bfloat16 [21, 41], replicated, may hold values from -1 to 1
- kernel_y: bfloat16 [21, 41], replicated, may hold values from -1 to 1
Outputs:
- band_coadd: float32 [8, 32, 256, 256], P(('tract', 'band'), 'sky'), parts along dimension 0
- detection: float32 [64, 256, 256], P(('tract', 'sky'), 'band'), parts along dimension 0
There are 2 independent parts, one for each index of `tract`. A program takes and returns all parts, laid end to end along the dimension named above; an argument that names none is the same for every part. Nothing has to cross between parts.
Inputs may be any that keep to these rules, and one draw needn't show every extreme that they name: `slot_owner`: among the pieces of one device no owner appears more than 4 times; some device gives exactly 4 pieces to one owner.
All inputs are finite; a program needn't handle non-finite values.
Results may differ from a plain program's by a relative error of at most 0.015.
Values may be sent and summed in bfloat16 or wider, within the bound.
No kernel may reach another device: no remote copies, remote signals or barrier semaphores. Data moves between devices by JAX's collectives and lax.ppermute only.
A program may use at most 128 MiB of HBM per device.

v0:
```python
import jax
import jax.numpy as jnp
from jax import lax
from jax.sharding import PartitionSpec as P

PATCH_DEV = 8


def tables(kernel_x, kernel_y, tile_side):
    kernel_len = kernel_x.shape[1]
    half_len = kernel_len // 2
    row_ids = lax.broadcasted_iota(jnp.int32, (tile_side, tile_side, kernel_len), 0)
    col_ids = lax.broadcasted_iota(jnp.int32, (tile_side, tile_side, kernel_len), 1)
    tap_ids = lax.broadcasted_iota(jnp.int32, (tile_side, tile_side, kernel_len), 2)
    picked = (col_ids - row_ids + half_len == tap_ids).astype(jnp.float32)
    across = jnp.einsum(
        "jma,ka->kjm", picked, kernel_x.astype(jnp.float32), precision=lax.Precision.HIGHEST
    ).astype(jnp.bfloat16)
    down_tables = jnp.einsum(
        "ima,ka->kim", picked, kernel_y.astype(jnp.float32), precision=lax.Precision.HIGHEST
    ).astype(jnp.bfloat16)
    return (across, down_tables)


def mixing_from(slot_info):
    return (slot_info[:, 0:1].astype(jnp.float32) * slot_info[:, 3:].astype(jnp.float32)).astype(
        jnp.bfloat16
    )


def membership(slot_info, tile_side):
    weight = slot_info[:, 0].astype(jnp.float32)
    row_count = slot_info[:, 1].astype(jnp.float32)
    local_ids = slot_info[:, 2].astype(jnp.float32)
    member = (local_ids[None, :] == jnp.arange(PATCH_DEV, dtype=jnp.float32)[:, None]).astype(
        jnp.float32
    )
    row_ids = jnp.arange(tile_side, dtype=jnp.float32)
    covered = weight[:, None] * (row_ids[None, :] < row_count[:, None]).astype(jnp.float32)
    coverage = jnp.dot(member, covered, precision=lax.Precision.HIGHEST)
    return (member, coverage)


def per_device(
    patches, valid_rows, slot_owner, slot_local, slot_visit, basis_coef, inv_var, kernel_x, kernel_y
):
    band_tiles = patches[0]
    slot_total = band_tiles.shape[0]
    tile_side = band_tiles.shape[1]
    sky_size = lax.axis_size("sky")
    capacity = max(2, 2 * slot_total // sky_size)
    across, down_tables = tables(kernel_x, kernel_y, tile_side)
    row_ids = lax.broadcasted_iota(jnp.int32, (slot_total, tile_side), 1)
    kept_rows = row_ids < valid_rows[0][:, None]
    masked = jnp.where(kept_rows[:, :, None], band_tiles, 0.0).astype(jnp.bfloat16)
    visit_ids = lax.broadcasted_iota(jnp.int32, (slot_total, basis_coef.shape[1]), 1)
    visit_pick = (slot_visit[0][:, None] == visit_ids).astype(jnp.float32)
    weight = jnp.dot(visit_pick, inv_var[0], precision=lax.Precision.HIGHEST).astype(jnp.bfloat16)
    coeffs = jnp.dot(visit_pick, basis_coef[0], precision=lax.Precision.HIGHEST).astype(
        jnp.bfloat16
    )
    owners = slot_owner[0][:, 0]
    same_owner = owners[:, None] == owners[None, :]
    earlier = lax.broadcasted_iota(jnp.int32, (slot_total, slot_total), 1) < lax.broadcasted_iota(
        jnp.int32, (slot_total, slot_total), 0
    )
    slot_rank = jnp.sum((same_owner & earlier).astype(jnp.int32), axis=1)
    position = owners * capacity + slot_rank
    slot_info = jnp.concatenate(
        [
            weight.astype(jnp.float32)[:, None],
            valid_rows[0].astype(jnp.float32)[:, None],
            slot_local[0].astype(jnp.float32)[:, None],
            coeffs.astype(jnp.float32),
        ],
        axis=1,
    ).astype(jnp.bfloat16)
    info_width = slot_info.shape[1]
    info_box = (
        jnp.zeros((sky_size * capacity, info_width), jnp.bfloat16)
        .at[position]
        .set(slot_info)
        .reshape(sky_size, capacity, info_width)
    )
    box_slots = sky_size * capacity
    tile_box = (
        jnp.zeros((box_slots, tile_side, tile_side), jnp.bfloat16)
        .at[position]
        .set(masked)
        .reshape(sky_size, capacity, tile_side, tile_side)
    )
    tiles_in, info_in = (
        lax.all_to_all(tile_box, "sky", split_axis=0, concat_axis=0, tiled=True),
        lax.all_to_all(info_box, "sky", split_axis=0, concat_axis=0, tiled=True),
    )
    flat_info = info_in.reshape(box_slots, info_width)
    member, coverage = membership(flat_info, tile_side)
    mixing_in = mixing_from(flat_info)
    patch_mix = (member[:, :, None] * mixing_in.astype(jnp.float32)[None, :, :]).astype(
        jnp.bfloat16
    )
    combined = jnp.einsum(
        "psk,sij->pkij",
        patch_mix,
        tiles_in.reshape(box_slots, tile_side, tile_side),
        preferred_element_type=jnp.float32,
    ).astype(jnp.bfloat16)
    section_one = jnp.einsum(
        "pkim,kjm->pkij", combined, across, preferred_element_type=jnp.float32
    ).astype(jnp.bfloat16)
    numerator = jnp.einsum(
        "kim,pkmj->pij", down_tables, section_one, preferred_element_type=jnp.float32
    )
    band_coadd = numerator / jnp.maximum(coverage, 1.0)[:, :, None]
    detection = lax.psum_scatter(
        band_coadd.astype(jnp.bfloat16), "band", scatter_dimension=1, tiled=True
    ).astype(jnp.float32)
    return (band_coadd[None], detection)


def solution(mesh):
    in_specs = (
        P(("tract", "band"), "sky", None, None),
        P(("tract", "band"), "sky"),
        P(("tract", "band"), "sky", None),
        P(("tract", "band"), "sky"),
        P(("tract", "band"), "sky"),
        P(("tract", "band"), None, None),
        P(("tract", "band"), None),
        P(),
        P(),
    )
    out_specs = (P(("tract", "band"), "sky", None, None), P(("tract", "sky"), "band", None))
    return jax.shard_map(
        per_device, mesh=mesh, in_specs=in_specs, out_specs=out_specs, check_vma=False
    )
```

profile of v0, /device:TPU:0, one launch (start us, length us, event | category | flops | bytes accessed | tf_op | source)
XLA Modules:
  0.0 135.2 jit_solution(6077922497058976813)
XLA Ops:
  7.2 0.7 convert_bitcast_fusion.2
  7.8 0.9 convert_reduce_fusion.3
  8.8 0.7 fusion.57
  9.4 0.7 convert_bitcast_fusion.3
  10.2 0.9 fusion.29
  11.2 0.9 convolution_convert_fusion.1
  12.1 1.2 scatter_custom_fusion
  13.4 4.2 %all-to-all-start = ((bf16[4,4,24]{2,1,0:T(4,128)(2,1)}), bf16[4,4,24]{2,1,0:T(4,128)(2,1)S(1)}, u32[]{:S(2)}, u32[]{:S(2)}) async-start(bf16[4,4,24]{2,1,0:T(4,128)(2,1)} %bitcast.14), calls=%async_computation | async-start | bytes 8192 | tf_op jit(solution)/shard_map/all_to_all | solution.py:94
  17.6 0.7 iota_compare_fusion.9
  18.3 1.8 %fusion.19 = bf16[8,256,256]{2,1,0:T(8,128)(2,1)S(1)} fusion(f32[1,8,256,256]{3,2,1,0:T(8,128)} %param.9, pred[8,256]{1,0:T(8,128)(4,1)S(1)} %iota_compare_fusion.9), kind=kLoop, calls=%fused_computation.22 | loop fusion | flops 524288 | bytes 3147776 | tf_op jit(solution)/shard_map/convert_element_type | solution.py:55
  20.3 0.9 scatter_fusion
  21.1 2.9 %copy.53 = bf16[4,4,256,256]{3,1,2,0:T(4,128)(2,1)} copy(bf16[4,4,256,256]{3,2,1,0:T(8,128)(2,1)S(1)} %bitcast.86) | data formatting | bytes 4194304 | tf_op jit(solution)/shard_map/reshape | solution.py:90
  24.1 3.6 %all-to-all-start.1 = ((bf16[4,4,256,256]{3,1,2,0:T(4,128)(2,1)}), bf16[4,4,256,256]{3,1,2,0:T(4,128)(2,1)S(1)}, u32[]{:S(2)}, u32[]{:S(2)}) async-start(bf16[4,4,256,256]{3,1,2,0:T(4,128)(2,1)} %copy.53), calls=%async_computation.1 | async-start | bytes 4194304 | tf_op jit(solution)/shard_map/all_to_all | solution.py:93
  27.8 3.8 %convert_bitcast_fusion.1 = bf16[21,256,256]{2,0,1:T(8,128)(2,1)} fusion(bf16[21,41]{1,0:T(8,128)(2,1)S(1)} %copy-done), kind=kOutput, calls=%fused_computation.14 | convolution fusion | flops 122290176 | bytes 2754234 | tf_op jit(solution)/shard_map/jma,ka->kjm/dot_general | solution.py:16
  31.5 3.8 %convert_bitcast_fusion = bf16[21,256,256]{2,0,1:T(8,128)(2,1)} fusion(bf16[21,41]{1,0:T(8,128)(2,1)S(1)} %copy-done.1), kind=kOutput, calls=%fused_computation.13 | convolution fusion | flops 122290176 | bytes 2754234 | tf_op jit(solution)/shard_map/ima,ka->kim/dot_general | solution.py:19
  35.8 17.6 %all-to-all-done.1 = bf16[4,4,256,256]{3,1,2,0:T(4,128)(2,1)S(1)} async-done(((bf16[4,4,256,256]{3,1,2,0:T(4,128)(2,1)}), bf16[4,4,256,256]{3,1,2,0:T(4,128)(2,1)S(1)}, u32[]{:S(2)}, u32[]{:S(2)}) %all-to-all-start.1) | async-done | bytes 2097184 | tf_op jit(solution)/shard_map/all_to_all | solution.py:93
  53.4 2.0 %copy.54 = bf16[4,4,256,256]{3,1,0,2:T(4,128)(2,1)} copy(bf16[4,4,256,256]{3,1,2,0:T(4,128)(2,1)S(1)} %all-to-all-done.1) | data formatting | bytes 4194304 | tf_op jit(solution)/shard_map/all_to_all | solution.py:93
  55.4 2.5 %reshape.149 = bf16[16,256,256,1]{2,0,1,3:T(8,128)(2,1)S(1)} reshape(bf16[4,4,256,256]{3,1,0,2:T(4,128)(2,1)} %copy.54) | data formatting | bytes 4194304 | tf_op jit(solution)/shard_map/reshape | solution.py:105
  58.0 11.4 %convolution_convert_fusion = bf16[8,21,256,256]{3,1,2,0:T(8,128)(2,1)} fusion(bf16[16,256,256,1]{2,0,1,3:T(8,128)(2,1)S(1)} %reshape.149, f32[16,21]{1,0:T(8,128)S(1)} %fusion.42, f32[8,16]{1,0:T(8,128)S(1)} %fusion.43), kind=kOutput, calls=%fused_computation.7 | convolution fusion | flops 363336960 | bytes 24119104 | tf_op jit(solution)/shard_map/psk,sij->pkij/dot_general | solution.py:102
  69.4 27.2 %bitcast_convert_fusion = (bf16[8,256,256]{1,2,0:T(8,128)(2,1)S(1)}, f32[8,256,256]{2,1,0:T(8,128)S(1)}) fusion(f32[8,256]{1,0:T(8,128)S(1)} %convolution_maximum_fusion, bf16[21,256,256]{2,0,1:T(8,128)(2,1)} %convert_bitcast_fusion, bf16[8,21,256,256]{3,1,2,0:T(8,128)(2,1)} %convolution_convert_fusion, bf16[21,256,256]{2,0,1:T(8,128)(2,1)} %convert_bitcast_fusion.1), kind=kOutput, calls=%fused_computation.19 | convolution fusion | flops 11286347776 | bytes 30679040 | tf_op jit(solution)/shard_map/kim,pkmj->pij/dot_general | solution.py:111
  96.6 1.8 %copy.58 = bf16[8,256,256]{2,0,1:T(8,128)(2,1)} copy(bf16[8,256,256]{1,2,0:T(8,128)(2,1)S(1)} %get-tuple-element.17) | data formatting | bytes 2097152 | tf_op jit(solution)/shard_map/convert_element_type | solution.py:116
  98.4 1.8 %copy.59 = f32[1,8,256,256]{3,2,1,0:T(8,128)} copy(f32[1,8,256,256]{2,3,1,0:T(8,128)S(1)} %bitcast.87) | data formatting | bytes 4194304
  100.2 26.3 %reduce-scatter.2.cloned.1.call-done = bf16[8,64,256]{2,0,1:T(8,128)(2,1)} async-done(((bf16[8,256,256]{2,0,1:T(8,128)(2,1)}), bf16[8,64,256]{2,0,1:T(8,128)(2,1)}) %reduce-scatter.2.cloned.1.call-update) | async-done | bytes 262160 | tf_op jit(solution)/shard_map/reduce_scatter | solution.py:115
  126.6 1.8 %copy.60 = f32[8,64,256]{2,1,0:T(8,128)} copy(bf16[8,64,256]{2,0,1:T(8,128)(2,1)} %reduce-scatter.2.cloned.1.call-done) | data formatting | bytes 786432
  (15 shorter events, 1.0 us)
Async XLA Ops:
  7.2 20.6 %copy-start = (bf16[21,41]{1,0:T(8,128)(2,1)S(1)}, bf16[21,41]{1,0:T(8,128)(2,1)}, u32[]{:S(2)}) copy-start(bf16[21,41]{1,0:T(8,128)(2,1)} %param.16) | copy-start | bytes 5170
  13.4 10.7 %all-to-all-start = ((bf16[4,4,24]{2,1,0:T(4,128)(2,1)}), bf16[4,4,24]{2,1,0:T(4,128)(2,1)S(1)}, u32[]{:S(2)}, u32[]{:S(2)}) async-start(bf16[4,4,24]{2,1,0:T(4,128)(2,1)} %bitcast.14), calls=%async_computation | async-start | bytes 8192 | tf_op jit(solution)/shard_map/all_to_all | solution.py:94
  24.1 29.3 %all-to-all-start.1 = ((bf16[4,4,256,256]{3,1,2,0:T(4,128)(2,1)}), bf16[4,4,256,256]{3,1,2,0:T(4,128)(2,1)S(1)}, u32[]{:S(2)}, u32[]{:S(2)}) async-start(bf16[4,4,256,256]{3,1,2,0:T(4,128)(2,1)} %copy.53), calls=%async_computation.1 | async-start | bytes 4194304 | tf_op jit(solution)/shard_map/all_to_all | solution.py:93
  27.7 3.8 %copy-start.1 = (bf16[21,41]{1,0:T(8,128)(2,1)S(1)}, bf16[21,41]{1,0:T(8,128)(2,1)}, u32[]{:S(2)}) copy-start(bf16[21,41]{1,0:T(8,128)(2,1)} %param.17) | copy-start | bytes 5170
  27.7 98.8 %reduce-scatter.2.cloned.1.call-start = ((), (), s32[]{:S(2)}) async-start(), calls=%async_computation.3 | async-start | bytes 1310720 | tf_op jit(solution)/shard_map/reduce_scatter | solution.py:115
Sparse Core Ops, SparseCore 0:
  98.5 27.9 reduce-scatter.1
where the time goes:
time: 136 us; the launch traced here: 135 us
  matrix products  48.1 us (35%)
  waiting for transfers between devices  44 us (32%)
  local copies, waits for them, and re-layouts  14.3 us (11%)
  between operations  14.1 us (10%)
  starting transfers between devices  7.86 us (6%)
  other arithmetic  6.9 us (5%)
    dot_general x1, matrix products, per_device(): jnp.einsum('kim,pkmj->pij', down_tables, section_one, preferred_element_t...  27.2 us
    reduce_scatter x1, waiting for transfers between devices, per_device(): lax.psum_scatter(band_coadd.astype(jnp.bfloat16), 'band', scatter_dimensi...  26.3 us
    all_to_all x1, waiting for transfers between devices, per_device(): lax.all_to_all(tile_box, 'sky', split_axis=0, concat_axis=0, tiled=True)  17.6 us
    dot_general x1, matrix products, per_device(): jnp.einsum('psk,sij->pkij', patch_mix, tiles_in.reshape(box_slots, tile_s...  11.4 us
    all_to_all x1, starting transfers between devices, per_device(): lax.all_to_all(info_box, 'sky', split_axis=0, concat_axis=0, tiled=True)  4.21 us
    dot_general x1, matrix products, tables(): jnp.einsum('ima,ka->kim', picked, kernel_y.astype(jnp.float32), precision...  3.76 us
    dot_general x1, matrix products, tables(): jnp.einsum('jma,ka->kjm', picked, kernel_x.astype(jnp.float32), precision...  3.75 us
    unnamed x6, local copies, waits for them, and re-layouts  3.62 us
  transfers between devices with their start and end apart: 3, of which 2 were waited for; matrix products, arithmetic and copies ran while one was open for 12% of the time, Pallas kernels for 0%

commit v1 on v0

v1 whole, which is shorter than its diff:
```python
import functools

import jax
import jax.numpy as jnp
import ml_dtypes
import numpy as np
from jax import lax
from jax.experimental import pallas as pl
from jax.experimental.pallas import tpu as pltpu
from jax.sharding import PartitionSpec as P

PATCH_DEV = 8
F32, BF16 = jnp.float32, jnp.bfloat16
VMEM_BYTES = 52 * 1024 * 1024


def round_up(value, multiple):
    return -(-value // multiple) * multiple


def wave_tables(side, kernel_len):
    half_len = kernel_len // 2
    count = -(-(side + half_len) // 2)
    omega = np.pi * (np.arange(count) + 0.5) / count
    sub, lane = round_up(count, 16), round_up(count, 128)

    def waves(points, width):
        out = np.zeros((len(points), 2 * width), np.float64)
        out[:, :count] = np.cos(np.outer(points, omega))
        out[:, width : width + count] = np.sin(np.outer(points, omega))
        return out

    pixels, taps = np.arange(side), np.arange(kernel_len) - half_len
    held = lambda a: np.ascontiguousarray(a).astype(ml_dtypes.bfloat16)
    return dict(
        sub=sub,
        lane=lane,
        scale=1.0 / (count * count),
        to_col=held(waves(pixels, lane)),
        to_row=held(waves(pixels, sub).T),
        from_col=held(waves(pixels, lane).T),
        from_row=held(waves(pixels, sub)),
        tap_col=held(waves(taps, lane)),
        tap_row=held(waves(taps, sub).T),
    )


def dot(a, b, contract=((1,), (0,))):
    return lax.dot_general(a, b, (contract, ((), ())), preferred_element_type=F32)


def convolve_kernel(plan, owner, valid, visit, patch, coef, inv_var, kx, ky, to_col, to_row, from_col, from_row,
                    tap_col, tap_row, *rest):
    outs, (row_waves, col_waves, back) = rest[:-3], rest[-3:]
    sub, lane, rows, nb = plan["sub"], plan["lane"], plan["rows"], plan["nb"]
    slot = pl.program_id(0)
    side = patch.shape[1]

    @pl.when(slot == 0)
    def _():
        row_waves[...] = dot(tap_row[...], ky[...], ((1,), (1,)))
        col_waves[...] = (dot(kx[...], tap_col[...]) * plan["scale"]).astype(BF16)
        band = lax.axis_index("band")
        for phase, shift in enumerate(plan["shifts"]):
            start = pl.multiple_of(lax.rem(band + shift, nb) * rows, rows)
            back[phase * rows : (phase + 1) * rows, :] = from_row[pl.ds(start, rows), :]

    basis = kx.shape[0]
    weight = jnp.full((1, basis), inv_var[0, visit[slot]], F32).astype(BF16).astype(F32)
    coeff = coef[pl.ds(visit[slot], 1), :].astype(BF16).astype(F32)
    mixing = (weight * coeff).astype(BF16).astype(F32)
    row_ids = lax.broadcasted_iota(jnp.int32, (side, side), 0)
    masked = jnp.where(row_ids < valid[slot], patch[0], 0.0).astype(BF16)
    col = dot(masked, to_col[...]).astype(BF16)
    mixed = (row_waves[...] * mixing).astype(BF16)
    parts = []
    for half in range(2):
        cols = slice(0, 2 * lane)
        parts.append(dot(to_row[half * sub : (half + 1) * sub, :], col))
    resp_c = dot(mixed[:sub], col_waves[...])
    resp_s = dot(mixed[sub:], col_waves[...])
    pa, pb, qa, qb = resp_c[:, :lane], resp_c[:, lane:], resp_s[:, :lane], resp_s[:, lane:]
    cc, cs, sc, ss = parts[0][:, :lane], parts[0][:, lane:], parts[1][:, :lane], parts[1][:, lane:]
    y_cc = (pa * cc + pb * cs + qa * sc + qb * ss).astype(BF16)
    y_cs = (pa * cs - pb * cc + qa * ss - qb * sc).astype(BF16)
    y_sc = (pa * sc + pb * ss - qa * cc - qb * cs).astype(BF16)
    y_ss = (pa * ss - pb * sc - qa * cs + qb * cc).astype(BF16)
    z_c = dot(y_cc, from_col[:lane, :]) + dot(y_cs, from_col[lane:, :])
    z_s = dot(y_sc, from_col[:lane, :]) + dot(y_ss, from_col[lane:, :])
    full = (
        dot(back[:, :sub], z_c.astype(BF16)) + dot(back[:, sub:], z_s.astype(BF16))
    ).astype(BF16)

    mine = owner[slot]
    rank = jnp.int32(0)
    for other in range(plan["slots"]):
        rank = rank + jnp.where((other < slot) & (owner[other] == mine), 1, 0).astype(jnp.int32)
    me = lax.axis_index("sky")
    if plan["single"]:
        targets = [(0, mine * plan["cap"] + rank, None)]
    else:
        targets = [(g, rank, (mine ^ me) == g) for g in range(plan["sky"])]
    for group, position, taken in targets:
        first = sum(plan["outs_of"][:group])

        def store(group=group, position=position, first=first):
            if plan["outs_of"][group] == 1:
                for phase in range(nb):
                    outs[first][phase, position] = full[phase * rows : (phase + 1) * rows, :]
            else:
                for phase in range(nb):
                    outs[first + phase][0, position] = full[phase * rows : (phase + 1) * rows, :]

        if taken is None:
            store()
        else:
            pl.when(taken)(store)


def sum_kernel(plan, phase, *refs):
    sky, nb, rows, cap, slots = plan["sky"], plan["nb"], plan["rows"], plan["cap"], plan["slots"]
    last = phase == nb - 1
    refs = list(refs)
    take = lambda n: [refs.pop(0) for _ in range(n)]
    metas = take(plan["n_meta"])
    (inv_var,) = take(1)
    boxes = take(len(plan["outs_of"]))
    arrived = take(nb - 1) if last else []
    if phase:
        take(1)
    band_out, extra, acc, cov, sem = refs
    me = lax.axis_index("sky")
    chunk = lax.rem(lax.axis_index("band") + plan["shifts"][phase], nb)
    acc[...] = jnp.zeros_like(acc)
    cov[...] = jnp.zeros_like(cov)
    row_ids = chunk * rows + lax.broadcasted_iota(jnp.int32, (rows, 128), 0)
    for source in range(sky):
        group, base = (0, source * cap) if plan["single"] else (source, 0)
        meta = lambda line, slot: (metas[0][source, line, slot] if plan["single"] else metas[source][line, slot])

        def step(slot, rank):
            here = meta(0, slot) == me

            @pl.when(here)
            def _():
                local = meta(1, slot)
                acc[local] += boxes[group][0, base + rank].astype(F32)
                weight = jnp.full((rows, 128), inv_var[0, meta(3, slot)], F32).astype(BF16).astype(F32)
                cov[local] += jnp.where(row_ids < meta(2, slot), weight, 0.0)

            return rank + jnp.where(here, 1, 0).astype(jnp.int32)

        lax.fori_loop(0, slots, step, jnp.int32(0))
    width = acc.shape[2]
    for patch in range(PATCH_DEV):
        factor = 1.0 / jnp.maximum(cov[patch], 1.0)
        for at in range(0, width, 128):
            value = acc[patch, :, at : at + 128] * factor
            acc[patch, :, at : at + 128] = value
            if last:
                for other in arrived:
                    value = value + other[patch, :, at : at + 128].astype(F32)
            extra[patch, :, at : at + 128] = value.astype(extra.dtype)
    copy = pltpu.make_async_copy(acc, band_out.at[:, pl.ds(pl.multiple_of(chunk * rows, rows), rows), :], sem)
    copy.start()
    copy.wait()


def per_device(patches, valid_rows, slot_owner, slot_local, slot_visit, basis_coef, inv_var, kernel_x, kernel_y):
    tiles = patches[0]
    slots, side, width = tiles.shape
    sky, nb = lax.axis_size("sky"), lax.axis_size("band")
    cap = max(2, 2 * slots // sky)
    rows = side // nb
    single = sky > 4 or sky & (sky - 1) != 0
    tables = wave_tables(side, kernel_x.shape[1])
    sub, lane = tables["sub"], tables["lane"]
    shifts = sorted(range(1, nb), key=lambda k: -min(k, nb - k)) + [0]
    near = 0 if single else min(2, sky)
    outs_of = [nb] if single else [1 if r < near else nb for r in range(sky)]
    box = (sky * cap if single else cap, rows, width)
    plan = dict(sub=sub, lane=lane, rows=rows, nb=nb, shifts=shifts, scale=tables["scale"], slots=slots, cap=cap,
                sky=sky, single=single, outs_of=outs_of, n_meta=1 if single else sky)
    meta = jnp.stack([slot_owner[0, :, 0], slot_local[0], valid_rows[0], slot_visit[0]])
    smem = pl.BlockSpec(memory_space=pltpu.SMEM)
    whole = lambda shape: pl.BlockSpec(shape, lambda *_: (0,) * len(shape))
    consts = [jnp.asarray(tables[n]) for n in ("to_col", "to_row", "from_col", "from_row", "tap_col", "tap_row")]
    out_shapes = []
    for n in outs_of:
        out_shapes += [jax.ShapeDtypeStruct((nb,) + box, BF16)] if n == 1 else [
            jax.ShapeDtypeStruct((1,) + box, BF16)] * nb
    coef, basis = basis_coef[0], kernel_x.shape[0]
    sent = pl.pallas_call(
        functools.partial(convolve_kernel, plan),
        grid=(slots,),
        out_shape=out_shapes,
        in_specs=[smem, smem, smem, pl.BlockSpec((1, side, width), lambda s: (s, 0, 0)), whole(coef.shape), smem,
                  whole(kernel_x.shape), whole(kernel_y.shape)] + [whole(c.shape) for c in consts],
        out_specs=[whole(o.shape) for o in out_shapes],
        scratch_shapes=[pltpu.VMEM((2 * sub, basis), F32), pltpu.VMEM((basis, 2 * lane), BF16),
                        pltpu.VMEM((side, 2 * sub), BF16)],
        compiler_params=pltpu.CompilerParams(vmem_limit_bytes=VMEM_BYTES),
        cost_estimate=pl.CostEstimate(flops=slots * 22 * side**3, bytes_accessed=slots * side * side * 6,
                                      transcendentals=0),
        name="convolve",
    )(slot_owner[0, :, 0], valid_rows[0], slot_visit[0], tiles, coef, inv_var, kernel_x, kernel_y, *consts)

    if single:
        metas = [lax.all_gather(meta, "sky")]
        boxes = [[lax.all_to_all(s, "sky", split_axis=1, concat_axis=1, tiled=True)] for s in sent]
        boxes = [[b[0], 0] for b in boxes]
        at_phase = lambda phase: [boxes[phase]]
    else:
        swap = lambda a, r: a if r == 0 else lax.ppermute(a, "sky", [(i, i ^ r) for i in range(sky)])
        metas = [swap(meta, r) for r in range(sky)]
        groups, first = [], 0
        for n in outs_of:
            groups.append(sent[first : first + n])
            first += n
        moved = [None] * sky
        for r in range(near):
            moved[r] = [swap(groups[r][0], r)]
        for r in range(near, sky):
            moved[r] = []
        for phase in range(nb):
            for r in range(near, sky):
                moved[r].append(swap(groups[r][phase], r))
        at_phase = lambda phase: [(moved[r][0], phase) if r < near else (moved[r][phase], 0) for r in range(sky)]

    band_buf, arrived, detection = None, [], None
    band_shape = jax.ShapeDtypeStruct((PATCH_DEV, side, width), F32)
    hbm = pl.BlockSpec(memory_space=pl.ANY)
    for phase in range(nb):
        last = phase == nb - 1
        pieces = at_phase(phase)
        args = metas + [inv_var] + [b for b, _ in pieces] + (arrived if last else [])
        specs = [smem] * (len(metas) + 1)
        specs += [pl.BlockSpec((1,) + box, lambda i, at=at: (at, 0, 0, 0)) for _, at in pieces]
        chunk_shape = (PATCH_DEV, rows, width)
        specs += [whole(chunk_shape)] * (len(arrived) if last else 0)
        aliases = {}
        if phase:
            aliases = {len(args): 0}
            args, specs = args + [band_buf], specs + [hbm]
        band_buf, extra = pl.pallas_call(
            functools.partial(sum_kernel, plan, phase),
            grid=(1,),
            out_shape=[band_shape, jax.ShapeDtypeStruct(chunk_shape, F32 if last else BF16)],
            in_specs=specs,
            out_specs=[hbm, whole(chunk_shape)],
            scratch_shapes=[pltpu.VMEM(chunk_shape, F32), pltpu.VMEM((PATCH_DEV, rows, 128), F32),
                            pltpu.SemaphoreType.DMA],
            input_output_aliases=aliases,
            compiler_params=pltpu.CompilerParams(vmem_limit_bytes=VMEM_BYTES),
            cost_estimate=pl.CostEstimate(flops=4 * PATCH_DEV * rows * width, bytes_accessed=12 * PATCH_DEV * rows * width,
                                          transcendentals=0),
            name="add_up",
        )(*args)
        if last:
            detection = extra
        else:
            shift = shifts[phase]
            arrived.append(lax.ppermute(extra, "band", [(b, (b + shift) % nb) for b in range(nb)]))
    return (band_buf[None], detection)


def solution(mesh):
    in_specs = (
        P(("tract", "band"), "sky", None, None),
        P(("tract", "band"), "sky"),
        P(("tract", "band"), "sky", None),
        P(("tract", "band"), "sky"),
        P(("tract", "band"), "sky"),
        P(("tract", "band"), None, None),
        P(("tract", "band"), None),
        P(),
        P(),
    )
    out_specs = (P(("tract", "band"), "sky", None, None), P(("tract", "sky"), "band", None))
    return jax.shard_map(per_device, mesh=mesh, in_specs=in_specs, out_specs=out_specs, check_vma=False)
```

time: 136 us -> 68.5 us (0.50)
  matrix products: 48.1 us -> 0 us
  waiting for transfers between devices: 44 us -> 17.7 us
  Pallas kernels: 0 us -> 20.5 us
  between operations: 14.1 us -> 0.7 us
  starting transfers between devices: 7.86 us -> 18.7 us
  other arithmetic: 6.9 us -> 0.01 us
  local copies, waits for them, and re-layouts: 14.3 us -> 10.4 us
    dot_general x7 -> x0, matrix products: 48.1 us -> none  [the longest x1 27.2 us: per_device(): jnp.einsum('kim,pkmj->pij', down_tables, section_one, preferred_element_t...]
    reduce_scatter x1 -> x0, waiting for transfers between devices: 26.3 us -> none  [per_device(): lax.psum_scatter(band_coadd.astype(jnp.bfloat16), 'band', scatter_dimensi...]
    pallas_call x0 -> x5, Pallas kernels: none -> 20.5 us  [the longest x1 11.1 us: per_device(): pl.pallas_call(functools.partial(convolve_kernel, plan), grid=(slots,), o...]
    ppermute x0 -> x15, starting transfers between devices: none -> 18.7 us  [the longest x12 11.2 us: per_device(): lax.ppermute(a, 'sky', [(i, i ^ r) for i in range(sky)])]
    ppermute x0 -> x15, waiting for transfers between devices: none -> 17.7 us  [the longest x12 11.6 us: per_device(): lax.ppermute(a, 'sky', [(i, i ^ r) for i in range(sky)])]
    all_to_all x2 -> x0, waiting for transfers between devices: 17.6 us -> none  [the longest x1 17.6 us: per_device(): lax.all_to_all(tile_box, 'sky', split_axis=0, concat_axis=0, tiled=True)]
    all_to_all x2 -> x0, starting transfers between devices: 7.82 us -> none  [the longest x1 4.21 us: per_device(): lax.all_to_all(info_box, 'sky', split_axis=0, concat_axis=0, tiled=True)]
    unnamed x6 -> x31, local copies, waits for them, and re-layouts: 3.62 us -> 10.4 us
  transfers between devices with their start and end apart: 3 -> 15, of which waited for: 2 -> 6; matrix products, arithmetic and copies ran while one was open for 12% -> 0% of each run, Pallas kernels for 0% -> 9%
where the time goes in v1:
time: 68.5 us; the launch traced here: 67.9 us
  Pallas kernels  20.5 us (30%)
  starting transfers between devices  18.7 us (27%)
  waiting for transfers between devices  17.7 us (26%)
  local copies, waits for them, and re-layouts  10.4 us (15%)
  between operations  0.7 us (1%)
    ppermute x12, waiting for transfers between devices, per_device(): lax.ppermute(a, 'sky', [(i, i ^ r) for i in range(sky)])  11.6 us
    ppermute x12, starting transfers between devices, per_device(): lax.ppermute(a, 'sky', [(i, i ^ r) for i in range(sky)])  11.2 us
    pallas_call x1, Pallas kernels, per_device(): pl.pallas_call(functools.partial(convolve_kernel, plan), grid=(slots,), o...  11.1 us
    unnamed x31, local copies, waits for them, and re-layouts  10.4 us
    pallas_call x4, Pallas kernels, per_device(): pl.pallas_call(functools.partial(sum_kernel, plan, phase), grid=(1,), out...  9.43 us
    ppermute x3, starting transfers between devices, per_device(): lax.ppermute(extra, 'band', [(b, (b + shift) % nb) for b in range(nb)])  7.5 us
    ppermute x3, waiting for transfers between devices, per_device(): lax.ppermute(extra, 'band', [(b, (b + shift) % nb) for b in range(nb)])  6.09 us
  transfers between devices with their start and end apart: 15, of which 6 were waited for; matrix products, arithmetic and copies ran while one was open for 0% of the time, Pallas kernels for 9%

profile of v1, /device:TPU:0, one launch (start us, length us, event | category | flops | bytes accessed | tf_op | source)
XLA Modules:
  0.0 67.9 jit_solution(11599601917085608008)
XLA Ops:
  5.3 0.9 %copy-done.9 = bf16[256,512]{1,0:T(8,128)(2,1)S(1)} copy-done((bf16[256,512]{1,0:T(8,128)(2,1)S(1)}, bf16[256,512]{1,0:T(8,128)(2,1)}, u32[]{:S(2)}) %copy-start.9) | copy-done | bytes 262168
  6.3 0.9 %copy-done.10 = bf16[256,288]{1,0:T(8,128)(2,1)S(1)} copy-done((bf16[256,288]{1,0:T(8,128)(2,1)S(1)}, bf16[256,288]{1,0:T(8,128)(2,1)}, u32[]{:S(2)}) %copy-start.10) | copy-done | bytes 147480
  7.2 0.9 %copy-done.11 = bf16[288,256]{1,0:T(8,128)(2,1)S(1)} copy-done((bf16[288,256]{1,0:T(8,128)(2,1)S(1)}, bf16[288,256]{1,0:T(8,128)(2,1)}, u32[]{:S(2)}) %copy-start.11) | copy-done | bytes 147480
  8.1 0.9 %copy-done.12 = bf16[288,41]{1,0:T(8,128)(2,1)S(1)} copy-done((bf16[288,41]{1,0:T(8,128)(2,1)S(1)}, bf16[288,41]{1,0:T(8,128)(2,1)}, u32[]{:S(2)}) %copy-start.12) | copy-done | bytes 23640
  9.0 0.8 %copy-done.13 = bf16[41,512]{1,0:T(8,128)(2,1)S(1)} copy-done((bf16[41,512]{1,0:T(8,128)(2,1)S(1)}, bf16[41,512]{1,0:T(8,128)(2,1)}, u32[]{:S(2)}) %copy-start.13) | copy-done | bytes 42008
  9.8 11.1 %convolve.1 = (bf16[4,4,64,256]{3,2,1,0:T(8,128)(2,1)}, bf16[4,4,64,256]{3,2,1,0:T(8,128)(2,1)}, bf16[1,4,64,256]{3,2,1,0:T(8,128)(2,1)S(1)}, bf16[1,4,64,256]{3...) custom-call(s32[8]{0:T(128)S(1)} %bitcast.12, ...), custom_call_target="tpu_custom_call" | custom-call | flops 2952790016 | bytes 3145728 | tf_op jit(solution)/shard_map/convolve/pallas_call | solution.py:193
  21.3 2.5 %collective-permute-start.6 = (bf16[1,4,64,256]{3,2,1,0:T(8,128)(2,1)S(1)}, bf16[1,4,64,256]{3,2,1,0:T(8,128)(2,1)S(1)}, u32[]{:S(2)}, u32[]{:S(2)}) collective-permute-start(bf16[1,4,64,256]{3,2,1,0:T(8,128)(2,1)S(1)} %get-tuple-element.24), channel_id=1, source_target_pairs={{0,8},{4,12},{8,0},{12,4},{1,9},{5,13},{9,1},{13,5},{2,10},{6,14},... | collective-permute-start | bytes 393224 | tf_op jit(solution)/shard_map/ppermute | solution.py:214
  24.0 1.7 %collective-permute-start.2 = (s32[4,8]{1,0:T(4,128)S(1)}, s32[4,8]{1,0:T(4,128)S(1)}, u32[]{:S(2)}, u32[]{:S(2)}) collective-permute-start(s32[4,8]{1,0:T(4,128)S(1)} %pad_add_fusion.refs_0_), channel_id=1, source_target_pairs={{0,12},{4,8},{8,4},{12,0},{1,13},{5,9},{9,5},{13,1},{2,14},{6,10},... | collective-permute-start | bytes 392 | tf_op jit(solution)/shard_map/ppermute | solution.py:214
  25.8 4.8 %collective-permute-done.2.refs_3_ = s32[4,8]{1,0:T(4,128)S(1)} collective-permute-done((s32[4,8]{1,0:T(4,128)S(1)}, s32[4,8]{1,0:T(4,128)S(1)}, u32[]{:S(2)}, u32[]{:S(2)}) %collective-permute-start.2) | collective-permute-done | bytes 160 | tf_op jit(solution)/shard_map/ppermute | solution.py:214
  30.9 1.8 %collective-permute-start.9 = (bf16[1,4,64,256]{3,2,1,0:T(8,128)(2,1)S(1)}, bf16[1,4,64,256]{3,2,1,0:T(8,128)(2,1)S(1)}, u32[]{:S(2)}, u32[]{:S(2)}) collective-permute-start(bf16[1,4,64,256]{3,2,1,0:T(8,128)(2,1)S(1)} %get-tuple-element.27), channel_id=1, source_target_pairs={{0,8},{4,12},{8,0},{12,4},{1,9},{5,13},{9,1},{13,5},{2,10},{6,14},... | collective-permute-start | bytes 393224 | tf_op jit(solution)/shard_map/ppermute | solution.py:214
  33.2 0.9 %collective-permute-start.12 = (bf16[1,4,64,256]{3,2,1,0:T(8,128)(2,1)S(1)}, bf16[1,4,64,256]{3,2,1,0:T(8,128)(2,1)S(1)}, u32[]{:S(2)}, u32[]{:S(2)}) collective-permute-start(bf16[1,4,64,256]{3,2,1,0:T(8,128)(2,1)S(1)} %get-tuple-element.31), channel_id=1, source_target_pairs={{0,8},{4,12},{8,0},{12,4},{1,9},{5,13},{9,1},{13,5},{2,10},{6,14},... | collective-permute-start | bytes 393224 | tf_op jit(solution)/shard_map/ppermute | solution.py:214
  34.9 1.2 %copy-done = bf16[4,4,64,256]{3,2,1,0:T(8,128)(2,1)S(1)} copy-done((bf16[4,4,64,256]{3,2,1,0:T(8,128)(2,1)S(1)}, bf16[4,4,64,256]{3,2,1,0:T(8,128)(2,1)}, u32[]{:S(2)}) %copy-start) | copy-done | bytes 524312
  36.1 2.1 %add_up.4 = (f32[8,256,256]{2,1,0:T(8,128)}, bf16[8,64,256]{2,1,0:T(8,128)(2,1)S(1)}) custom-call(s32[4,8]{1,0:T(4,128)S(1)} %pad_add_fusion.refs_0_, s32[4,8]{1,0:T(4,128)S(1)} %collective-permute-done.refs_1_, s32[4,8]{1,0:T(4,128)S(1)} %collective-permute-done.1.refs_2_, s32[4,8]{1,0:T(4,128)S(1)} %collective-permute-done.2.refs_3_, ...), custom_call_target="tpu_custom_call" | custom-call | flops 524288 | bytes 1572864 | tf_op jit(solution)/shard_map/add_up/pallas_call | solution.py:245
  38.2 2.6 %collective-permute-start.8 = (bf16[8,64,256]{2,1,0:T(8,128)(2,1)S(1)}, bf16[8,64,256]{2,1,0:T(8,128)(2,1)S(1)}, u32[]{:S(2)}, u32[]{:S(2)}) collective-permute-start(bf16[8,64,256]{2,1,0:T(8,128)(2,1)S(1)} %get-tuple-element.26), channel_id=1, source_target_pairs={{0,2},{1,3},{2,0},{3,1},{4,6},{5,7},{6,4},{7,5},{8,10},{9,11},{10,... | collective-permute-start | bytes 786440 | tf_op jit(solution)/shard_map/ppermute | solution.py:263
  40.8 2.1 %add_up.5 = (f32[8,256,256]{2,1,0:T(8,128)}, bf16[8,64,256]{2,1,0:T(8,128)(2,1)S(1)}) custom-call(s32[4,8]{1,0:T(4,128)S(1)} %pad_add_fusion.refs_0_, s32[4,8]{1,0:T(4,128)S(1)} %collective-permute-done.refs_1_, s32[4,8]{1,0:T(4,128)S(1)} %collective-permute-done.1.refs_2_, ...), custom_call_target="tpu_custom_call", output_to_operand_aliasing={{0}: (9, {})} | custom-call | flops 524288 | bytes 1572864 | tf_op jit(solution)/shard_map/add_up/pallas_call | solution.py:245
  42.9 1.6 %collective-permute-start.11 = (bf16[8,64,256]{2,1,0:T(8,128)(2,1)S(1)}, bf16[8,64,256]{2,1,0:T(8,128)(2,1)S(1)}, u32[]{:S(2)}, u32[]{:S(2)}) collective-permute-start(bf16[8,64,256]{2,1,0:T(8,128)(2,1)S(1)} %get-tuple-element.30), channel_id=1, source_target_pairs={{0,1},{1,2},{2,3},{3,0},{4,5},{5,6},{6,7},{7,4},{8,9},{9,10},{10,1... | collective-permute-start | bytes 786440 | tf_op jit(solution)/shard_map/ppermute | solution.py:263
  44.6 2.1 %add_up.6 = (f32[8,256,256]{2,1,0:T(8,128)}, bf16[8,64,256]{2,1,0:T(8,128)(2,1)S(1)}) custom-call(s32[4,8]{1,0:T(4,128)S(1)} %pad_add_fusion.refs_0_, s32[4,8]{1,0:T(4,128)S(1)} %collective-permute-done.refs_1_, s32[4,8]{1,0:T(4,128)S(1)} %collective-permute-done.1.refs_2_, ...), custom_call_target="tpu_custom_call", output_to_operand_aliasing={{0}: (9, {})} | custom-call | flops 524288 | bytes 1572864 | tf_op jit(solution)/shard_map/add_up/pallas_call | solution.py:245
  46.7 3.2 %collective-permute-start.14 = (bf16[8,64,256]{2,1,0:T(8,128)(2,1)S(1)}, bf16[8,64,256]{2,1,0:T(8,128)(2,1)S(1)}, u32[]{:S(2)}, u32[]{:S(2)}) collective-permute-start(bf16[8,64,256]{2,1,0:T(8,128)(2,1)S(1)} %get-tuple-element.34), channel_id=1, source_target_pairs={{0,3},{1,0},{2,1},{3,2},{4,7},{5,4},{6,5},{7,6},{8,11},{9,8},{10,9... | collective-permute-start | bytes 786440 | tf_op jit(solution)/shard_map/ppermute | solution.py:263
  49.9 1.5 %collective-permute-start.4 = (bf16[1,4,64,256]{3,2,1,0:T(8,128)(2,1)S(1)}, bf16[1,4,64,256]{3,2,1,0:T(8,128)(2,1)S(1)}, u32[]{:S(2)}, u32[]{:S(2)}) collective-permute-start(bf16[1,4,64,256]{3,2,1,0:T(8,128)(2,1)S(1)} %get-tuple-element.22), channel_id=1, source_target_pairs={{0,8},{4,12},{8,0},{12,4},{1,9},{5,13},{9,1},{13,5},{2,10},{6,14},... | collective-permute-start | bytes 393224 | tf_op jit(solution)/shard_map/ppermute | solution.py:214
  52.0 4.3 %collective-permute-done.4.refs_7_ = bf16[1,4,64,256]{3,2,1,0:T(8,128)(2,1)S(1)} collective-permute-done((bf16[1,4,64,256]{3,2,1,0:T(8,128)(2,1)S(1)}, bf16[1,4,64,256]{3,2,1,0:T(8,128)(2,1)S(1)}, u32[]{:S(2)}, u32[]{:S(2)}) %collective-permute-start.4) | collective-permute-done | bytes 131104 | tf_op jit(solution)/shard_map/ppermute | solution.py:214
  56.3 2.4 %collective-permute-done.5.refs_8_ = bf16[1,4,64,256]{3,2,1,0:T(8,128)(2,1)S(1)} collective-permute-done((bf16[1,4,64,256]{3,2,1,0:T(8,128)(2,1)S(1)}, bf16[1,4,64,256]{3,2,1,0:T(8,128)(2,1)S(1)}, u32[]{:S(2)}, u32[]{:S(2)}) %collective-permute-start.5) | collective-permute-done | bytes 131104 | tf_op jit(solution)/shard_map/ppermute | solution.py:214
  58.7 0.9 %collective-permute-done.8.refs_9_ = bf16[8,64,256]{2,1,0:T(8,128)(2,1)S(1)} collective-permute-done((bf16[8,64,256]{2,1,0:T(8,128)(2,1)S(1)}, bf16[8,64,256]{2,1,0:T(8,128)(2,1)S(1)}, u32[]{:S(2)}, u32[]{:S(2)}) %collective-permute-start.8) | collective-permute-done | bytes 262176 | tf_op jit(solution)/shard_map/ppermute | solution.py:263
  59.5 5.2 %collective-permute-done.14.refs_11_ = bf16[8,64,256]{2,1,0:T(8,128)(2,1)S(1)} collective-permute-done((bf16[8,64,256]{2,1,0:T(8,128)(2,1)S(1)}, bf16[8,64,256]{2,1,0:T(8,128)(2,1)S(1)}, u32[]{:S(2)}, u32[]{:S(2)}) %collective-permute-start.14) | collective-permute-done | bytes 262176 | tf_op jit(solution)/shard_map/ppermute | solution.py:263
  64.8 3.2 %add_up.7 = (f32[8,256,256]{2,1,0:T(8,128)}, f32[8,64,256]{2,1,0:T(8,128)}) custom-call(s32[4,8]{1,0:T(4,128)S(1)} %pad_add_fusion.refs_0_, s32[4,8]{1,0:T(4,128)S(1)} %collective-permute-done.refs_1_, s32[4,8]{1,0:T(4,128)S(1)} %collective-permute-done.1.refs_2_, s32[4,8]{1,0:T(4,128)S(1)} %collective-permute-done.2.refs_3_, ...), custom_call_target="tpu_custom_call", output_to_operand_aliasing={{0}: (12, {})} | custom-call | flops 524288 | bytes 1572864 | tf_op jit(solution)/shard_map/add_up/pallas_call | solution.py:245
  (43 shorter events, 7.7 us)
Async XLA Ops:
  5.3 0.9 %copy-start.9 = (bf16[256,512]{1,0:T(8,128)(2,1)S(1)}, bf16[256,512]{1,0:T(8,128)(2,1)}, u32[]{:S(2)}) copy-start(bf16[256,512]{1,0:T(8,128)(2,1)} %constant.12.clone.to_col) | copy-start | bytes 786436
  6.3 0.9 %copy-start.10 = (bf16[256,288]{1,0:T(8,128)(2,1)S(1)}, bf16[256,288]{1,0:T(8,128)(2,1)}, u32[]{:S(2)}) copy-start(bf16[256,288]{1,0:T(8,128)(2,1)} %constant.15.clone.from_row) | copy-start | bytes 442372
  7.2 0.9 %copy-start.11 = (bf16[288,256]{1,0:T(8,128)(2,1)S(1)}, bf16[288,256]{1,0:T(8,128)(2,1)}, u32[]{:S(2)}) copy-start(bf16[288,256]{1,0:T(8,128)(2,1)} %constant.13.clone.to_row) | copy-start | bytes 442372
  8.1 0.9 %copy-start.12 = (bf16[288,41]{1,0:T(8,128)(2,1)S(1)}, bf16[288,41]{1,0:T(8,128)(2,1)}, u32[]{:S(2)}) copy-start(bf16[288,41]{1,0:T(8,128)(2,1)} %constant.17.clone.tap_row) | copy-start | bytes 70852
  9.0 0.8 %copy-start.13 = (bf16[41,512]{1,0:T(8,128)(2,1)S(1)}, bf16[41,512]{1,0:T(8,128)(2,1)}, u32[]{:S(2)}) copy-start(bf16[41,512]{1,0:T(8,128)(2,1)} %constant.16.clone.tap_col) | copy-start | bytes 125956
  9.8 14.2 %copy-start.14 = (s32[1,8]{1,0:T(1,128)S(1)}, s32[1,8]{1,0:T(1,128)}, u32[]{:S(2)}) copy-start(s32[1,8]{1,0:T(1,128)} %param.18) | copy-start | bytes 100
  9.8 25.1 %copy-start.3 = (f32[1,12]{1,0:T(1,128)S(1)}, f32[1,12]{1,0:T(1,128)}, u32[]{:S(2)}) copy-start(f32[1,12]{1,0:T(1,128)} %refs_4_.7) | copy-start | bytes 148
  20.9 14.0 %collective-permute-start.3 = (bf16[4,4,64,256]{3,2,1,0:T(8,128)(2,1)}, bf16[4,4,64,256]{3,2,1,0:T(8,128)(2,1)S(1)}, u32[]{:S(2)}, u32[]{:S(2)}) collective-permute-start(bf16[4,4,64,256]{3,2,1,0:T(8,128)(2,1)} %get-tuple-element.21), channel_id=1, source_target_pairs={{0,4},{4,0},{8,12},{12,8},{1,5},{5,1},{9,13},{13,9},{2,6},{6,2},{1... | collective-permute-start | bytes 1572872 | tf_op jit(solution)/shard_map/ppermute | solution.py:214
  21.3 11.9 %collective-permute-start.6 = (bf16[1,4,64,256]{3,2,1,0:T(8,128)(2,1)S(1)}, bf16[1,4,64,256]{3,2,1,0:T(8,128)(2,1)S(1)}, u32[]{:S(2)}, u32[]{:S(2)}) collective-permute-start(bf16[1,4,64,256]{3,2,1,0:T(8,128)(2,1)S(1)} %get-tuple-element.24), channel_id=1, source_target_pairs={{0,8},{4,12},{8,0},{12,4},{1,9},{5,13},{9,1},{13,5},{2,10},{6,14},... | collective-permute-start | bytes 393224 | tf_op jit(solution)/shard_map/ppermute | solution.py:214
  23.8 10.3 %collective-permute-start.7 = (bf16[1,4,64,256]{3,2,1,0:T(8,128)(2,1)S(1)}, bf16[1,4,64,256]{3,2,1,0:T(8,128)(2,1)S(1)}, u32[]{:S(2)}, u32[]{:S(2)}) collective-permute-start(bf16[1,4,64,256]{3,2,1,0:T(8,128)(2,1)S(1)} %get-tuple-element.25), channel_id=1, source_target_pairs={{0,12},{4,8},{8,4},{12,0},{1,13},{5,9},{9,5},{13,1},{2,14},{6,10},... | collective-permute-start | bytes 393224 | tf_op jit(solution)/shard_map/ppermute | solution.py:214
  24.0 6.7 %collective-permute-start.2 = (s32[4,8]{1,0:T(4,128)S(1)}, s32[4,8]{1,0:T(4,128)S(1)}, u32[]{:S(2)}, u32[]{:S(2)}) collective-permute-start(s32[4,8]{1,0:T(4,128)S(1)} %pad_add_fusion.refs_0_), channel_id=1, source_target_pairs={{0,12},{4,8},{8,4},{12,0},{1,13},{5,9},{9,5},{13,1},{2,14},{6,10},... | collective-permute-start | bytes 392 | tf_op jit(solution)/shard_map/ppermute | solution.py:214
  25.6 5.2 %collective-permute-start.1 = (s32[4,8]{1,0:T(4,128)S(1)}, s32[4,8]{1,0:T(4,128)S(1)}, u32[]{:S(2)}, u32[]{:S(2)}) collective-permute-start(s32[4,8]{1,0:T(4,128)S(1)} %pad_add_fusion.refs_0_), channel_id=1, source_target_pairs={{0,8},{4,12},{8,0},{12,4},{1,9},{5,13},{9,1},{13,5},{2,10},{6,14},... | collective-permute-start | bytes 392 | tf_op jit(solution)/shard_map/ppermute | solution.py:214
  30.6 2.0 %collective-permute-start = (s32[4,8]{1,0:T(4,128)S(1)}, s32[4,8]{1,0:T(4,128)S(1)}, u32[]{:S(2)}, u32[]{:S(2)}) collective-permute-start(s32[4,8]{1,0:T(4,128)S(1)} %pad_add_fusion.refs_0_), channel_id=1, source_target_pairs={{0,4},{4,0},{8,12},{12,8},{1,5},{5,1},{9,13},{13,9},{2,6},{6,2},{1... | collective-permute-start | bytes 392 | tf_op jit(solution)/shard_map/ppermute | solution.py:214
  30.9 9.9 %collective-permute-start.9 = (bf16[1,4,64,256]{3,2,1,0:T(8,128)(2,1)S(1)}, bf16[1,4,64,256]{3,2,1,0:T(8,128)(2,1)S(1)}, u32[]{:S(2)}, u32[]{:S(2)}) collective-permute-start(bf16[1,4,64,256]{3,2,1,0:T(8,128)(2,1)S(1)} %get-tuple-element.27), channel_id=1, source_target_pairs={{0,8},{4,12},{8,0},{12,4},{1,9},{5,13},{9,1},{13,5},{2,10},{6,14},... | collective-permute-start | bytes 393224 | tf_op jit(solution)/shard_map/ppermute | solution.py:214
  32.6 8.2 %collective-permute-start.10 = (bf16[1,4,64,256]{3,2,1,0:T(8,128)(2,1)S(1)}, bf16[1,4,64,256]{3,2,1,0:T(8,128)(2,1)S(1)}, u32[]{:S(2)}, u32[]{:S(2)}) collective-permute-start(bf16[1,4,64,256]{3,2,1,0:T(8,128)(2,1)S(1)} %get-tuple-element.28), channel_id=1, source_target_pairs={{0,12},{4,8},{8,4},{12,0},{1,13},{5,9},{9,5},{13,1},{2,14},{6,10},... | collective-permute-start | bytes 393224 | tf_op jit(solution)/shard_map/ppermute | solution.py:214
  33.2 11.4 %collective-permute-start.12 = (bf16[1,4,64,256]{3,2,1,0:T(8,128)(2,1)S(1)}, bf16[1,4,64,256]{3,2,1,0:T(8,128)(2,1)S(1)}, u32[]{:S(2)}, u32[]{:S(2)}) collective-permute-start(bf16[1,4,64,256]{3,2,1,0:T(8,128)(2,1)S(1)} %get-tuple-element.31), channel_id=1, source_target_pairs={{0,8},{4,12},{8,0},{12,4},{1,9},{5,13},{9,1},{13,5},{2,10},{6,14},... | collective-permute-start | bytes 393224 | tf_op jit(solution)/shard_map/ppermute | solution.py:214
  34.1 10.5 %collective-permute-start.13 = (bf16[1,4,64,256]{3,2,1,0:T(8,128)(2,1)S(1)}, bf16[1,4,64,256]{3,2,1,0:T(8,128)(2,1)S(1)}, u32[]{:S(2)}, u32[]{:S(2)}) collective-permute-start(bf16[1,4,64,256]{3,2,1,0:T(8,128)(2,1)S(1)} %get-tuple-element.32), channel_id=1, source_target_pairs={{0,12},{4,8},{8,4},{12,0},{1,13},{5,9},{9,5},{13,1},{2,14},{6,10},... | collective-permute-start | bytes 393224 | tf_op jit(solution)/shard_map/ppermute | solution.py:214
  34.9 9.7 %copy-start.1 = (bf16[4,4,64,256]{3,2,1,0:T(8,128)(2,1)}, bf16[4,4,64,256]{3,2,1,0:T(8,128)(2,1)S(1)}, u32[]{:S(2)}) copy-start(bf16[4,4,64,256]{3,2,1,0:T(8,128)(2,1)S(1)} %collective-permute-done.3.refs_6_) | copy-start | bytes 1572868
  34.9 1.2 %copy-start = (bf16[4,4,64,256]{3,2,1,0:T(8,128)(2,1)S(1)}, bf16[4,4,64,256]{3,2,1,0:T(8,128)(2,1)}, u32[]{:S(2)}) copy-start(bf16[4,4,64,256]{3,2,1,0:T(8,128)(2,1)} %get-tuple-element.20.refs_5_) | copy-start | bytes 1572868
  38.2 21.3 %collective-permute-start.8 = (bf16[8,64,256]{2,1,0:T(8,128)(2,1)S(1)}, bf16[8,64,256]{2,1,0:T(8,128)(2,1)S(1)}, u32[]{:S(2)}, u32[]{:S(2)}) collective-permute-start(bf16[8,64,256]{2,1,0:T(8,128)(2,1)S(1)} %get-tuple-element.26), channel_id=1, source_target_pairs={{0,2},{1,3},{2,0},{3,1},{4,6},{5,7},{6,4},{7,5},{8,10},{9,11},{10,... | collective-permute-start | bytes 786440 | tf_op jit(solution)/shard_map/ppermute | solution.py:263
  42.9 16.6 %collective-permute-start.11 = (bf16[8,64,256]{2,1,0:T(8,128)(2,1)S(1)}, bf16[8,64,256]{2,1,0:T(8,128)(2,1)S(1)}, u32[]{:S(2)}, u32[]{:S(2)}) collective-permute-start(bf16[8,64,256]{2,1,0:T(8,128)(2,1)S(1)} %get-tuple-element.30), channel_id=1, source_target_pairs={{0,1},{1,2},{2,3},{3,0},{4,5},{5,6},{6,7},{7,4},{8,9},{9,10},{10,1... | collective-permute-start | bytes 786440 | tf_op jit(solution)/shard_map/ppermute | solution.py:263
  46.7 18.1 %collective-permute-start.14 = (bf16[8,64,256]{2,1,0:T(8,128)(2,1)S(1)}, bf16[8,64,256]{2,1,0:T(8,128)(2,1)S(1)}, u32[]{:S(2)}, u32[]{:S(2)}) collective-permute-start(bf16[8,64,256]{2,1,0:T(8,128)(2,1)S(1)} %get-tuple-element.34), channel_id=1, source_target_pairs={{0,3},{1,0},{2,1},{3,2},{4,7},{5,4},{6,5},{7,6},{8,11},{9,8},{10,9... | collective-permute-start | bytes 786440 | tf_op jit(solution)/shard_map/ppermute | solution.py:263
  49.9 6.4 %collective-permute-start.4 = (bf16[1,4,64,256]{3,2,1,0:T(8,128)(2,1)S(1)}, bf16[1,4,64,256]{3,2,1,0:T(8,128)(2,1)S(1)}, u32[]{:S(2)}, u32[]{:S(2)}) collective-permute-start(bf16[1,4,64,256]{3,2,1,0:T(8,128)(2,1)S(1)} %get-tuple-element.22), channel_id=1, source_target_pairs={{0,8},{4,12},{8,0},{12,4},{1,9},{5,13},{9,1},{13,5},{2,10},{6,14},... | collective-permute-start | bytes 393224 | tf_op jit(solution)/shard_map/ppermute | solution.py:214
  51.4 7.3 %collective-permute-start.5 = (bf16[1,4,64,256]{3,2,1,0:T(8,128)(2,1)S(1)}, bf16[1,4,64,256]{3,2,1,0:T(8,128)(2,1)S(1)}, u32[]{:S(2)}, u32[]{:S(2)}) collective-permute-start(bf16[1,4,64,256]{3,2,1,0:T(8,128)(2,1)S(1)} %get-tuple-element.23), channel_id=1, source_target_pairs={{0,12},{4,8},{8,4},{12,0},{1,13},{5,9},{9,5},{13,1},{2,14},{6,10},... | collective-permute-start | bytes 393224 | tf_op jit(solution)/shard_map/ppermute | solution.py:214
  (6 other events, 4.0 us)

commit v2 on v1

v2 whole, which is shorter than its diff:
```python
import functools

import jax
import jax.numpy as jnp
import ml_dtypes
import numpy as np
from jax import lax
from jax.experimental import pallas as pl
from jax.experimental.pallas import tpu as pltpu
from jax.sharding import PartitionSpec as P

PATCH_DEV = 8
F32, BF16 = jnp.float32, jnp.bfloat16
MIB = 1024 * 1024
HEAD = 16
UNROLL = 2


def round_up(value, multiple):
    return -(-value // multiple) * multiple


def wave_tables(side, kernel_len):
    half_len = kernel_len // 2
    count = -(-(side + half_len) // 2)
    omega = np.pi * (np.arange(count) + 0.5) / count
    sub, lane = round_up(count, 16), round_up(count, 128)

    def waves(points, width):
        out = np.zeros((len(points), 2 * width), np.float64)
        out[:, :count] = np.cos(np.outer(points, omega))
        out[:, width : width + count] = np.sin(np.outer(points, omega))
        return out

    pixels, taps = np.arange(side), np.arange(kernel_len) - half_len
    held = lambda a: np.ascontiguousarray(a).astype(ml_dtypes.bfloat16)
    return dict(
        sub=sub,
        lane=lane,
        scale=1.0 / (count * count),
        to_col=held(waves(pixels, lane)),
        to_row=held(waves(pixels, sub).T),
        from_col=held(waves(pixels, lane).T),
        from_row=held(waves(pixels, sub)),
        tap_col=held(waves(taps, lane)),
        tap_row=held(waves(taps, sub).T),
    )


def dot(a, b, contract=((1,), (0,))):
    return lax.dot_general(a, b, (contract, ((), ())), preferred_element_type=F32)


def weigh(rows, tables):
    lane = rows[0].shape[1] // 2
    (c, s), (tc, ts) = rows, tables
    cc, cs, sc, ss = c[:, :lane], c[:, lane:], s[:, :lane], s[:, lane:]
    pa, pb, qa, qb = tc[:, :lane], tc[:, lane:], ts[:, :lane], ts[:, lane:]
    return (
        (pa * cc + pb * cs + qa * sc + qb * ss).astype(BF16),
        (pa * cs - pb * cc + qa * ss - qb * sc).astype(BF16),
        (pa * sc + pb * ss - qa * cc - qb * cs).astype(BF16),
        (pa * ss - pb * sc - qa * cs + qb * cc).astype(BF16),
    )


def convolve_kernel(plan, *refs):
    n_in, n_out = plan["n_in"], plan["n_out"]
    sources, outs, held = refs[:n_in], refs[n_in : n_in + n_out], refs[n_in + n_out :]
    local, (sems, row_waves, col_waves, back, heads) = held[:n_in], held[n_in:]
    sub, lane, rows, nb, cap, slots = (plan[k] for k in ("sub", "lane", "rows", "nb", "cap", "slots"))
    copies = [pltpu.make_async_copy(a, b, sems.at[i]) for i, (a, b) in enumerate(zip(sources[:-1], local[:-1]))]
    tiles = [
        pltpu.make_async_copy(sources[-1].at[s], local[-1].at[s], sems.at[n_in - 1 + s]) for s in range(slots)
    ]
    for copy in copies + tiles:
        copy.start()
    owner, local_id, valid, visit, inv_var, coef, kx, ky, to_col, to_row, from_col, from_row, tap_col, tap_row, patch = local
    for copy in copies:
        copy.wait()
    side = patch.shape[1]
    row_waves[...] = dot(tap_row[...], ky[...], ((1,), (1,)))
    col_waves[...] = (dot(kx[...], tap_col[...]) * plan["scale"]).astype(BF16)
    band = lax.axis_index("band")
    for phase in range(nb):
        start = pl.multiple_of(plan["chunk"](band, phase) * rows, rows)
        back[phase * rows : (phase + 1) * rows, :] = from_row[pl.ds(start, rows), :]
    heads[...] = jnp.full(heads.shape, -1.0, F32)
    me = lax.axis_index("sky")
    basis = kx.shape[0]
    lanes = lax.broadcasted_iota(jnp.int32, (1, 128), 1)

    def convolved(slot):
        seen = visit[0, slot]
        weight = jnp.full((1, basis), inv_var[0, seen], F32).astype(BF16).astype(F32)
        mixing = (weight * coef[seen].astype(BF16).astype(F32)).astype(BF16).astype(F32)
        row_ids = lax.broadcasted_iota(jnp.int32, (side, side), 0)
        masked = jnp.where(row_ids < valid[0, slot], patch[slot], 0.0).astype(BF16)
        col = dot(masked, to_col[...]).astype(BF16)
        mixed = (row_waves[...] * mixing).astype(BF16)
        parts = (dot(to_row[:sub, :], col), dot(to_row[sub:, :], col))
        tables = (dot(mixed[:sub], col_waves[...]), dot(mixed[sub:], col_waves[...]))
        y_cc, y_cs, y_sc, y_ss = weigh(parts, tables)
        z_c = dot(y_cc, from_col[:lane, :]) + dot(y_cs, from_col[lane:, :])
        z_s = dot(y_sc, from_col[:lane, :]) + dot(y_ss, from_col[lane:, :])
        return (dot(back[:, :sub], z_c.astype(BF16)) + dot(back[:, sub:], z_s.astype(BF16))).astype(BF16)

    def deliver(slot, full):
        mine = owner[0, slot]
        rank = jnp.int32(0)
        for other in range(slots):
            rank = rank + jnp.where((other < slot) & (owner[0, other] == mine), 1, 0).astype(jnp.int32)
        box = mine if plan["single"] else mine ^ me
        weight = jnp.full((1, 128), inv_var[0, visit[0, slot]], F32)
        facts = jnp.where(lanes == 8 * rank, local_id[0, slot].astype(F32), heads[box])
        facts = jnp.where(lanes == 8 * rank + 1, valid[0, slot].astype(F32), facts)
        heads[box] = jnp.where(lanes == 8 * rank + 2, weight, facts)
        for group in range(len(plan["split"])):
            at = mine if plan["single"] else 0

            def store(group=group, at=at):
                for phase in range(nb):
                    ref, first = plan["place"](outs, group, phase)
                    start = pl.multiple_of(first + rank * rows, rows)
                    ref[at, pl.ds(start, rows), :] = full[phase * rows : (phase + 1) * rows, :]

            if plan["single"]:
                store()
            else:
                pl.when(box == group)(store)

    def some(step, carry):
        slots_now = [step * UNROLL + u for u in range(UNROLL)]
        for s in slots_now:
            pltpu.make_async_copy(sources[-1].at[s], local[-1].at[s], sems.at[n_in - 1 + s]).wait()
        results = [convolved(s) for s in slots_now]
        for s, full in zip(slots_now, results):
            deliver(s, full)
        return carry

    lax.fori_loop(0, slots // UNROLL, some, 0)
    width = patch.shape[2]
    for group in range(len(plan["split"])):
        ref, first = plan["head"](outs, group)
        for at in range(ref.shape[0]):
            row = heads[at if plan["single"] else group]
            row = jnp.concatenate([row] * (width // 128), axis=1)
            ref[at, first : first + HEAD, :] = jnp.broadcast_to(row, (HEAD, width)).astype(BF16)


def sum_kernel(plan, phase, *refs):
    sky, nb, rows, cap, per = plan["sky"], plan["nb"], plan["rows"], plan["cap"], plan["per"]
    first, last = phase == 0, phase == nb - 1
    refs = list(refs)
    take = lambda n: [refs.pop(0) for _ in range(n)]
    boxes = take(len(plan["split"]))
    arrived = take(len(plan["adds"][phase]))
    heads = take(len(plan["split"])) if first else None
    facts = None if first else take(2)
    if not first:
        take(1)
    band_out, extra = take(2)
    if first:
        facts = take(2)
    acc, cov, sems = take(3)
    if first:
        whole_facts, weights = take(2)
        rows_of = [h[d, 0:1, :128].astype(F32) for h in heads for d in range(h.shape[0])]
        for source, row in enumerate(rows_of):
            whole_facts[source : source + 1, :] = row.astype(jnp.int32)
            weights[source : source + 1, :] = row
        copies = [pltpu.make_async_copy(a, b, sems.at[i]) for i, (a, b) in enumerate(((whole_facts, facts[0]), (weights, facts[1])))]
        for copy in copies:
            copy.start()
    chunk = plan["chunk"](lax.axis_index("band"), phase)
    acc[...] = jnp.zeros_like(acc)
    cov[...] = jnp.zeros_like(cov)
    row_ids = chunk * rows + lax.broadcasted_iota(jnp.int32, (rows, 128), 0)
    if first:
        for copy in copies:
            copy.wait()
    for source in range(sky):
        group, at = (0, source) if plan["single"] else (source, 0)
        for rank in range(cap):
            local = facts[0][source, 8 * rank]

            @pl.when(local >= 0)
            def _(group=group, at=at, rank=rank, source=source, local=local):
                acc[local] += boxes[group][at, rank * rows : (rank + 1) * rows, :].astype(F32)
                weight = jnp.full((rows, 128), facts[1][source, 8 * rank + 2], F32)
                cov[local] += jnp.where(row_ids < facts[0][source, 8 * rank + 1], weight, 0.0)

    width = acc.shape[2]
    copies = []
    for patch in range(per):
        factor = 1.0 / jnp.maximum(cov[patch], 1.0)
        for at in range(0, width, 128):
            value = acc[patch, :, at : at + 128] * factor
            acc[patch, :, at : at + 128] = value
            for other in arrived:
                value = value + other[patch, :, at : at + 128].astype(F32)
            extra[patch, :, at : at + 128] = value.astype(extra.dtype)
        copies.append(pltpu.make_async_copy(
            acc.at[patch], band_out.at[patch, pl.ds(pl.multiple_of(chunk * rows, rows), rows), :], sems.at[patch]))
        copies[-1].start()
    for copy in copies:
        copy.wait()


def band_plan(nb):
    if nb == 4:
        masks = [3, 2, 1, 0]
        chunk = lambda band, phase: band ^ masks[phase]
        partner = lambda band, phase: band ^ (1, 2, 1)[phase]
        adds = [[], [0], [], [1, 2]]
    else:
        shifts = sorted(range(1, nb), key=lambda k: -min(k, nb - k)) + [0]
        chunk = lambda band, phase: (band + shifts[phase]) % nb if isinstance(band, int) else lax.rem(band + shifts[phase], nb)
        partner = chunk
        adds = [[]] * (nb - 1) + [list(range(nb - 1))]
    return chunk, partner, adds


def per_device(patches, valid_rows, slot_owner, slot_local, slot_visit, basis_coef, inv_var, kernel_x, kernel_y):
    tiles = patches[0]
    slots, side, width = tiles.shape
    sky, nb = lax.axis_size("sky"), lax.axis_size("band")
    cap = max(2, 2 * slots // sky)
    rows = side // nb
    single = sky > 4 or sky & (sky - 1) != 0
    tables = wave_tables(side, kernel_x.shape[1])
    sub, lane = tables["sub"], tables["lane"]
    chunk, partner, adds = band_plan(nb)
    near = 0 if single else min(2, sky)
    split = [True] if single else [r >= near for r in range(sky)]
    n_dest = sky if single else 1
    box = cap * rows
    out_shapes, first_out = [], []
    for cut in split:
        first_out.append(len(out_shapes))
        heights = [box + (HEAD if phase == 0 else 0) for phase in range(nb)] if cut else [nb * box + HEAD]
        out_shapes += [jax.ShapeDtypeStruct((n_dest, h, width), BF16) for h in heights]

    def place(outs, group, phase):
        return (outs[first_out[group] + phase], 0) if split[group] else (outs[first_out[group]], phase * box)

    def head(outs, group):
        return outs[first_out[group]], box if split[group] else nb * box

    plan = dict(sub=sub, lane=lane, rows=rows, nb=nb, scale=tables["scale"], slots=slots, cap=cap, sky=sky, per=PATCH_DEV,
                single=single, split=split, place=place, head=head, chunk=chunk, adds=adds)
    smem = pl.BlockSpec(memory_space=pltpu.SMEM)
    hbm = pl.BlockSpec(memory_space=pltpu.HBM)
    vmem = pl.BlockSpec(memory_space=pltpu.VMEM)
    consts = [jnp.asarray(tables[n]) for n in ("to_col", "to_row", "from_col", "from_row", "tap_col", "tap_row")]
    weights = lax.reduce_precision(inv_var, 8, 7)
    args = [slot_owner.reshape(1, slots), slot_local, valid_rows, slot_visit, weights, basis_coef.transpose(1, 0, 2),
            kernel_x, kernel_y] + consts + [tiles]
    plan.update(n_in=len(args), n_out=len(out_shapes))
    landing = [pltpu.SMEM(a.shape, a.dtype) for a in args[:5]] + [pltpu.VMEM(a.shape, a.dtype) for a in args[5:]]
    sent = pl.pallas_call(
        functools.partial(convolve_kernel, plan),
        out_shape=out_shapes,
        in_specs=[hbm] * len(args),
        out_specs=[vmem] * len(out_shapes),
        scratch_shapes=landing + [
            pltpu.SemaphoreType.DMA((len(args) - 1 + slots,)), pltpu.VMEM((2 * sub, kernel_x.shape[0]), F32),
            pltpu.VMEM((kernel_x.shape[0], 2 * lane), BF16), pltpu.VMEM((side, 2 * sub), BF16),
            pltpu.VMEM((sky, 1, 128), F32)],
        compiler_params=pltpu.CompilerParams(vmem_limit_bytes=40 * MIB),
        cost_estimate=pl.CostEstimate(flops=slots * 22 * side**3, bytes_accessed=slots * side * side * 6,
                                      transcendentals=0),
        name="convolve",
    )(*args)

    swap = lambda a, r: a if r == 0 else lax.ppermute(a, "sky", [(i, i ^ r) for i in range(sky)])
    moved = list(sent)
    if single:
        moved = [lax.all_to_all(s, "sky", split_axis=0, concat_axis=0, tiled=True) for s in sent]
    else:
        for r in range(1, near):
            moved[first_out[r]] = swap(sent[first_out[r]], r)
        for phase in range(nb):
            for r in range(near, sky):
                moved[first_out[r] + phase] = swap(sent[first_out[r] + phase], r)

    band_buf, facts, arrived = None, None, []
    band_shape = jax.ShapeDtypeStruct((PATCH_DEV, side, width), F32)
    chunk_shape = (PATCH_DEV, rows, width)
    whole = lambda shape: pl.BlockSpec(shape, lambda *_: (0,) * len(shape))
    fact_shapes = [jax.ShapeDtypeStruct((sky, 128), jnp.int32), jax.ShapeDtypeStruct((sky, 128), F32)]
    for phase in range(nb):
        first, last = phase == 0, phase == nb - 1
        inputs, specs = [], []
        for group, cut in enumerate(split):
            inputs.append(place(moved, group, phase)[0])
            specs.append(pl.BlockSpec((n_dest, box, width), lambda i, at=0 if cut else phase: (0, at, 0)))
        for earlier in adds[phase]:
            inputs.append(arrived[earlier])
            specs.append(whole(chunk_shape))
        outs = [band_shape, jax.ShapeDtypeStruct(chunk_shape, F32 if last else BF16)]
        out_specs, aliases, scratch = [hbm, whole(chunk_shape)], {}, []
        if first:
            for group in range(len(split)):
                ref, start = head(moved, group)
                inputs.append(ref)
                specs.append(pl.BlockSpec((n_dest, HEAD, width), lambda i, at=start // HEAD: (0, at, 0)))
            outs, out_specs = outs + fact_shapes, out_specs + [smem] * 2
            scratch = [pltpu.VMEM(s.shape, s.dtype) for s in fact_shapes]
        else:
            inputs, specs = inputs + facts, specs + [smem] * 2
            aliases = {len(inputs): 0}
            inputs, specs = inputs + [band_buf], specs + [hbm]
        band_buf, extra, *rest = pl.pallas_call(
            functools.partial(sum_kernel, plan, phase),
            grid=(1,),
            out_shape=outs,
            in_specs=specs,
            out_specs=out_specs,
            scratch_shapes=[pltpu.VMEM(chunk_shape, F32), pltpu.VMEM((PATCH_DEV, rows, 128), F32),
                            pltpu.SemaphoreType.DMA((PATCH_DEV,))] + scratch,
            input_output_aliases=aliases,
            compiler_params=pltpu.CompilerParams(vmem_limit_bytes=24 * MIB),
            cost_estimate=pl.CostEstimate(flops=4 * PATCH_DEV * rows * width,
                                          bytes_accessed=12 * PATCH_DEV * rows * width, transcendentals=0),
            name="add_up",
        )(*inputs)
        facts = rest if first else facts
        if not last:
            arrived.append(lax.ppermute(extra, "band", [(b, partner(b, phase)) for b in range(nb)]))
    return (band_buf[None], extra)


def solution(mesh):
    in_specs = (
        P(("tract", "band"), "sky", None, None),
        P(("tract", "band"), "sky"),
        P(("tract", "band"), "sky", None),
        P(("tract", "band"), "sky"),
        P(("tract", "band"), "sky"),
        P(("tract", "band"), None, None),
        P(("tract", "band"), None),
        P(),
        P(),
    )
    out_specs = (P(("tract", "band"), "sky", None, None), P(("tract", "sky"), "band", None))
    return jax.shard_map(per_device, mesh=mesh, in_specs=in_specs, out_specs=out_specs, check_vma=False)
```

time: 68.5 us -> 67.7 us (0.988)
  waiting for transfers between devices: 17.7 us -> 24.1 us
  starting transfers between devices: 18.7 us -> 13.5 us
  Pallas kernels: 20.5 us -> 16.6 us
  local copies, waits for them, and re-layouts: 10.4 us -> 11.7 us
    ppermute x12 -> x9, waiting for transfers between devices: 11.6 us -> 18.4 us  [per_device(): lax.ppermute(a, 'sky', [(i, i ^ r) for i in range(sky)])]
    ppermute x3, starting transfers between devices: 7.5 us -> 4.86 us  [per_device(): lax.ppermute(extra, 'band', [(b, partner(b, phase)) for b in range(nb)])]
    pallas_call x1, Pallas kernels: 11.1 us -> 8.46 us  [per_device(): pl.pallas_call(functools.partial(convolve_kernel, plan), out_shape=out_sh...]
    ppermute x12 -> x9, starting transfers between devices: 11.2 us -> 8.59 us  [per_device(): lax.ppermute(a, 'sky', [(i, i ^ r) for i in range(sky)])]
    unnamed x31 -> x28, local copies, waits for them, and re-layouts: 10.4 us -> 11.7 us
    pallas_call x4, Pallas kernels: 9.43 us -> 8.19 us  [per_device(): pl.pallas_call(functools.partial(sum_kernel, plan, phase), grid=(1,), out...]
  transfers between devices with their start and end apart: 15 -> 12, of which waited for: 6 -> 9; matrix products, arithmetic and copies ran while one was open for 0% -> 0% of each run, Pallas kernels for 9% -> 5%
where the time goes in v2:
time: 67.7 us; the launch traced here: 67.2 us
  waiting for transfers between devices  24.1 us (36%)
  Pallas kernels  16.6 us (25%)
  starting transfers between devices  13.5 us (20%)
  local copies, waits for them, and re-layouts  11.7 us (17%)
  between operations  0.69 us (1%)
    ppermute x9, waiting for transfers between devices, per_device(): lax.ppermute(a, 'sky', [(i, i ^ r) for i in range(sky)])  18.4 us
    unnamed x28, local copies, waits for them, and re-layouts  11.7 us
    ppermute x9, starting transfers between devices, per_device(): lax.ppermute(a, 'sky', [(i, i ^ r) for i in range(sky)])  8.59 us
    pallas_call x1, Pallas kernels, per_device(): pl.pallas_call(functools.partial(convolve_kernel, plan), out_shape=out_sh...  8.46 us
    pallas_call x4, Pallas kernels, per_device(): pl.pallas_call(functools.partial(sum_kernel, plan, phase), grid=(1,), out...  8.19 us
    ppermute x3, waiting for transfers between devices, per_device(): lax.ppermute(extra, 'band', [(b, partner(b, phase)) for b in range(nb)])  5.72 us
    ppermute x3, starting transfers between devices, per_device(): lax.ppermute(extra, 'band', [(b, partner(b, phase)) for b in range(nb)])  4.86 us
  transfers between devices with their start and end apart: 12, of which 9 were waited for; matrix products, arithmetic and copies ran while one was open for 0% of the time, Pallas kernels for 5%

profile of v2, /device:TPU:0, one launch (start us, length us, event | category | flops | bytes accessed | tf_op | source)
XLA Modules:
  0.0 67.2 jit_solution(11084374210170938772)
XLA Ops:
  1.3 1.6 %copy-done = f32[1,8,256,256]{3,2,1,0:T(8,128)S(1)} copy-done((f32[1,8,256,256]{3,2,1,0:T(8,128)S(1)}, f32[1,8,256,256]{3,2,1,0:T(8,128)}, u32[]{:S(2)}) %copy-start) | copy-done | bytes 2097176
  7.6 0.9 %copy-done.8 = bf16[512,256]{1,0:T(8,128)(2,1)S(1)} copy-done((bf16[512,256]{1,0:T(8,128)(2,1)S(1)}, bf16[512,256]{1,0:T(8,128)(2,1)}, u32[]{:S(2)}) %copy-start.8) | copy-done | bytes 262168
  8.5 0.9 %copy-done.9 = bf16[256,512]{1,0:T(8,128)(2,1)S(1)} copy-done((bf16[256,512]{1,0:T(8,128)(2,1)S(1)}, bf16[256,512]{1,0:T(8,128)(2,1)}, u32[]{:S(2)}) %copy-start.9) | copy-done | bytes 262168
  9.5 0.9 %copy-done.10 = bf16[256,288]{1,0:T(8,128)(2,1)S(1)} copy-done((bf16[256,288]{1,0:T(8,128)(2,1)S(1)}, bf16[256,288]{1,0:T(8,128)(2,1)}, u32[]{:S(2)}) %copy-start.10) | copy-done | bytes 147480
  10.4 0.9 %copy-done.11 = bf16[288,256]{1,0:T(8,128)(2,1)S(1)} copy-done((bf16[288,256]{1,0:T(8,128)(2,1)S(1)}, bf16[288,256]{1,0:T(8,128)(2,1)}, u32[]{:S(2)}) %copy-start.11) | copy-done | bytes 147480
  13.0 8.5 %convolve.1 = (bf16[1,1040,256]{2,1,0:T(8,128)(2,1)S(1)}, bf16[1,1040,256]{2,1,0:T(8,128)(2,1)S(1)}, bf16[1,272,256]{2,1,0:T(8,128)(2,1)S(1)}, bf16[1,256,256]{2...) custom-call(s32[1,8]{1,0:T(1,128)S(1)} %bitcast.6, ...), custom_call_target="tpu_custom_call" | custom-call | flops 2952790016 | bytes 3145728 | tf_op jit(solution)/shard_map/convolve/pallas_call | solution.py:261
  22.0 2.6 %collective-permute-start.5 = (bf16[1,272,256]{2,1,0:T(8,128)(2,1)S(1)}, bf16[1,272,256]{2,1,0:T(8,128)(2,1)S(1)}, u32[]{:S(2)}, u32[]{:S(2)}) collective-permute-start(bf16[1,272,256]{2,1,0:T(8,128)(2,1)S(1)} %get-tuple-element.28), channel_id=1, source_target_pairs={{0,8},{4,12},{8,0},{12,4},{1,9},{5,13},{9,1},{13,5},{2,10},{6,14},... | collective-permute-start | bytes 417800 | tf_op jit(solution)/shard_map/ppermute | solution.py:276
  24.6 4.5 %collective-permute-done.5.refs_2_.refs_6_ = bf16[1,272,256]{2,1,0:T(8,128)(2,1)S(1)} collective-permute-done((bf16[1,272,256]{2,1,0:T(8,128)(2,1)S(1)}, bf16[1,272,256]{2,1,0:T(8,128)(2,1)S(1)}, u32[]{:S(2)}, u32[]{:S(2)}) %collective-permute-start.5) | collective-permute-done | bytes 139296 | tf_op jit(solution)/shard_map/ppermute | solution.py:276
  29.1 2.5 %collective-permute-done.6.refs_3_.refs_7_ = bf16[1,272,256]{2,1,0:T(8,128)(2,1)S(1)} collective-permute-done((bf16[1,272,256]{2,1,0:T(8,128)(2,1)S(1)}, bf16[1,272,256]{2,1,0:T(8,128)(2,1)S(1)}, u32[]{:S(2)}, u32[]{:S(2)}) %collective-permute-start.6) | collective-permute-done | bytes 139296 | tf_op jit(solution)/shard_map/ppermute | solution.py:276
  31.6 2.3 %add_up.4 = (f32[8,256,256]{2,1,0:T(8,128)}, bf16[8,64,256]{2,1,0:T(8,128)(2,1)S(1)}, s32[4,128]{1,0:T(4,128)S(1)}, f32[4,128]{1,0:T(4,128)S(1)}) custom-call(bf16[1,1040,256]{2,1,0:T(8,128)(2,1)S(1)} %get-tuple-element.22.refs_0_.refs_4_, bf16[1,1040,256]{2,1,0:T(8,128)(2,1)S(1)} %collective-permute-done.refs_1_.refs_5_, ...), custom_call_target="tpu_custom_call" | custom-call | flops 524288 | bytes 1572864 | tf_op jit(solution)/shard_map/add_up/pallas_call | solution.py:314
  33.9 1.7 %collective-permute-start.7 = (bf16[8,64,256]{2,1,0:T(8,128)(2,1)S(1)}, bf16[8,64,256]{2,1,0:T(8,128)(2,1)S(1)}, u32[]{:S(2)}, u32[]{:S(2)}) collective-permute-start(bf16[8,64,256]{2,1,0:T(8,128)(2,1)S(1)} %get-tuple-element.30), channel_id=1, source_target_pairs={{0,1},{1,0},{2,3},{3,2},{4,5},{5,4},{6,7},{7,6},{8,9},{9,8},{10,11... | collective-permute-start | bytes 786440 | tf_op jit(solution)/shard_map/ppermute | solution.py:330
  35.6 1.5 %collective-permute-start.3 = (bf16[1,256,256]{2,1,0:T(8,128)(2,1)S(1)}, bf16[1,256,256]{2,1,0:T(8,128)(2,1)S(1)}, u32[]{:S(2)}, u32[]{:S(2)}) collective-permute-start(bf16[1,256,256]{2,1,0:T(8,128)(2,1)S(1)} %get-tuple-element.26), channel_id=1, source_target_pairs={{0,8},{4,12},{8,0},{12,4},{1,9},{5,13},{9,1},{13,5},{2,10},{6,14},... | collective-permute-start | bytes 393224 | tf_op jit(solution)/shard_map/ppermute | solution.py:276
  37.1 1.4 %collective-permute-start.9 = (bf16[1,256,256]{2,1,0:T(8,128)(2,1)S(1)}, bf16[1,256,256]{2,1,0:T(8,128)(2,1)S(1)}, u32[]{:S(2)}, u32[]{:S(2)}) collective-permute-start(bf16[1,256,256]{2,1,0:T(8,128)(2,1)S(1)} %get-tuple-element.35), channel_id=1, source_target_pairs={{0,8},{4,12},{8,0},{12,4},{1,9},{5,13},{9,1},{13,5},{2,10},{6,14},... | collective-permute-start | bytes 393224 | tf_op jit(solution)/shard_map/ppermute | solution.py:276
  39.1 2.9 %collective-permute-done.3.refs_2_ = bf16[1,256,256]{2,1,0:T(8,128)(2,1)S(1)} collective-permute-done((bf16[1,256,256]{2,1,0:T(8,128)(2,1)S(1)}, bf16[1,256,256]{2,1,0:T(8,128)(2,1)S(1)}, u32[]{:S(2)}, u32[]{:S(2)}) %collective-permute-start.3) | collective-permute-done | bytes 131104 | tf_op jit(solution)/shard_map/ppermute | solution.py:276
  42.0 1.8 %collective-permute-done.4.refs_3_ = bf16[1,256,256]{2,1,0:T(8,128)(2,1)S(1)} collective-permute-done((bf16[1,256,256]{2,1,0:T(8,128)(2,1)S(1)}, bf16[1,256,256]{2,1,0:T(8,128)(2,1)S(1)}, u32[]{:S(2)}, u32[]{:S(2)}) %collective-permute-start.4) | collective-permute-done | bytes 131104 | tf_op jit(solution)/shard_map/ppermute | solution.py:276
  43.8 1.7 %add_up.5 = (f32[8,256,256]{2,1,0:T(8,128)}, bf16[8,64,256]{2,1,0:T(8,128)(2,1)S(1)}) custom-call(bf16[1,1040,256]{2,1,0:T(8,128)(2,1)S(1)} %get-tuple-element.22.refs_0_.refs_4_, bf16[1,1040,256]{2,1,0:T(8,128)(2,1)S(1)} %collective-permute-done.refs_1_.refs_5_, ...), custom_call_target="tpu_custom_call", output_to_operand_aliasing={{0}: (7, {})} | custom-call | flops 524288 | bytes 1572864 | tf_op jit(solution)/shard_map/add_up/pallas_call | solution.py:314
  45.4 2.7 %collective-permute-start.8 = (bf16[8,64,256]{2,1,0:T(8,128)(2,1)S(1)}, bf16[8,64,256]{2,1,0:T(8,128)(2,1)S(1)}, u32[]{:S(2)}, u32[]{:S(2)}) collective-permute-start(bf16[8,64,256]{2,1,0:T(8,128)(2,1)S(1)} %get-tuple-element.34), channel_id=1, source_target_pairs={{0,2},{1,3},{2,0},{3,1},{4,6},{5,7},{6,4},{7,5},{8,10},{9,11},{10,... | collective-permute-start | bytes 786440 | tf_op jit(solution)/shard_map/ppermute | solution.py:330
  48.5 1.7 %add_up.6 = (f32[8,256,256]{2,1,0:T(8,128)}, bf16[8,64,256]{2,1,0:T(8,128)(2,1)S(1)}) custom-call(bf16[1,1040,256]{2,1,0:T(8,128)(2,1)S(1)} %get-tuple-element.22.refs_0_.refs_4_, bf16[1,1040,256]{2,1,0:T(8,128)(2,1)S(1)} %collective-permute-done.refs_1_.refs_5_, ...), custom_call_target="tpu_custom_call", output_to_operand_aliasing={{0}: (6, {})} | custom-call | flops 524288 | bytes 1572864 | tf_op jit(solution)/shard_map/add_up/pallas_call | solution.py:314
  50.7 1.5 %collective-permute-start.1 = (bf16[1,256,256]{2,1,0:T(8,128)(2,1)S(1)}, bf16[1,256,256]{2,1,0:T(8,128)(2,1)S(1)}, u32[]{:S(2)}, u32[]{:S(2)}) collective-permute-start(bf16[1,256,256]{2,1,0:T(8,128)(2,1)S(1)} %get-tuple-element.24), channel_id=1, source_target_pairs={{0,8},{4,12},{8,0},{12,4},{1,9},{5,13},{9,1},{13,5},{2,10},{6,14},... | collective-permute-start | bytes 393224 | tf_op jit(solution)/shard_map/ppermute | solution.py:276
  52.6 4.4 %collective-permute-done.1.refs_2_ = bf16[1,256,256]{2,1,0:T(8,128)(2,1)S(1)} collective-permute-done((bf16[1,256,256]{2,1,0:T(8,128)(2,1)S(1)}, bf16[1,256,256]{2,1,0:T(8,128)(2,1)S(1)}, u32[]{:S(2)}, u32[]{:S(2)}) %collective-permute-start.1) | collective-permute-done | bytes 131104 | tf_op jit(solution)/shard_map/ppermute | solution.py:276
  57.0 2.0 %collective-permute-done.2.refs_3_ = bf16[1,256,256]{2,1,0:T(8,128)(2,1)S(1)} collective-permute-done((bf16[1,256,256]{2,1,0:T(8,128)(2,1)S(1)}, bf16[1,256,256]{2,1,0:T(8,128)(2,1)S(1)}, u32[]{:S(2)}, u32[]{:S(2)}) %collective-permute-start.2) | collective-permute-done | bytes 131104 | tf_op jit(solution)/shard_map/ppermute | solution.py:276
  59.0 2.0 %collective-permute-done.8.refs_4_ = bf16[8,64,256]{2,1,0:T(8,128)(2,1)S(1)} collective-permute-done((bf16[8,64,256]{2,1,0:T(8,128)(2,1)S(1)}, bf16[8,64,256]{2,1,0:T(8,128)(2,1)S(1)}, u32[]{:S(2)}, u32[]{:S(2)}) %collective-permute-start.8) | collective-permute-done | bytes 262176 | tf_op jit(solution)/shard_map/ppermute | solution.py:330
  61.0 3.7 %collective-permute-done.11.refs_5_ = bf16[8,64,256]{2,1,0:T(8,128)(2,1)S(1)} collective-permute-done((bf16[8,64,256]{2,1,0:T(8,128)(2,1)S(1)}, bf16[8,64,256]{2,1,0:T(8,128)(2,1)S(1)}, u32[]{:S(2)}, u32[]{:S(2)}) %collective-permute-start.11) | collective-permute-done | bytes 262176 | tf_op jit(solution)/shard_map/ppermute | solution.py:330
  64.7 2.5 %add_up.7 = (f32[8,256,256]{2,1,0:T(8,128)}, f32[8,64,256]{2,1,0:T(8,128)}) custom-call(bf16[1,1040,256]{2,1,0:T(8,128)(2,1)S(1)} %get-tuple-element.22.refs_0_.refs_4_, bf16[1,1040,256]{2,1,0:T(8,128)(2,1)S(1)} %collective-permute-done.refs_1_.refs_5_, bf16[1,256,256]{2,1,0:T(8,128)(2,1)S(1)} %collective-permute-done.1.refs_2_, ...), custom_call_target="tpu_custom_call", output_to_operand_aliasing={{0}: (8, {})} | custom-call | flops 524288 | bytes 1572864 | tf_op jit(solution)/shard_map/add_up/pallas_call | solution.py:314
  (34 shorter events, 9.5 us)
Async XLA Ops:
  1.3 1.6 %copy-start = (f32[1,8,256,256]{3,2,1,0:T(8,128)S(1)}, f32[1,8,256,256]{3,2,1,0:T(8,128)}, u32[]{:S(2)}) copy-start(f32[1,8,256,256]{3,2,1,0:T(8,128)} %param.15) | copy-start | bytes 6291460
  2.9 0.7 %copy-start.1 = (f32[1,12,21]{2,0,1:T(1,128)S(1)}, f32[1,12,21]{2,0,1:T(1,128)}, u32[]{:S(2)}) copy-start(f32[1,12,21]{2,0,1:T(1,128)} %param.20) | copy-start | bytes 3028
  3.6 0.7 %copy-start.2 = (bf16[21,41]{1,0:T(8,128)(2,1)S(1)}, bf16[21,41]{1,0:T(8,128)(2,1)}, u32[]{:S(2)}) copy-start(bf16[21,41]{1,0:T(8,128)(2,1)} %refs_6_.1) | copy-start | bytes 5170
  4.3 0.7 %copy-start.3 = (bf16[21,41]{1,0:T(8,128)(2,1)S(1)}, bf16[21,41]{1,0:T(8,128)(2,1)}, u32[]{:S(2)}) copy-start(bf16[21,41]{1,0:T(8,128)(2,1)} %refs_7_.1) | copy-start | bytes 5170
  5.0 0.7 copy-start.4
  5.6 0.7 copy-start.5
  7.6 0.9 %copy-start.8 = (bf16[512,256]{1,0:T(8,128)(2,1)S(1)}, bf16[512,256]{1,0:T(8,128)(2,1)}, u32[]{:S(2)}) copy-start(bf16[512,256]{1,0:T(8,128)(2,1)} %constant.14.clone.refs_10_) | copy-start | bytes 786436
  8.5 0.9 %copy-start.9 = (bf16[256,512]{1,0:T(8,128)(2,1)S(1)}, bf16[256,512]{1,0:T(8,128)(2,1)}, u32[]{:S(2)}) copy-start(bf16[256,512]{1,0:T(8,128)(2,1)} %constant.12.clone.refs_8_) | copy-start | bytes 786436
  9.5 0.9 %copy-start.10 = (bf16[256,288]{1,0:T(8,128)(2,1)S(1)}, bf16[256,288]{1,0:T(8,128)(2,1)}, u32[]{:S(2)}) copy-start(bf16[256,288]{1,0:T(8,128)(2,1)} %constant.15.clone.refs_11_) | copy-start | bytes 442372
  10.4 0.9 %copy-start.11 = (bf16[288,256]{1,0:T(8,128)(2,1)S(1)}, bf16[288,256]{1,0:T(8,128)(2,1)}, u32[]{:S(2)}) copy-start(bf16[288,256]{1,0:T(8,128)(2,1)} %constant.13.clone.refs_9_) | copy-start | bytes 442372
  11.3 0.9 %copy-start.12 = (bf16[288,41]{1,0:T(8,128)(2,1)S(1)}, bf16[288,41]{1,0:T(8,128)(2,1)}, u32[]{:S(2)}) copy-start(bf16[288,41]{1,0:T(8,128)(2,1)} %constant.17.clone.refs_13_) | copy-start | bytes 70852
  12.2 0.8 %copy-start.13 = (bf16[41,512]{1,0:T(8,128)(2,1)S(1)}, bf16[41,512]{1,0:T(8,128)(2,1)}, u32[]{:S(2)}) copy-start(bf16[41,512]{1,0:T(8,128)(2,1)} %constant.16.clone.refs_12_) | copy-start | bytes 125956
  21.5 10.1 %collective-permute-start = (bf16[1,1040,256]{2,1,0:T(8,128)(2,1)S(1)}, bf16[1,1040,256]{2,1,0:T(8,128)(2,1)S(1)}, u32[]{:S(2)}, u32[]{:S(2)}) collective-permute-start(bf16[1,1040,256]{2,1,0:T(8,128)(2,1)S(1)} %get-tuple-element.23), channel_id=1, source_target_pairs={{0,4},{4,0},{8,12},{12,8},{1,5},{5,1},{9,13},{13,9},{2,6},{6,2},{1... | collective-permute-start | bytes 1597448 | tf_op jit(solution)/shard_map/ppermute | solution.py:276
  22.0 7.1 %collective-permute-start.5 = (bf16[1,272,256]{2,1,0:T(8,128)(2,1)S(1)}, bf16[1,272,256]{2,1,0:T(8,128)(2,1)S(1)}, u32[]{:S(2)}, u32[]{:S(2)}) collective-permute-start(bf16[1,272,256]{2,1,0:T(8,128)(2,1)S(1)} %get-tuple-element.28), channel_id=1, source_target_pairs={{0,8},{4,12},{8,0},{12,4},{1,9},{5,13},{9,1},{13,5},{2,10},{6,14},... | collective-permute-start | bytes 417800 | tf_op jit(solution)/shard_map/ppermute | solution.py:276
  24.6 7.0 %collective-permute-start.6 = (bf16[1,272,256]{2,1,0:T(8,128)(2,1)S(1)}, bf16[1,272,256]{2,1,0:T(8,128)(2,1)S(1)}, u32[]{:S(2)}, u32[]{:S(2)}) collective-permute-start(bf16[1,272,256]{2,1,0:T(8,128)(2,1)S(1)} %get-tuple-element.29), channel_id=1, source_target_pairs={{0,12},{4,8},{8,4},{12,0},{1,13},{5,9},{9,5},{13,1},{2,14},{6,10},... | collective-permute-start | bytes 417800 | tf_op jit(solution)/shard_map/ppermute | solution.py:276
  33.9 9.9 %collective-permute-start.7 = (bf16[8,64,256]{2,1,0:T(8,128)(2,1)S(1)}, bf16[8,64,256]{2,1,0:T(8,128)(2,1)S(1)}, u32[]{:S(2)}, u32[]{:S(2)}) collective-permute-start(bf16[8,64,256]{2,1,0:T(8,128)(2,1)S(1)} %get-tuple-element.30), channel_id=1, source_target_pairs={{0,1},{1,0},{2,3},{3,2},{4,5},{5,4},{6,7},{7,6},{8,9},{9,8},{10,11... | collective-permute-start | bytes 786440 | tf_op jit(solution)/shard_map/ppermute | solution.py:330
  35.6 6.4 %collective-permute-start.3 = (bf16[1,256,256]{2,1,0:T(8,128)(2,1)S(1)}, bf16[1,256,256]{2,1,0:T(8,128)(2,1)S(1)}, u32[]{:S(2)}, u32[]{:S(2)}) collective-permute-start(bf16[1,256,256]{2,1,0:T(8,128)(2,1)S(1)} %get-tuple-element.26), channel_id=1, source_target_pairs={{0,8},{4,12},{8,0},{12,4},{1,9},{5,13},{9,1},{13,5},{2,10},{6,14},... | collective-permute-start | bytes 393224 | tf_op jit(solution)/shard_map/ppermute | solution.py:276
  37.1 6.7 %collective-permute-start.4 = (bf16[1,256,256]{2,1,0:T(8,128)(2,1)S(1)}, bf16[1,256,256]{2,1,0:T(8,128)(2,1)S(1)}, u32[]{:S(2)}, u32[]{:S(2)}) collective-permute-start(bf16[1,256,256]{2,1,0:T(8,128)(2,1)S(1)} %get-tuple-element.27), channel_id=1, source_target_pairs={{0,12},{4,8},{8,4},{12,0},{1,13},{5,9},{9,5},{13,1},{2,14},{6,10},... | collective-permute-start | bytes 393224 | tf_op jit(solution)/shard_map/ppermute | solution.py:276
  37.1 11.0 %collective-permute-start.9 = (bf16[1,256,256]{2,1,0:T(8,128)(2,1)S(1)}, bf16[1,256,256]{2,1,0:T(8,128)(2,1)S(1)}, u32[]{:S(2)}, u32[]{:S(2)}) collective-permute-start(bf16[1,256,256]{2,1,0:T(8,128)(2,1)S(1)} %get-tuple-element.35), channel_id=1, source_target_pairs={{0,8},{4,12},{8,0},{12,4},{1,9},{5,13},{9,1},{13,5},{2,10},{6,14},... | collective-permute-start | bytes 393224 | tf_op jit(solution)/shard_map/ppermute | solution.py:276
  38.5 10.0 %collective-permute-start.10 = (bf16[1,256,256]{2,1,0:T(8,128)(2,1)S(1)}, bf16[1,256,256]{2,1,0:T(8,128)(2,1)S(1)}, u32[]{:S(2)}, u32[]{:S(2)}) collective-permute-start(bf16[1,256,256]{2,1,0:T(8,128)(2,1)S(1)} %get-tuple-element.36), channel_id=1, source_target_pairs={{0,12},{4,8},{8,4},{12,0},{1,13},{5,9},{9,5},{13,1},{2,14},{6,10},... | collective-permute-start | bytes 393224 | tf_op jit(solution)/shard_map/ppermute | solution.py:276
  45.4 15.6 %collective-permute-start.8 = (bf16[8,64,256]{2,1,0:T(8,128)(2,1)S(1)}, bf16[8,64,256]{2,1,0:T(8,128)(2,1)S(1)}, u32[]{:S(2)}, u32[]{:S(2)}) collective-permute-start(bf16[8,64,256]{2,1,0:T(8,128)(2,1)S(1)} %get-tuple-element.34), channel_id=1, source_target_pairs={{0,2},{1,3},{2,0},{3,1},{4,6},{5,7},{6,4},{7,5},{8,10},{9,11},{10,... | collective-permute-start | bytes 786440 | tf_op jit(solution)/shard_map/ppermute | solution.py:330
  50.2 14.6 %collective-permute-start.11 = (bf16[8,64,256]{2,1,0:T(8,128)(2,1)S(1)}, bf16[8,64,256]{2,1,0:T(8,128)(2,1)S(1)}, u32[]{:S(2)}, u32[]{:S(2)}) collective-permute-start(bf16[8,64,256]{2,1,0:T(8,128)(2,1)S(1)} %get-tuple-element.38), channel_id=1, source_target_pairs={{0,1},{1,0},{2,3},{3,2},{4,5},{5,4},{6,7},{7,6},{8,9},{9,8},{10,11... | collective-permute-start | bytes 786440 | tf_op jit(solution)/shard_map/ppermute | solution.py:330
  50.7 6.3 %collective-permute-start.1 = (bf16[1,256,256]{2,1,0:T(8,128)(2,1)S(1)}, bf16[1,256,256]{2,1,0:T(8,128)(2,1)S(1)}, u32[]{:S(2)}, u32[]{:S(2)}) collective-permute-start(bf16[1,256,256]{2,1,0:T(8,128)(2,1)S(1)} %get-tuple-element.24), channel_id=1, source_target_pairs={{0,8},{4,12},{8,0},{12,4},{1,9},{5,13},{9,1},{13,5},{2,10},{6,14},... | collective-permute-start | bytes 393224 | tf_op jit(solution)/shard_map/ppermute | solution.py:276
  52.2 6.8 %collective-permute-start.2 = (bf16[1,256,256]{2,1,0:T(8,128)(2,1)S(1)}, bf16[1,256,256]{2,1,0:T(8,128)(2,1)S(1)}, u32[]{:S(2)}, u32[]{:S(2)}) collective-permute-start(bf16[1,256,256]{2,1,0:T(8,128)(2,1)S(1)} %get-tuple-element.25), channel_id=1, source_target_pairs={{0,12},{4,8},{8,4},{12,0},{1,13},{5,9},{9,5},{13,1},{2,14},{6,10},... | collective-permute-start | bytes 393224 | tf_op jit(solution)/shard_map/ppermute | solution.py:276
  (2 other events, 1.3 us)

commit v3 on v2

--- a/solution.py
+++ b/solution.py
@@ -13,7 +13,9 @@
 F32, BF16 = jnp.float32, jnp.bfloat16
 MIB = 1024 * 1024
 HEAD = 16
-UNROLL = 2
+UNROLL = 4
+CONV_VMEM = 64
+SUM_VMEM = 24
 
 
 def round_up(value, multiple):
@@ -67,7 +69,7 @@
 def convolve_kernel(plan, *refs):
     n_in, n_out = plan["n_in"], plan["n_out"]
     sources, outs, held = refs[:n_in], refs[n_in : n_in + n_out], refs[n_in + n_out :]
-    local, (sems, row_waves, col_waves, back, heads) = held[:n_in], held[n_in:]
+    local, (sems, out_sems, row_waves, col_waves, back, heads, done, head_rows) = held[:n_in], held[n_in:]
     sub, lane, rows, nb, cap, slots = (plan[k] for k in ("sub", "lane", "rows", "nb", "cap", "slots"))
     copies = [pltpu.make_async_copy(a, b, sems.at[i]) for i, (a, b) in enumerate(zip(sources[:-1], local[:-1]))]
     tiles = [
@@ -105,7 +107,11 @@
         z_s = dot(y_sc, from_col[:lane, :]) + dot(y_ss, from_col[lane:, :])
         return (dot(back[:, :sub], z_c.astype(BF16)) + dot(back[:, sub:], z_s.astype(BF16))).astype(BF16)
 
+    def sent(slot, phase, ref):
+        return pltpu.make_async_copy(done.at[slot, phase * rows : (phase + 1) * rows, :], ref, out_sems.at[slot, phase])
+
     def deliver(slot, full):
+        done[slot] = full
         mine = owner[0, slot]
         rank = jnp.int32(0)
         for other in range(slots):
@@ -122,7 +128,7 @@
                 for phase in range(nb):
                     ref, first = plan["place"](outs, group, phase)
                     start = pl.multiple_of(first + rank * rows, rows)
-                    ref[at, pl.ds(start, rows), :] = full[phase * rows : (phase + 1) * rows, :]
+                    sent(slot, phase, ref.at[at, pl.ds(start, rows), :]).start()
 
             if plan["single"]:
                 store()
@@ -140,12 +146,21 @@
 
     lax.fori_loop(0, slots // UNROLL, some, 0)
     width = patch.shape[2]
+    copies = []
     for group in range(len(plan["split"])):
         ref, first = plan["head"](outs, group)
         for at in range(ref.shape[0]):
-            row = heads[at if plan["single"] else group]
-            row = jnp.concatenate([row] * (width // 128), axis=1)
-            ref[at, first : first + HEAD, :] = jnp.broadcast_to(row, (HEAD, width)).astype(BF16)
+            index = at if plan["single"] else group
+            row = jnp.concatenate([heads[index]] * (width // 128), axis=1)
+            head_rows[index] = jnp.broadcast_to(row, (HEAD, width)).astype(BF16)
+            copies.append(pltpu.make_async_copy(
+                head_rows.at[index], ref.at[at, first : first + HEAD, :], sems.at[index]))
+            copies[-1].start()
+    for copy in copies:
+        copy.wait()
+    for slot in range(slots):
+        for phase in range(nb):
+            sent(slot, phase, plan["place"](outs, 0, phase)[0].at[0, 0:rows, :]).wait()
 
 
 def sum_kernel(plan, phase, *refs):
@@ -251,10 +266,8 @@
                 single=single, split=split, place=place, head=head, chunk=chunk, adds=adds)
     smem = pl.BlockSpec(memory_space=pltpu.SMEM)
     hbm = pl.BlockSpec(memory_space=pltpu.HBM)
-    vmem = pl.BlockSpec(memory_space=pltpu.VMEM)
     consts = [jnp.asarray(tables[n]) for n in ("to_col", "to_row", "from_col", "from_row", "tap_col", "tap_row")]
-    weights = lax.reduce_precision(inv_var, 8, 7)
-    args = [slot_owner.reshape(1, slots), slot_local, valid_rows, slot_visit, weights, basis_coef.transpose(1, 0, 2),
+    args = [slot_owner.reshape(1, slots), slot_local, valid_rows, slot_visit, inv_var, basis_coef.transpose(1, 0, 2),
             kernel_x, kernel_y] + consts + [tiles]
     plan.update(n_in=len(args), n_out=len(out_shapes))
     landing = [pltpu.SMEM(a.shape, a.dtype) for a in args[:5]] + [pltpu.VMEM(a.shape, a.dtype) for a in args[5:]]
@@ -262,12 +275,14 @@
         functools.partial(convolve_kernel, plan),
         out_shape=out_shapes,
         in_specs=[hbm] * len(args),
-        out_specs=[vmem] * len(out_shapes),
+        out_specs=[hbm] * len(out_shapes),
         scratch_shapes=landing + [
-            pltpu.SemaphoreType.DMA((len(args) - 1 + slots,)), pltpu.VMEM((2 * sub, kernel_x.shape[0]), F32),
+            pltpu.SemaphoreType.DMA((max(len(args) - 1 + slots, sky),)), pltpu.SemaphoreType.DMA((slots, nb)),
+            pltpu.VMEM((2 * sub, kernel_x.shape[0]), F32),
             pltpu.VMEM((kernel_x.shape[0], 2 * lane), BF16), pltpu.VMEM((side, 2 * sub), BF16),
-            pltpu.VMEM((sky, 1, 128), F32)],
-        compiler_params=pltpu.CompilerParams(vmem_limit_bytes=40 * MIB),
+            pltpu.VMEM((sky, 1, 128), F32),
+            pltpu.VMEM((slots, side, width), BF16), pltpu.VMEM((sky, HEAD, width), BF16)],
+        compiler_params=pltpu.CompilerParams(vmem_limit_bytes=CONV_VMEM * MIB),
         cost_estimate=pl.CostEstimate(flops=slots * 22 * side**3, bytes_accessed=slots * side * side * 6,
                                       transcendentals=0),
         name="convolve",
@@ -320,7 +335,7 @@
             scratch_shapes=[pltpu.VMEM(chunk_shape, F32), pltpu.VMEM((PATCH_DEV, rows, 128), F32),
                             pltpu.SemaphoreType.DMA((PATCH_DEV,))] + scratch,
             input_output_aliases=aliases,
-            compiler_params=pltpu.CompilerParams(vmem_limit_bytes=24 * MIB),
+            compiler_params=pltpu.CompilerParams(vmem_limit_bytes=SUM_VMEM * MIB),
             cost_estimate=pl.CostEstimate(flops=4 * PATCH_DEV * rows * width,
                                           bytes_accessed=12 * PATCH_DEV * rows * width, transcendentals=0),
             name="add_up",

time: 67.7 us -> 56.7 us (0.84)
  local copies, waits for them, and re-layouts: 11.7 us -> 1.07 us
    unnamed x28 -> x14, local copies, waits for them, and re-layouts: 11.7 us -> 1.07 us
  transfers between devices with their start and end apart: 12 -> 12, of which waited for: 9 -> 9; matrix products, arithmetic and copies ran while one was open for 0% -> 0% of each run, Pallas kernels for 5% -> 6%
where the time goes in v3:
time: 56.7 us; the launch traced here: 56.5 us
  waiting for transfers between devices  24.3 us (43%)
  Pallas kernels  17.2 us (30%)
  starting transfers between devices  13.3 us (23%)
  local copies, waits for them, and re-layouts  1.07 us (2%)
  between operations  0.7 us (1%)
    ppermute x9, waiting for transfers between devices, per_device(): lax.ppermute(a, 'sky', [(i, i ^ r) for i in range(sky)])  18.3 us
    pallas_call x1, Pallas kernels, per_device(): pl.pallas_call(functools.partial(convolve_kernel, plan), out_shape=out_sh...  8.82 us
    ppermute x9, starting transfers between devices, per_device(): lax.ppermute(a, 'sky', [(i, i ^ r) for i in range(sky)])  8.47 us
    pallas_call x4, Pallas kernels, per_device(): pl.pallas_call(functools.partial(sum_kernel, plan, phase), grid=(1,), out...  8.34 us
    ppermute x3, waiting for transfers between devices, per_device(): lax.ppermute(extra, 'band', [(b, partner(b, phase)) for b in range(nb)])  5.94 us
    ppermute x3, starting transfers between devices, per_device(): lax.ppermute(extra, 'band', [(b, partner(b, phase)) for b in range(nb)])  4.87 us
  transfers between devices with their start and end apart: 12, of which 9 were waited for; matrix products, arithmetic and copies ran while one was open for 0% of the time, Pallas kernels for 6%

profile of v3, /device:TPU:0, one launch (start us, length us, event | category | flops | bytes accessed | tf_op | source)
XLA Modules:
  0.0 56.5 jit_solution(6877155079583132110)
XLA Ops:
  0.6 8.8 %convolve.1 = (bf16[1,1040,256]{2,1,0:T(8,128)(2,1)}, bf16[1,1040,256]{2,1,0:T(8,128)(2,1)}, bf16[1,272,256]{2,1,0:T(8,128)(2,1)}, bf16[1,256,256]{2,1,0:T(8,128...) custom-call(s32[1,8]{1,0:T(1,128)} %bitcast.7, ...), custom_call_target="tpu_custom_call" | custom-call | flops 2952790016 | bytes 3145728 | tf_op jit(solution)/shard_map/convolve/pallas_call | solution.py:274
  9.5 0.5 collective-permute-start
  10.0 2.6 %collective-permute-start.5 = (bf16[1,272,256]{2,1,0:T(8,128)(2,1)}, bf16[1,272,256]{2,1,0:T(8,128)(2,1)S(1)}, u32[]{:S(2)}, u32[]{:S(2)}) collective-permute-start(bf16[1,272,256]{2,1,0:T(8,128)(2,1)} %get-tuple-element.28), channel_id=1, source_target_pairs={{0,8},{4,12},{8,0},{12,4},{1,9},{5,13},{9,1},{13,5},{2,10},{6,14},... | collective-permute-start | bytes 417800 | tf_op jit(solution)/shard_map/ppermute | solution.py:291
  12.6 4.7 %collective-permute-done.5.refs_2_.refs_6_ = bf16[1,272,256]{2,1,0:T(8,128)(2,1)S(1)} collective-permute-done((bf16[1,272,256]{2,1,0:T(8,128)(2,1)}, bf16[1,272,256]{2,1,0:T(8,128)(2,1)S(1)}, u32[]{:S(2)}, u32[]{:S(2)}) %collective-permute-start.5) | collective-permute-done | bytes 139296 | tf_op jit(solution)/shard_map/ppermute | solution.py:291
  17.3 2.5 %collective-permute-done.6.refs_3_.refs_7_ = bf16[1,272,256]{2,1,0:T(8,128)(2,1)S(1)} collective-permute-done((bf16[1,272,256]{2,1,0:T(8,128)(2,1)}, bf16[1,272,256]{2,1,0:T(8,128)(2,1)S(1)}, u32[]{:S(2)}, u32[]{:S(2)}) %collective-permute-start.6) | collective-permute-done | bytes 139296 | tf_op jit(solution)/shard_map/ppermute | solution.py:291
  19.7 1.0 %copy-done = bf16[1,1040,256]{2,1,0:T(8,128)(2,1)S(1)} copy-done((bf16[1,1040,256]{2,1,0:T(8,128)(2,1)S(1)}, bf16[1,1040,256]{2,1,0:T(8,128)(2,1)}, u32[]{:S(2)}) %copy-start) | copy-done | bytes 532504
  20.8 2.4 %add_up.4 = (f32[8,256,256]{2,1,0:T(8,128)}, bf16[8,64,256]{2,1,0:T(8,128)(2,1)S(1)}, s32[4,128]{1,0:T(4,128)S(1)}, f32[4,128]{1,0:T(4,128)S(1)}) custom-call(bf16[1,1040,256]{2,1,0:T(8,128)(2,1)S(1)} %copy-done, bf16[1,1040,256]{2,1,0:T(8,128)(2,1)S(1)} %collective-permute-done.refs_1_.refs_5_, ...), custom_call_target="tpu_custom_call" | custom-call | flops 524288 | bytes 1572864 | tf_op jit(solution)/shard_map/add_up/pallas_call | solution.py:329
  23.2 1.7 %collective-permute-start.7 = (bf16[8,64,256]{2,1,0:T(8,128)(2,1)S(1)}, bf16[8,64,256]{2,1,0:T(8,128)(2,1)S(1)}, u32[]{:S(2)}, u32[]{:S(2)}) collective-permute-start(bf16[8,64,256]{2,1,0:T(8,128)(2,1)S(1)} %get-tuple-element.30), channel_id=1, source_target_pairs={{0,1},{1,0},{2,3},{3,2},{4,5},{5,4},{6,7},{7,6},{8,9},{9,8},{10,11... | collective-permute-start | bytes 786440 | tf_op jit(solution)/shard_map/ppermute | solution.py:345
  24.9 1.4 %collective-permute-start.3 = (bf16[1,256,256]{2,1,0:T(8,128)(2,1)S(1)}, bf16[1,256,256]{2,1,0:T(8,128)(2,1)S(1)}, u32[]{:S(2)}, u32[]{:S(2)}) collective-permute-start(bf16[1,256,256]{2,1,0:T(8,128)(2,1)S(1)} %copy-done.6), channel_id=1, source_target_pairs={{0,8},{4,12},{8,0},{12,4},{1,9},{5,13},{9,1},{13,5},{2,10},{6,14},... | collective-permute-start | bytes 393224 | tf_op jit(solution)/shard_map/ppermute | solution.py:291
  26.4 1.4 %collective-permute-start.9 = (bf16[1,256,256]{2,1,0:T(8,128)(2,1)S(1)}, bf16[1,256,256]{2,1,0:T(8,128)(2,1)S(1)}, u32[]{:S(2)}, u32[]{:S(2)}) collective-permute-start(bf16[1,256,256]{2,1,0:T(8,128)(2,1)S(1)} %copy-done.4), channel_id=1, source_target_pairs={{0,8},{4,12},{8,0},{12,4},{1,9},{5,13},{9,1},{13,5},{2,10},{6,14},... | collective-permute-start | bytes 393224 | tf_op jit(solution)/shard_map/ppermute | solution.py:291
  27.7 0.7 %collective-permute-start.10 = (bf16[1,256,256]{2,1,0:T(8,128)(2,1)S(1)}, bf16[1,256,256]{2,1,0:T(8,128)(2,1)S(1)}, u32[]{:S(2)}, u32[]{:S(2)}) collective-permute-start(bf16[1,256,256]{2,1,0:T(8,128)(2,1)S(1)} %copy-done.3), channel_id=1, source_target_pairs={{0,12},{4,8},{8,4},{12,0},{1,13},{5,9},{9,5},{13,1},{2,14},{6,10},... | collective-permute-start | bytes 393224 | tf_op jit(solution)/shard_map/ppermute | solution.py:291
  28.4 2.8 %collective-permute-done.3.refs_2_ = bf16[1,256,256]{2,1,0:T(8,128)(2,1)S(1)} collective-permute-done((bf16[1,256,256]{2,1,0:T(8,128)(2,1)S(1)}, bf16[1,256,256]{2,1,0:T(8,128)(2,1)S(1)}, u32[]{:S(2)}, u32[]{:S(2)}) %collective-permute-start.3) | collective-permute-done | bytes 131104 | tf_op jit(solution)/shard_map/ppermute | solution.py:291
  31.2 1.8 %collective-permute-done.4.refs_3_ = bf16[1,256,256]{2,1,0:T(8,128)(2,1)S(1)} collective-permute-done((bf16[1,256,256]{2,1,0:T(8,128)(2,1)S(1)}, bf16[1,256,256]{2,1,0:T(8,128)(2,1)S(1)}, u32[]{:S(2)}, u32[]{:S(2)}) %collective-permute-start.4) | collective-permute-done | bytes 131104 | tf_op jit(solution)/shard_map/ppermute | solution.py:291
  33.0 1.7 %add_up.5 = (f32[8,256,256]{2,1,0:T(8,128)}, bf16[8,64,256]{2,1,0:T(8,128)(2,1)S(1)}) custom-call(bf16[1,1040,256]{2,1,0:T(8,128)(2,1)S(1)} %copy-done, bf16[1,1040,256]{2,1,0:T(8,128)(2,1)S(1)} %collective-permute-done.refs_1_.refs_5_, bf16[1,256,256]{2,1,0:T(8,128)(2,1)S(1)} %collective-permute-done.3.refs_2_, ...), custom_call_target="tpu_custom_call", output_to_operand_aliasing={{0}: (7, {})} | custom-call | flops 524288 | bytes 1572864 | tf_op jit(solution)/shard_map/add_up/pallas_call | solution.py:329
  34.8 2.6 %collective-permute-start.8 = (bf16[8,64,256]{2,1,0:T(8,128)(2,1)S(1)}, bf16[8,64,256]{2,1,0:T(8,128)(2,1)S(1)}, u32[]{:S(2)}, u32[]{:S(2)}) collective-permute-start(bf16[8,64,256]{2,1,0:T(8,128)(2,1)S(1)} %get-tuple-element.34), channel_id=1, source_target_pairs={{0,2},{1,3},{2,0},{3,1},{4,6},{5,7},{6,4},{7,5},{8,10},{9,11},{10,... | collective-permute-start | bytes 786440 | tf_op jit(solution)/shard_map/ppermute | solution.py:345
  37.7 1.7 %add_up.6 = (f32[8,256,256]{2,1,0:T(8,128)}, bf16[8,64,256]{2,1,0:T(8,128)(2,1)S(1)}) custom-call(bf16[1,1040,256]{2,1,0:T(8,128)(2,1)S(1)} %copy-done, bf16[1,1040,256]{2,1,0:T(8,128)(2,1)S(1)} %collective-permute-done.refs_1_.refs_5_, bf16[1,256,256]{2,1,0:T(8,128)(2,1)S(1)} %collective-permute-done.9.refs_2_, ...), custom_call_target="tpu_custom_call", output_to_operand_aliasing={{0}: (6, {})} | custom-call | flops 524288 | bytes 1572864 | tf_op jit(solution)/shard_map/add_up/pallas_call | solution.py:329
  39.5 0.5 collective-permute-start.11
  40.0 1.4 %collective-permute-start.1 = (bf16[1,256,256]{2,1,0:T(8,128)(2,1)S(1)}, bf16[1,256,256]{2,1,0:T(8,128)(2,1)S(1)}, u32[]{:S(2)}, u32[]{:S(2)}) collective-permute-start(bf16[1,256,256]{2,1,0:T(8,128)(2,1)S(1)} %copy-done.2), channel_id=1, source_target_pairs={{0,8},{4,12},{8,0},{12,4},{1,9},{5,13},{9,1},{13,5},{2,10},{6,14},... | collective-permute-start | bytes 393224 | tf_op jit(solution)/shard_map/ppermute | solution.py:291
  41.4 0.4 collective-permute-start.2
  41.8 4.5 %collective-permute-done.1.refs_2_ = bf16[1,256,256]{2,1,0:T(8,128)(2,1)S(1)} collective-permute-done((bf16[1,256,256]{2,1,0:T(8,128)(2,1)S(1)}, bf16[1,256,256]{2,1,0:T(8,128)(2,1)S(1)}, u32[]{:S(2)}, u32[]{:S(2)}) %collective-permute-start.1) | collective-permute-done | bytes 131104 | tf_op jit(solution)/shard_map/ppermute | solution.py:291
  46.3 1.8 %collective-permute-done.2.refs_3_ = bf16[1,256,256]{2,1,0:T(8,128)(2,1)S(1)} collective-permute-done((bf16[1,256,256]{2,1,0:T(8,128)(2,1)S(1)}, bf16[1,256,256]{2,1,0:T(8,128)(2,1)S(1)}, u32[]{:S(2)}, u32[]{:S(2)}) %collective-permute-start.2) | collective-permute-done | bytes 131104 | tf_op jit(solution)/shard_map/ppermute | solution.py:291
  48.1 2.2 %collective-permute-done.8.refs_4_ = bf16[8,64,256]{2,1,0:T(8,128)(2,1)S(1)} collective-permute-done((bf16[8,64,256]{2,1,0:T(8,128)(2,1)S(1)}, bf16[8,64,256]{2,1,0:T(8,128)(2,1)S(1)}, u32[]{:S(2)}, u32[]{:S(2)}) %collective-permute-start.8) | collective-permute-done | bytes 262176 | tf_op jit(solution)/shard_map/ppermute | solution.py:345
  50.3 3.7 %collective-permute-done.11.refs_5_ = bf16[8,64,256]{2,1,0:T(8,128)(2,1)S(1)} collective-permute-done((bf16[8,64,256]{2,1,0:T(8,128)(2,1)S(1)}, bf16[8,64,256]{2,1,0:T(8,128)(2,1)S(1)}, u32[]{:S(2)}, u32[]{:S(2)}) %collective-permute-start.11) | collective-permute-done | bytes 262176 | tf_op jit(solution)/shard_map/ppermute | solution.py:345
  54.0 2.5 %add_up.7 = (f32[8,256,256]{2,1,0:T(8,128)}, f32[8,64,256]{2,1,0:T(8,128)}) custom-call(bf16[1,1040,256]{2,1,0:T(8,128)(2,1)S(1)} %copy-done, bf16[1,1040,256]{2,1,0:T(8,128)(2,1)S(1)} %collective-permute-done.refs_1_.refs_5_, bf16[1,256,256]{2,1,0:T(8,128)(2,1)S(1)} %collective-permute-done.1.refs_2_, ...), custom_call_target="tpu_custom_call", output_to_operand_aliasing={{0}: (8, {})} | custom-call | flops 524288 | bytes 1572864 | tf_op jit(solution)/shard_map/add_up/pallas_call | solution.py:329
  (19 shorter events, 0.4 us)
Async XLA Ops:
  9.5 10.3 %collective-permute-start = (bf16[1,1040,256]{2,1,0:T(8,128)(2,1)}, bf16[1,1040,256]{2,1,0:T(8,128)(2,1)S(1)}, u32[]{:S(2)}, u32[]{:S(2)}) collective-permute-start(bf16[1,1040,256]{2,1,0:T(8,128)(2,1)} %get-tuple-element.23), channel_id=1, source_target_pairs={{0,4},{4,0},{8,12},{12,8},{1,5},{5,1},{9,13},{13,9},{2,6},{6,2},{1... | collective-permute-start | bytes 1597448 | tf_op jit(solution)/shard_map/ppermute | solution.py:291
  10.0 7.3 %collective-permute-start.5 = (bf16[1,272,256]{2,1,0:T(8,128)(2,1)}, bf16[1,272,256]{2,1,0:T(8,128)(2,1)S(1)}, u32[]{:S(2)}, u32[]{:S(2)}) collective-permute-start(bf16[1,272,256]{2,1,0:T(8,128)(2,1)} %get-tuple-element.28), channel_id=1, source_target_pairs={{0,8},{4,12},{8,0},{12,4},{1,9},{5,13},{9,1},{13,5},{2,10},{6,14},... | collective-permute-start | bytes 417800 | tf_op jit(solution)/shard_map/ppermute | solution.py:291
  12.5 7.2 %collective-permute-start.6 = (bf16[1,272,256]{2,1,0:T(8,128)(2,1)}, bf16[1,272,256]{2,1,0:T(8,128)(2,1)S(1)}, u32[]{:S(2)}, u32[]{:S(2)}) collective-permute-start(bf16[1,272,256]{2,1,0:T(8,128)(2,1)} %get-tuple-element.29), channel_id=1, source_target_pairs={{0,12},{4,8},{8,4},{12,0},{1,13},{5,9},{9,5},{13,1},{2,14},{6,10},... | collective-permute-start | bytes 417800 | tf_op jit(solution)/shard_map/ppermute | solution.py:291
  19.7 1.0 %copy-start = (bf16[1,1040,256]{2,1,0:T(8,128)(2,1)S(1)}, bf16[1,1040,256]{2,1,0:T(8,128)(2,1)}, u32[]{:S(2)}) copy-start(bf16[1,1040,256]{2,1,0:T(8,128)(2,1)} %get-tuple-element.22.refs_0_.refs_4_) | copy-start | bytes 1597444
  20.8 4.1 %copy-start.6 = (bf16[1,256,256]{2,1,0:T(8,128)(2,1)S(1)}, bf16[1,256,256]{2,1,0:T(8,128)(2,1)}, u32[]{:S(2)}) copy-start(bf16[1,256,256]{2,1,0:T(8,128)(2,1)} %get-tuple-element.26) | copy-start | bytes 393220
  20.8 5.6 %copy-start.5 = (bf16[1,256,256]{2,1,0:T(8,128)(2,1)S(1)}, bf16[1,256,256]{2,1,0:T(8,128)(2,1)}, u32[]{:S(2)}) copy-start(bf16[1,256,256]{2,1,0:T(8,128)(2,1)} %get-tuple-element.27) | copy-start | bytes 393220
  20.8 5.6 %copy-start.4 = (bf16[1,256,256]{2,1,0:T(8,128)(2,1)S(1)}, bf16[1,256,256]{2,1,0:T(8,128)(2,1)}, u32[]{:S(2)}) copy-start(bf16[1,256,256]{2,1,0:T(8,128)(2,1)} %get-tuple-element.35) | copy-start | bytes 393220
  20.8 6.9 %copy-start.3 = (bf16[1,256,256]{2,1,0:T(8,128)(2,1)S(1)}, bf16[1,256,256]{2,1,0:T(8,128)(2,1)}, u32[]{:S(2)}) copy-start(bf16[1,256,256]{2,1,0:T(8,128)(2,1)} %get-tuple-element.36) | copy-start | bytes 393220
  23.2 9.8 %collective-permute-start.7 = (bf16[8,64,256]{2,1,0:T(8,128)(2,1)S(1)}, bf16[8,64,256]{2,1,0:T(8,128)(2,1)S(1)}, u32[]{:S(2)}, u32[]{:S(2)}) collective-permute-start(bf16[8,64,256]{2,1,0:T(8,128)(2,1)S(1)} %get-tuple-element.30), channel_id=1, source_target_pairs={{0,1},{1,0},{2,3},{3,2},{4,5},{5,4},{6,7},{7,6},{8,9},{9,8},{10,11... | collective-permute-start | bytes 786440 | tf_op jit(solution)/shard_map/ppermute | solution.py:345
  24.9 6.3 %collective-permute-start.3 = (bf16[1,256,256]{2,1,0:T(8,128)(2,1)S(1)}, bf16[1,256,256]{2,1,0:T(8,128)(2,1)S(1)}, u32[]{:S(2)}, u32[]{:S(2)}) collective-permute-start(bf16[1,256,256]{2,1,0:T(8,128)(2,1)S(1)} %copy-done.6), channel_id=1, source_target_pairs={{0,8},{4,12},{8,0},{12,4},{1,9},{5,13},{9,1},{13,5},{2,10},{6,14},... | collective-permute-start | bytes 393224 | tf_op jit(solution)/shard_map/ppermute | solution.py:291
  26.3 6.7 %collective-permute-start.4 = (bf16[1,256,256]{2,1,0:T(8,128)(2,1)S(1)}, bf16[1,256,256]{2,1,0:T(8,128)(2,1)S(1)}, u32[]{:S(2)}, u32[]{:S(2)}) collective-permute-start(bf16[1,256,256]{2,1,0:T(8,128)(2,1)S(1)} %copy-done.5), channel_id=1, source_target_pairs={{0,12},{4,8},{8,4},{12,0},{1,13},{5,9},{9,5},{13,1},{2,14},{6,10},... | collective-permute-start | bytes 393224 | tf_op jit(solution)/shard_map/ppermute | solution.py:291
  26.4 11.1 %collective-permute-start.9 = (bf16[1,256,256]{2,1,0:T(8,128)(2,1)S(1)}, bf16[1,256,256]{2,1,0:T(8,128)(2,1)S(1)}, u32[]{:S(2)}, u32[]{:S(2)}) collective-permute-start(bf16[1,256,256]{2,1,0:T(8,128)(2,1)S(1)} %copy-done.4), channel_id=1, source_target_pairs={{0,8},{4,12},{8,0},{12,4},{1,9},{5,13},{9,1},{13,5},{2,10},{6,14},... | collective-permute-start | bytes 393224 | tf_op jit(solution)/shard_map/ppermute | solution.py:291
  27.7 10.0 %collective-permute-start.10 = (bf16[1,256,256]{2,1,0:T(8,128)(2,1)S(1)}, bf16[1,256,256]{2,1,0:T(8,128)(2,1)S(1)}, u32[]{:S(2)}, u32[]{:S(2)}) collective-permute-start(bf16[1,256,256]{2,1,0:T(8,128)(2,1)S(1)} %copy-done.3), channel_id=1, source_target_pairs={{0,12},{4,8},{8,4},{12,0},{1,13},{5,9},{9,5},{13,1},{2,14},{6,10},... | collective-permute-start | bytes 393224 | tf_op jit(solution)/shard_map/ppermute | solution.py:291
  34.8 5.2 %copy-start.2 = (bf16[1,256,256]{2,1,0:T(8,128)(2,1)S(1)}, bf16[1,256,256]{2,1,0:T(8,128)(2,1)}, u32[]{:S(2)}) copy-start(bf16[1,256,256]{2,1,0:T(8,128)(2,1)} %get-tuple-element.24) | copy-start | bytes 393220
  34.8 6.6 %copy-start.1 = (bf16[1,256,256]{2,1,0:T(8,128)(2,1)S(1)}, bf16[1,256,256]{2,1,0:T(8,128)(2,1)}, u32[]{:S(2)}) copy-start(bf16[1,256,256]{2,1,0:T(8,128)(2,1)} %get-tuple-element.25) | copy-start | bytes 393220
  34.8 15.5 %collective-permute-start.8 = (bf16[8,64,256]{2,1,0:T(8,128)(2,1)S(1)}, bf16[8,64,256]{2,1,0:T(8,128)(2,1)S(1)}, u32[]{:S(2)}, u32[]{:S(2)}) collective-permute-start(bf16[8,64,256]{2,1,0:T(8,128)(2,1)S(1)} %get-tuple-element.34), channel_id=1, source_target_pairs={{0,2},{1,3},{2,0},{3,1},{4,6},{5,7},{6,4},{7,5},{8,10},{9,11},{10,... | collective-permute-start | bytes 786440 | tf_op jit(solution)/shard_map/ppermute | solution.py:345
  39.5 14.5 %collective-permute-start.11 = (bf16[8,64,256]{2,1,0:T(8,128)(2,1)S(1)}, bf16[8,64,256]{2,1,0:T(8,128)(2,1)S(1)}, u32[]{:S(2)}, u32[]{:S(2)}) collective-permute-start(bf16[8,64,256]{2,1,0:T(8,128)(2,1)S(1)} %get-tuple-element.38), channel_id=1, source_target_pairs={{0,1},{1,0},{2,3},{3,2},{4,5},{5,4},{6,7},{7,6},{8,9},{9,8},{10,11... | collective-permute-start | bytes 786440 | tf_op jit(solution)/shard_map/ppermute | solution.py:345
  40.0 6.3 %collective-permute-start.1 = (bf16[1,256,256]{2,1,0:T(8,128)(2,1)S(1)}, bf16[1,256,256]{2,1,0:T(8,128)(2,1)S(1)}, u32[]{:S(2)}, u32[]{:S(2)}) collective-permute-start(bf16[1,256,256]{2,1,0:T(8,128)(2,1)S(1)} %copy-done.2), channel_id=1, source_target_pairs={{0,8},{4,12},{8,0},{12,4},{1,9},{5,13},{9,1},{13,5},{2,10},{6,14},... | collective-permute-start | bytes 393224 | tf_op jit(solution)/shard_map/ppermute | solution.py:291
  41.4 6.7 %collective-permute-start.2 = (bf16[1,256,256]{2,1,0:T(8,128)(2,1)S(1)}, bf16[1,256,256]{2,1,0:T(8,128)(2,1)S(1)}, u32[]{:S(2)}, u32[]{:S(2)}) collective-permute-start(bf16[1,256,256]{2,1,0:T(8,128)(2,1)S(1)} %copy-done.1), channel_id=1, source_target_pairs={{0,12},{4,8},{8,4},{12,0},{1,13},{5,9},{9,5},{13,1},{2,14},{6,10},... | collective-permute-start | bytes 393224 | tf_op jit(solution)/shard_map/ppermute | solution.py:291

commit v4 on v3

--- a/solution.py
+++ b/solution.py
@@ -14,6 +14,7 @@
 MIB = 1024 * 1024
 HEAD = 16
 UNROLL = 4
+LATE = 3
 CONV_VMEM = 64
 SUM_VMEM = 24
 
@@ -121,19 +122,17 @@
         facts = jnp.where(lanes == 8 * rank, local_id[0, slot].astype(F32), heads[box])
         facts = jnp.where(lanes == 8 * rank + 1, valid[0, slot].astype(F32), facts)
         heads[box] = jnp.where(lanes == 8 * rank + 2, weight, facts)
-        for group in range(len(plan["split"])):
-            at = mine if plan["single"] else 0
-
-            def store(group=group, at=at):
-                for phase in range(nb):
-                    ref, first = plan["place"](outs, group, phase)
-                    start = pl.multiple_of(first + rank * rows, rows)
-                    sent(slot, phase, ref.at[at, pl.ds(start, rows), :]).start()
-
-            if plan["single"]:
-                store()
-            else:
-                pl.when(box == group)(store)
+        def store(box):
+            for phase in range(nb):
+                ref, at, first = plan["place"](outs, box, phase)
+                start = pl.multiple_of(first + rank * rows, rows)
+                sent(slot, phase, ref.at[at, pl.ds(start, rows), :]).start()
+
+        if plan["single"]:
+            store(mine)
+        else:
+            for index in range(plan["sky"]):
+                pl.when(box == index)(functools.partial(store, index))
 
     def some(step, carry):
         slots_now = [step * UNROLL + u for u in range(UNROLL)]
@@ -147,15 +146,12 @@
     lax.fori_loop(0, slots // UNROLL, some, 0)
     width = patch.shape[2]
     copies = []
-    for group in range(len(plan["split"])):
-        ref, first = plan["head"](outs, group)
-        for at in range(ref.shape[0]):
-            index = at if plan["single"] else group
-            row = jnp.concatenate([heads[index]] * (width // 128), axis=1)
-            head_rows[index] = jnp.broadcast_to(row, (HEAD, width)).astype(BF16)
-            copies.append(pltpu.make_async_copy(
-                head_rows.at[index], ref.at[at, first : first + HEAD, :], sems.at[index]))
-            copies[-1].start()
+    for index in range(plan["sky"]):
+        ref, at, first = plan["head"](outs, index)
+        row = jnp.concatenate([heads[index]] * (width // 128), axis=1)
+        head_rows[index] = jnp.broadcast_to(row, (HEAD, width)).astype(BF16)
+        copies.append(pltpu.make_async_copy(head_rows.at[index], ref.at[at, first : first + HEAD, :], sems.at[index]))
+        copies[-1].start()
     for copy in copies:
         copy.wait()
     for slot in range(slots):
@@ -168,9 +164,9 @@
     first, last = phase == 0, phase == nb - 1
     refs = list(refs)
     take = lambda n: [refs.pop(0) for _ in range(n)]
-    boxes = take(len(plan["split"]))
+    boxes = take(plan["n_boxes"])
     arrived = take(len(plan["adds"][phase]))
-    heads = take(len(plan["split"])) if first else None
+    heads = take(plan["n_boxes"]) if first else None
     facts = None if first else take(2)
     if not first:
         take(1)
@@ -223,17 +219,21 @@
 
 
 def band_plan(nb):
-    if nb == 4:
-        masks = [3, 2, 1, 0]
-        chunk = lambda band, phase: band ^ masks[phase]
-        partner = lambda band, phase: band ^ (1, 2, 1)[phase]
-        adds = [[], [0], [], [1, 2]]
-    else:
-        shifts = sorted(range(1, nb), key=lambda k: -min(k, nb - k)) + [0]
-        chunk = lambda band, phase: (band + shifts[phase]) % nb if isinstance(band, int) else lax.rem(band + shifts[phase], nb)
-        partner = chunk
-        adds = [[]] * (nb - 1) + [list(range(nb - 1))]
-    return chunk, partner, adds
+    if nb & (nb - 1) == 0:
+        masks = sorted(range(1, nb), key=lambda m: (-m.bit_length(), m)) + [0]
+        return lambda band, phase: band ^ masks[phase]
+    shifts = sorted(range(1, nb), key=lambda k: -min(k, nb - k)) + [0]
+    return lambda band, phase: (
+        (band + shifts[phase]) % nb if isinstance(band, int) else lax.rem(band + shifts[phase], nb)
+    )
+
+
+def accumulate_kernel(*refs):
+    total, *terms, out = refs
+    value = total[...]
+    for term in terms:
+        value = value + term[...].astype(F32)
+    out[...] = value
 
 
 def per_device(patches, valid_rows, slot_owner, slot_local, slot_visit, basis_coef, inv_var, kernel_x, kernel_y):
@@ -242,28 +242,32 @@
     sky, nb = lax.axis_size("sky"), lax.axis_size("band")
     cap = max(2, 2 * slots // sky)
     rows = side // nb
-    single = sky > 4 or sky & (sky - 1) != 0
+    single = sky != 4
     tables = wave_tables(side, kernel_x.shape[1])
     sub, lane = tables["sub"], tables["lane"]
-    chunk, partner, adds = band_plan(nb)
-    near = 0 if single else min(2, sky)
-    split = [True] if single else [r >= near for r in range(sky)]
-    n_dest = sky if single else 1
+    chunk = band_plan(nb)
+    late = min(LATE, nb - 1)
+    adds = [[]] * (nb - 1) + [list(range(nb - 1 - late))]
     box = cap * rows
-    out_shapes, first_out = [], []
-    for cut in split:
-        first_out.append(len(out_shapes))
-        heights = [box + (HEAD if phase == 0 else 0) for phase in range(nb)] if cut else [nb * box + HEAD]
-        out_shapes += [jax.ShapeDtypeStruct((n_dest, h, width), BF16) for h in heights]
-
-    def place(outs, group, phase):
-        return (outs[first_out[group] + phase], 0) if split[group] else (outs[first_out[group]], phase * box)
-
-    def head(outs, group):
-        return outs[first_out[group]], box if split[group] else nb * box
+    shaped = lambda count, height: jax.ShapeDtypeStruct((count, height, width), BF16)
+    if single:
+        out_shapes = [shaped(sky, box + (HEAD if phase == 0 else 0)) for phase in range(nb)]
+        place = lambda outs, dest, phase: (outs[phase], dest, 0)
+        head = lambda outs, dest: (outs[0], dest, box)
+    else:
+        cut = lambda phase: shaped(1, box + (HEAD if phase == 0 else 0))
+        out_shapes = [shaped(1, nb * box + HEAD)] + [cut(phase) for phase in range(nb) for _ in range(3)]
+
+        def place(outs, dest, phase):
+            if dest == 1:
+                return outs[0], 0, phase * box
+            return outs[1 + 3 * phase + max(0, dest - 1)], 0, 0
+
+        def head(outs, dest):
+            return place(outs, dest, 0)[0], 0, nb * box if dest == 1 else box
 
     plan = dict(sub=sub, lane=lane, rows=rows, nb=nb, scale=tables["scale"], slots=slots, cap=cap, sky=sky, per=PATCH_DEV,
-                single=single, split=split, place=place, head=head, chunk=chunk, adds=adds)
+                single=single, n_boxes=1 if single else sky, place=place, head=head, chunk=chunk, adds=adds)
     smem = pl.BlockSpec(memory_space=pltpu.SMEM)
     hbm = pl.BlockSpec(memory_space=pltpu.HBM)
     consts = [jnp.asarray(tables[n]) for n in ("to_col", "to_row", "from_col", "from_row", "tap_col", "tap_row")]
@@ -289,15 +293,16 @@
     )(*args)
 
     swap = lambda a, r: a if r == 0 else lax.ppermute(a, "sky", [(i, i ^ r) for i in range(sky)])
-    moved = list(sent)
     if single:
         moved = [lax.all_to_all(s, "sky", split_axis=0, concat_axis=0, tiled=True) for s in sent]
+        pieces = lambda phase: [(moved[phase], sky, 0, 0, box)]
     else:
-        for r in range(1, near):
-            moved[first_out[r]] = swap(sent[first_out[r]], r)
-        for phase in range(nb):
-            for r in range(near, sky):
-                moved[first_out[r] + phase] = swap(sent[first_out[r] + phase], r)
+        near = swap(sent[0], 1)
+        cuts = [swap(a, (0, 2, 3)[i % 3]) for i, a in enumerate(sent[1:])]
+
+        def pieces(phase):
+            mine, *others = cuts[3 * phase : 3 * phase + 3]
+            return [(mine, 1, 0, 0, box), (near, 1, 0, phase, nb * box)] + [(a, 1, 0, 0, box) for a in others]
 
     band_buf, facts, arrived = None, None, []
     band_shape = jax.ShapeDtypeStruct((PATCH_DEV, side, width), F32)
@@ -307,19 +312,18 @@
     for phase in range(nb):
         first, last = phase == 0, phase == nb - 1
         inputs, specs = [], []
-        for group, cut in enumerate(split):
-            inputs.append(place(moved, group, phase)[0])
-            specs.append(pl.BlockSpec((n_dest, box, width), lambda i, at=0 if cut else phase: (0, at, 0)))
+        for array, count, at, row, _ in pieces(phase):
+            inputs.append(array)
+            specs.append(pl.BlockSpec((count, box, width), lambda i, at=at, row=row: (at, row, 0)))
         for earlier in adds[phase]:
             inputs.append(arrived[earlier])
             specs.append(whole(chunk_shape))
         outs = [band_shape, jax.ShapeDtypeStruct(chunk_shape, F32 if last else BF16)]
         out_specs, aliases, scratch = [hbm, whole(chunk_shape)], {}, []
         if first:
-            for group in range(len(split)):
-                ref, start = head(moved, group)
-                inputs.append(ref)
-                specs.append(pl.BlockSpec((n_dest, HEAD, width), lambda i, at=start // HEAD: (0, at, 0)))
+            for array, count, at, _, end in pieces(phase):
+                inputs.append(array)
+                specs.append(pl.BlockSpec((count, HEAD, width), lambda i, at=at, end=end: (at, end // HEAD, 0)))
             outs, out_specs = outs + fact_shapes, out_specs + [smem] * 2
             scratch = [pltpu.VMEM(s.shape, s.dtype) for s in fact_shapes]
         else:
@@ -342,7 +346,16 @@
         )(*inputs)
         facts = rest if first else facts
         if not last:
-            arrived.append(lax.ppermute(extra, "band", [(b, partner(b, phase)) for b in range(nb)]))
+            arrived.append(lax.ppermute(extra, "band", [(b, chunk(b, phase)) for b in range(nb)]))
+    if late:
+        terms = arrived[nb - 1 - late :]
+        for i in range(late - 1):
+            extra, terms[i] = lax.optimization_barrier((extra, terms[i]))
+        extra = pl.pallas_call(
+            accumulate_kernel, grid=(1,), out_shape=jax.ShapeDtypeStruct(chunk_shape, F32),
+            in_specs=[whole(chunk_shape)] * (1 + late), out_specs=whole(chunk_shape), input_output_aliases={0: 0},
+            compiler_params=pltpu.CompilerParams(vmem_limit_bytes=SUM_VMEM * MIB), name="accumulate",
+        )(extra, *terms)
     return (band_buf[None], extra)
 
 

time: 56.7 us -> 52.9 us (0.933)
  waiting for transfers between devices: 24.3 us -> 15.8 us
  starting transfers between devices: 13.3 us -> 15.5 us
  Pallas kernels: 17.2 us -> 18.9 us
  local copies, waits for them, and re-layouts: 1.07 us -> 1.83 us
    ppermute x9, waiting for transfers between devices: 18.3 us -> 9.79 us  [per_device(): lax.ppermute(a, 'sky', [(i, i ^ r) for i in range(sky)])]
    pallas_call x0 -> x1, Pallas kernels: none -> 1.94 us  [per_device(): pl.pallas_call(accumulate_kernel, grid=(1,), out_shape=jax.ShapeDtypeStru...]
    ppermute x9, starting transfers between devices: 8.47 us -> 10.3 us  [per_device(): lax.ppermute(a, 'sky', [(i, i ^ r) for i in range(sky)])]
    unnamed x14 -> x12, local copies, waits for them, and re-layouts: 1.07 us -> 1.83 us
  transfers between devices with their start and end apart: 12 -> 12, of which waited for: 9 -> 6; matrix products, arithmetic and copies ran while one was open for 0% -> 0% of each run, Pallas kernels for 6% -> 15%
where the time goes in v4:
time: 52.9 us; the launch traced here: 52.7 us
  Pallas kernels  18.9 us (36%)
  waiting for transfers between devices  15.8 us (30%)
  starting transfers between devices  15.5 us (29%)
  local copies, waits for them, and re-layouts  1.83 us (3%)
  between operations  0.72 us (1%)
    ppermute x9, starting transfers between devices, per_device(): lax.ppermute(a, 'sky', [(i, i ^ r) for i in range(sky)])  10.3 us
    ppermute x9, waiting for transfers between devices, per_device(): lax.ppermute(a, 'sky', [(i, i ^ r) for i in range(sky)])  9.79 us
    pallas_call x1, Pallas kernels, per_device(): pl.pallas_call(functools.partial(convolve_kernel, plan), out_shape=out_sh...  8.82 us
    pallas_call x4, Pallas kernels, per_device(): pl.pallas_call(functools.partial(sum_kernel, plan, phase), grid=(1,), out...  8.09 us
    ppermute x3, waiting for transfers between devices, per_device(): lax.ppermute(extra, 'band', [(b, chunk(b, phase)) for b in range(nb)])  5.96 us
    ppermute x3, starting transfers between devices, per_device(): lax.ppermute(extra, 'band', [(b, chunk(b, phase)) for b in range(nb)])  5.19 us
    pallas_call x1, Pallas kernels, per_device(): pl.pallas_call(accumulate_kernel, grid=(1,), out_shape=jax.ShapeDtypeStru...  1.94 us
    unnamed x12, local copies, waits for them, and re-layouts  1.83 us
  transfers between devices with their start and end apart: 12, of which 6 were waited for; matrix products, arithmetic and copies ran while one was open for 0% of the time, Pallas kernels for 15%

profile of v4, /device:TPU:0, one launch (start us, length us, event | category | flops | bytes accessed | tf_op | source)
XLA Modules:
  0.0 52.7 jit_solution(10129171574743496081)
XLA Ops:
  0.6 8.8 %convolve.1 = (bf16[1,1040,256]{2,1,0:T(8,128)(2,1)}, bf16[1,272,256]{2,1,0:T(8,128)(2,1)}, bf16[1,272,256]{2,1,0:T(8,128)(2,1)}, bf16[1,272,256]{2,1,0:T(8,128)...) custom-call(s32[1,8]{1,0:T(1,128)} %bitcast.7, ...), custom_call_target="tpu_custom_call" | custom-call | flops 2952790016 | bytes 3145728 | tf_op jit(solution)/shard_map/convolve/pallas_call | solution.py:278
  9.5 0.5 collective-permute-start
  10.0 2.6 %collective-permute-start.3 = (bf16[1,272,256]{2,1,0:T(8,128)(2,1)}, bf16[1,272,256]{2,1,0:T(8,128)(2,1)S(1)}, u32[]{:S(2)}, u32[]{:S(2)}) collective-permute-start(bf16[1,272,256]{2,1,0:T(8,128)(2,1)} %get-tuple-element.34), channel_id=1, source_target_pairs={{0,8},{4,12},{8,0},{12,4},{1,9},{5,13},{9,1},{13,5},{2,10},{6,14},... | collective-permute-start | bytes 417800 | tf_op jit(solution)/shard_map/ppermute | solution.py:295
  12.6 1.7 %collective-permute-start.7 = (bf16[1,256,256]{2,1,0:T(8,128)(2,1)}, bf16[1,256,256]{2,1,0:T(8,128)(2,1)S(1)}, u32[]{:S(2)}, u32[]{:S(2)}) collective-permute-start(bf16[1,256,256]{2,1,0:T(8,128)(2,1)} %get-tuple-element.42), channel_id=1, source_target_pairs={{0,8},{4,12},{8,0},{12,4},{1,9},{5,13},{9,1},{13,5},{2,10},{6,14},... | collective-permute-start | bytes 393224 | tf_op jit(solution)/shard_map/ppermute | solution.py:295
  14.4 2.9 %collective-permute-done.3.refs_2_.refs_6_ = bf16[1,272,256]{2,1,0:T(8,128)(2,1)S(1)} collective-permute-done((bf16[1,272,256]{2,1,0:T(8,128)(2,1)}, bf16[1,272,256]{2,1,0:T(8,128)(2,1)S(1)}, u32[]{:S(2)}, u32[]{:S(2)}) %collective-permute-start.3) | collective-permute-done | bytes 139296 | tf_op jit(solution)/shard_map/ppermute | solution.py:295
  17.3 1.9 %collective-permute-start.5 = (bf16[1,256,256]{2,1,0:T(8,128)(2,1)}, bf16[1,256,256]{2,1,0:T(8,128)(2,1)S(1)}, u32[]{:S(2)}, u32[]{:S(2)}) collective-permute-start(bf16[1,256,256]{2,1,0:T(8,128)(2,1)} %get-tuple-element.39), channel_id=1, source_target_pairs={{0,8},{4,12},{8,0},{12,4},{1,9},{5,13},{9,1},{13,5},{2,10},{6,14},... | collective-permute-start | bytes 393224 | tf_op jit(solution)/shard_map/ppermute | solution.py:295
  19.2 0.6 %collective-permute-done.4.refs_3_.refs_7_ = bf16[1,272,256]{2,1,0:T(8,128)(2,1)S(1)} collective-permute-done((bf16[1,272,256]{2,1,0:T(8,128)(2,1)}, bf16[1,272,256]{2,1,0:T(8,128)(2,1)S(1)}, u32[]{:S(2)}, u32[]{:S(2)}) %collective-permute-start.4) | collective-permute-done | bytes 139296 | tf_op jit(solution)/shard_map/ppermute | solution.py:295
  19.8 1.8 %collective-permute-start.6 = (bf16[1,256,256]{2,1,0:T(8,128)(2,1)}, bf16[1,256,256]{2,1,0:T(8,128)(2,1)S(1)}, u32[]{:S(2)}, u32[]{:S(2)}) collective-permute-start(bf16[1,256,256]{2,1,0:T(8,128)(2,1)} %get-tuple-element.40), channel_id=1, source_target_pairs={{0,12},{4,8},{8,4},{12,0},{1,13},{5,9},{9,5},{13,1},{2,14},{6,10},... | collective-permute-start | bytes 393224 | tf_op jit(solution)/shard_map/ppermute | solution.py:295
  21.6 0.9 %copy-done = bf16[1,272,256]{2,1,0:T(8,128)(2,1)S(1)} copy-done((bf16[1,272,256]{2,1,0:T(8,128)(2,1)S(1)}, bf16[1,272,256]{2,1,0:T(8,128)(2,1)}, u32[]{:S(2)}) %copy-start) | copy-done | bytes 139288
  22.5 2.3 %add_up.4 = (f32[8,256,256]{2,1,0:T(8,128)}, bf16[8,64,256]{2,1,0:T(8,128)(2,1)S(1)}, s32[4,128]{1,0:T(4,128)S(1)}, f32[4,128]{1,0:T(4,128)S(1)}) custom-call(bf16[1,272,256]{2,1,0:T(8,128)(2,1)S(1)} %copy-done, bf16[1,1040,256]{2,1,0:T(8,128)(2,1)S(1)} %collective-permute-done.refs_1_.refs_5_, ...), custom_call_target="tpu_custom_call" | custom-call | flops 524288 | bytes 1572864 | tf_op jit(solution)/shard_map/add_up/pallas_call | solution.py:333
  24.9 2.7 %collective-permute-start.9 = (bf16[8,64,256]{2,1,0:T(8,128)(2,1)S(1)}, bf16[8,64,256]{2,1,0:T(8,128)(2,1)S(1)}, u32[]{:S(2)}, u32[]{:S(2)}) collective-permute-start(bf16[8,64,256]{2,1,0:T(8,128)(2,1)S(1)} %get-tuple-element.49), channel_id=1, source_target_pairs={{0,2},{1,3},{2,0},{3,1},{4,6},{5,7},{6,4},{7,5},{8,10},{9,11},{10,... | collective-permute-start | bytes 786440 | tf_op jit(solution)/shard_map/ppermute | solution.py:349
  27.5 0.9 %copy-done.3 = bf16[1,256,256]{2,1,0:T(8,128)(2,1)S(1)} copy-done((bf16[1,256,256]{2,1,0:T(8,128)(2,1)S(1)}, bf16[1,256,256]{2,1,0:T(8,128)(2,1)}, u32[]{:S(2)}) %copy-start.3) | copy-done | bytes 131096
  28.4 1.7 %add_up.5 = (f32[8,256,256]{2,1,0:T(8,128)}, bf16[8,64,256]{2,1,0:T(8,128)(2,1)S(1)}) custom-call(bf16[1,256,256]{2,1,0:T(8,128)(2,1)S(1)} %copy-done.3, bf16[1,1040,256]{2,1,0:T(8,128)(2,1)S(1)} %collective-permute-done.refs_1_.refs_5_, bf16[1,256,256]{2,1,0:T(8,128)(2,1)S(1)} %collective-permute-done.7.refs_2_, ...), custom_call_target="tpu_custom_call", output_to_operand_aliasing={{0}: (6, {})} | custom-call | flops 524288 | bytes 1572864 | tf_op jit(solution)/shard_map/add_up/pallas_call | solution.py:333
  30.1 1.6 %collective-permute-start.10 = (bf16[8,64,256]{2,1,0:T(8,128)(2,1)S(1)}, bf16[8,64,256]{2,1,0:T(8,128)(2,1)S(1)}, u32[]{:S(2)}, u32[]{:S(2)}) collective-permute-start(bf16[8,64,256]{2,1,0:T(8,128)(2,1)S(1)} %get-tuple-element.51), channel_id=1, source_target_pairs={{0,3},{1,2},{2,1},{3,0},{4,7},{5,6},{6,5},{7,4},{8,11},{9,10},{10,... | collective-permute-start | bytes 786440 | tf_op jit(solution)/shard_map/ppermute | solution.py:349
  31.7 1.7 %add_up.6 = (f32[8,256,256]{2,1,0:T(8,128)}, bf16[8,64,256]{2,1,0:T(8,128)(2,1)S(1)}) custom-call(bf16[1,256,256]{2,1,0:T(8,128)(2,1)S(1)} %copy-done.2, bf16[1,1040,256]{2,1,0:T(8,128)(2,1)S(1)} %collective-permute-done.refs_1_.refs_5_, bf16[1,256,256]{2,1,0:T(8,128)(2,1)S(1)} %collective-permute-done.5.refs_2_, ...), custom_call_target="tpu_custom_call", output_to_operand_aliasing={{0}: (6, {})} | custom-call | flops 524288 | bytes 1572864 | tf_op jit(solution)/shard_map/add_up/pallas_call | solution.py:333
  33.4 1.0 %collective-permute-start.11 = (bf16[8,64,256]{2,1,0:T(8,128)(2,1)S(1)}, bf16[8,64,256]{2,1,0:T(8,128)(2,1)S(1)}, u32[]{:S(2)}, u32[]{:S(2)}) collective-permute-start(bf16[8,64,256]{2,1,0:T(8,128)(2,1)S(1)} %get-tuple-element.55), channel_id=1, source_target_pairs={{0,1},{1,0},{2,3},{3,2},{4,5},{5,4},{6,7},{7,6},{8,9},{9,8},{10,11... | collective-permute-start | bytes 786440 | tf_op jit(solution)/shard_map/ppermute | solution.py:349
  34.4 1.5 %collective-permute-start.1 = (bf16[1,256,256]{2,1,0:T(8,128)(2,1)S(1)}, bf16[1,256,256]{2,1,0:T(8,128)(2,1)S(1)}, u32[]{:S(2)}, u32[]{:S(2)}) collective-permute-start(bf16[1,256,256]{2,1,0:T(8,128)(2,1)S(1)} %copy-done.5), channel_id=1, source_target_pairs={{0,8},{4,12},{8,0},{12,4},{1,9},{5,13},{9,1},{13,5},{2,10},{6,14},... | collective-permute-start | bytes 393224 | tf_op jit(solution)/shard_map/ppermute | solution.py:295
  35.9 0.1 collective-permute-start.2
  36.0 4.7 %collective-permute-done.1.refs_2_ = bf16[1,256,256]{2,1,0:T(8,128)(2,1)S(1)} collective-permute-done((bf16[1,256,256]{2,1,0:T(8,128)(2,1)S(1)}, bf16[1,256,256]{2,1,0:T(8,128)(2,1)S(1)}, u32[]{:S(2)}, u32[]{:S(2)}) %collective-permute-start.1) | collective-permute-done | bytes 131104 | tf_op jit(solution)/shard_map/ppermute | solution.py:295
  40.7 1.6 %collective-permute-done.2.refs_3_ = bf16[1,256,256]{2,1,0:T(8,128)(2,1)S(1)} collective-permute-done((bf16[1,256,256]{2,1,0:T(8,128)(2,1)S(1)}, bf16[1,256,256]{2,1,0:T(8,128)(2,1)S(1)}, u32[]{:S(2)}, u32[]{:S(2)}) %collective-permute-start.2) | collective-permute-done | bytes 131104 | tf_op jit(solution)/shard_map/ppermute | solution.py:295
  42.3 2.5 %add_up.7 = (f32[8,256,256]{2,1,0:T(8,128)}, f32[8,64,256]{2,1,0:T(8,128)}) custom-call(bf16[1,256,256]{2,1,0:T(8,128)(2,1)S(1)} %copy-done.1, bf16[1,1040,256]{2,1,0:T(8,128)(2,1)S(1)} %collective-permute-done.refs_1_.refs_5_, bf16[1,256,256]{2,1,0:T(8,128)(2,1)S(1)} %collective-permute-done.1.refs_2_, ...), custom_call_target="tpu_custom_call", output_to_operand_aliasing={{0}: (6, {})} | custom-call | flops 524288 | bytes 1572864 | tf_op jit(solution)/shard_map/add_up/pallas_call | solution.py:333
  44.7 1.5 %collective-permute-done.9.refs_1_ = bf16[8,64,256]{2,1,0:T(8,128)(2,1)S(1)} collective-permute-done((bf16[8,64,256]{2,1,0:T(8,128)(2,1)S(1)}, bf16[8,64,256]{2,1,0:T(8,128)(2,1)S(1)}, u32[]{:S(2)}, u32[]{:S(2)}) %collective-permute-start.9) | collective-permute-done | bytes 262176 | tf_op jit(solution)/shard_map/ppermute | solution.py:349
  46.3 4.4 %collective-permute-done.11.refs_3_ = bf16[8,64,256]{2,1,0:T(8,128)(2,1)S(1)} collective-permute-done((bf16[8,64,256]{2,1,0:T(8,128)(2,1)S(1)}, bf16[8,64,256]{2,1,0:T(8,128)(2,1)S(1)}, u32[]{:S(2)}, u32[]{:S(2)}) %collective-permute-start.11) | collective-permute-done | bytes 262176 | tf_op jit(solution)/shard_map/ppermute | solution.py:349
  50.7 1.9 %accumulate.1 = f32[8,64,256]{2,1,0:T(8,128)} custom-call(f32[8,64,256]{2,1,0:T(8,128)} %get-tuple-element.52.refs_0_, bf16[8,64,256]{2,1,0:T(8,128)(2,1)S(1)} %collective-permute-done.9.refs_1_, bf16[8,64,256]{2,1,0:T(8,128)(2,1)S(1)} %collective-permute-done.10.refs_2_, ...), custom_call_target="tpu_custom_call", output_to_operand_aliasing={{}: (0, {})} | custom-call | tf_op jit(solution)/shard_map/accumulate/pallas_call | solution.py:354
  (18 shorter events, 0.1 us)
Async XLA Ops:
  9.5 12.2 %collective-permute-start = (bf16[1,1040,256]{2,1,0:T(8,128)(2,1)}, bf16[1,1040,256]{2,1,0:T(8,128)(2,1)S(1)}, u32[]{:S(2)}, u32[]{:S(2)}) collective-permute-start(bf16[1,1040,256]{2,1,0:T(8,128)(2,1)} %get-tuple-element.30), channel_id=1, source_target_pairs={{0,4},{4,0},{8,12},{12,8},{1,5},{5,1},{9,13},{13,9},{2,6},{6,2},{1... | collective-permute-start | bytes 1597448 | tf_op jit(solution)/shard_map/ppermute | solution.py:295
  10.0 7.3 %collective-permute-start.3 = (bf16[1,272,256]{2,1,0:T(8,128)(2,1)}, bf16[1,272,256]{2,1,0:T(8,128)(2,1)S(1)}, u32[]{:S(2)}, u32[]{:S(2)}) collective-permute-start(bf16[1,272,256]{2,1,0:T(8,128)(2,1)} %get-tuple-element.34), channel_id=1, source_target_pairs={{0,8},{4,12},{8,0},{12,4},{1,9},{5,13},{9,1},{13,5},{2,10},{6,14},... | collective-permute-start | bytes 417800 | tf_op jit(solution)/shard_map/ppermute | solution.py:295
  12.5 7.3 %collective-permute-start.4 = (bf16[1,272,256]{2,1,0:T(8,128)(2,1)}, bf16[1,272,256]{2,1,0:T(8,128)(2,1)S(1)}, u32[]{:S(2)}, u32[]{:S(2)}) collective-permute-start(bf16[1,272,256]{2,1,0:T(8,128)(2,1)} %get-tuple-element.35), channel_id=1, source_target_pairs={{0,12},{4,8},{8,4},{12,0},{1,13},{5,9},{9,5},{13,1},{2,14},{6,10},... | collective-permute-start | bytes 417800 | tf_op jit(solution)/shard_map/ppermute | solution.py:295
  12.6 14.9 %collective-permute-start.7 = (bf16[1,256,256]{2,1,0:T(8,128)(2,1)}, bf16[1,256,256]{2,1,0:T(8,128)(2,1)S(1)}, u32[]{:S(2)}, u32[]{:S(2)}) collective-permute-start(bf16[1,256,256]{2,1,0:T(8,128)(2,1)} %get-tuple-element.42), channel_id=1, source_target_pairs={{0,8},{4,12},{8,0},{12,4},{1,9},{5,13},{9,1},{13,5},{2,10},{6,14},... | collective-permute-start | bytes 393224 | tf_op jit(solution)/shard_map/ppermute | solution.py:295
  14.4 13.2 %collective-permute-start.8 = (bf16[1,256,256]{2,1,0:T(8,128)(2,1)}, bf16[1,256,256]{2,1,0:T(8,128)(2,1)S(1)}, u32[]{:S(2)}, u32[]{:S(2)}) collective-permute-start(bf16[1,256,256]{2,1,0:T(8,128)(2,1)} %get-tuple-element.43), channel_id=1, source_target_pairs={{0,12},{4,8},{8,4},{12,0},{1,13},{5,9},{9,5},{13,1},{2,14},{6,10},... | collective-permute-start | bytes 393224 | tf_op jit(solution)/shard_map/ppermute | solution.py:295
  17.3 14.4 %collective-permute-start.5 = (bf16[1,256,256]{2,1,0:T(8,128)(2,1)}, bf16[1,256,256]{2,1,0:T(8,128)(2,1)S(1)}, u32[]{:S(2)}, u32[]{:S(2)}) collective-permute-start(bf16[1,256,256]{2,1,0:T(8,128)(2,1)} %get-tuple-element.39), channel_id=1, source_target_pairs={{0,8},{4,12},{8,0},{12,4},{1,9},{5,13},{9,1},{13,5},{2,10},{6,14},... | collective-permute-start | bytes 393224 | tf_op jit(solution)/shard_map/ppermute | solution.py:295
  19.8 11.9 %collective-permute-start.6 = (bf16[1,256,256]{2,1,0:T(8,128)(2,1)}, bf16[1,256,256]{2,1,0:T(8,128)(2,1)S(1)}, u32[]{:S(2)}, u32[]{:S(2)}) collective-permute-start(bf16[1,256,256]{2,1,0:T(8,128)(2,1)} %get-tuple-element.40), channel_id=1, source_target_pairs={{0,12},{4,8},{8,4},{12,0},{1,13},{5,9},{9,5},{13,1},{2,14},{6,10},... | collective-permute-start | bytes 393224 | tf_op jit(solution)/shard_map/ppermute | solution.py:295
  21.6 0.9 %copy-start = (bf16[1,272,256]{2,1,0:T(8,128)(2,1)S(1)}, bf16[1,272,256]{2,1,0:T(8,128)(2,1)}, u32[]{:S(2)}) copy-start(bf16[1,272,256]{2,1,0:T(8,128)(2,1)} %get-tuple-element.33.refs_0_.refs_4_) | copy-start | bytes 417796
  22.5 9.2 %copy-start.2 = (bf16[1,256,256]{2,1,0:T(8,128)(2,1)S(1)}, bf16[1,256,256]{2,1,0:T(8,128)(2,1)}, u32[]{:S(2)}) copy-start(bf16[1,256,256]{2,1,0:T(8,128)(2,1)} %get-tuple-element.38.refs_0_) | copy-start | bytes 393220
  24.9 21.4 %collective-permute-start.9 = (bf16[8,64,256]{2,1,0:T(8,128)(2,1)S(1)}, bf16[8,64,256]{2,1,0:T(8,128)(2,1)S(1)}, u32[]{:S(2)}, u32[]{:S(2)}) collective-permute-start(bf16[8,64,256]{2,1,0:T(8,128)(2,1)S(1)} %get-tuple-element.49), channel_id=1, source_target_pairs={{0,2},{1,3},{2,0},{3,1},{4,6},{5,7},{6,4},{7,5},{8,10},{9,11},{10,... | collective-permute-start | bytes 786440 | tf_op jit(solution)/shard_map/ppermute | solution.py:349
  27.5 0.9 %copy-start.3 = (bf16[1,256,256]{2,1,0:T(8,128)(2,1)S(1)}, bf16[1,256,256]{2,1,0:T(8,128)(2,1)}, u32[]{:S(2)}) copy-start(bf16[1,256,256]{2,1,0:T(8,128)(2,1)} %get-tuple-element.41.refs_0_) | copy-start | bytes 393220
  30.1 4.3 %copy-start.5 = (bf16[1,256,256]{2,1,0:T(8,128)(2,1)S(1)}, bf16[1,256,256]{2,1,0:T(8,128)(2,1)}, u32[]{:S(2)}) copy-start(bf16[1,256,256]{2,1,0:T(8,128)(2,1)} %get-tuple-element.31) | copy-start | bytes 393220
  30.1 5.8 %copy-start.4 = (bf16[1,256,256]{2,1,0:T(8,128)(2,1)S(1)}, bf16[1,256,256]{2,1,0:T(8,128)(2,1)}, u32[]{:S(2)}) copy-start(bf16[1,256,256]{2,1,0:T(8,128)(2,1)} %get-tuple-element.32) | copy-start | bytes 393220
  30.1 12.2 %copy-start.1 = (bf16[1,256,256]{2,1,0:T(8,128)(2,1)S(1)}, bf16[1,256,256]{2,1,0:T(8,128)(2,1)}, u32[]{:S(2)}) copy-start(bf16[1,256,256]{2,1,0:T(8,128)(2,1)} %get-tuple-element.29.refs_0_) | copy-start | bytes 393220
  30.1 16.1 %collective-permute-start.10 = (bf16[8,64,256]{2,1,0:T(8,128)(2,1)S(1)}, bf16[8,64,256]{2,1,0:T(8,128)(2,1)S(1)}, u32[]{:S(2)}, u32[]{:S(2)}) collective-permute-start(bf16[8,64,256]{2,1,0:T(8,128)(2,1)S(1)} %get-tuple-element.51), channel_id=1, source_target_pairs={{0,3},{1,2},{2,1},{3,0},{4,7},{5,6},{6,5},{7,4},{8,11},{9,10},{10,... | collective-permute-start | bytes 786440 | tf_op jit(solution)/shard_map/ppermute | solution.py:349
  33.4 17.3 %collective-permute-start.11 = (bf16[8,64,256]{2,1,0:T(8,128)(2,1)S(1)}, bf16[8,64,256]{2,1,0:T(8,128)(2,1)S(1)}, u32[]{:S(2)}, u32[]{:S(2)}) collective-permute-start(bf16[8,64,256]{2,1,0:T(8,128)(2,1)S(1)} %get-tuple-element.55), channel_id=1, source_target_pairs={{0,1},{1,0},{2,3},{3,2},{4,5},{5,4},{6,7},{7,6},{8,9},{9,8},{10,11... | collective-permute-start | bytes 786440 | tf_op jit(solution)/shard_map/ppermute | solution.py:349
  34.4 6.3 %collective-permute-start.1 = (bf16[1,256,256]{2,1,0:T(8,128)(2,1)S(1)}, bf16[1,256,256]{2,1,0:T(8,128)(2,1)S(1)}, u32[]{:S(2)}, u32[]{:S(2)}) collective-permute-start(bf16[1,256,256]{2,1,0:T(8,128)(2,1)S(1)} %copy-done.5), channel_id=1, source_target_pairs={{0,8},{4,12},{8,0},{12,4},{1,9},{5,13},{9,1},{13,5},{2,10},{6,14},... | collective-permute-start | bytes 393224 | tf_op jit(solution)/shard_map/ppermute | solution.py:295
  35.9 6.4 %collective-permute-start.2 = (bf16[1,256,256]{2,1,0:T(8,128)(2,1)S(1)}, bf16[1,256,256]{2,1,0:T(8,128)(2,1)S(1)}, u32[]{:S(2)}, u32[]{:S(2)}) collective-permute-start(bf16[1,256,256]{2,1,0:T(8,128)(2,1)S(1)} %copy-done.4), channel_id=1, source_target_pairs={{0,12},{4,8},{8,4},{12,0},{1,13},{5,9},{9,5},{13,1},{2,14},{6,10},... | collective-permute-start | bytes 393224 | tf_op jit(solution)/shard_map/ppermute | solution.py:295

commit v5 on v4

--- a/solution.py
+++ b/solution.py
@@ -13,7 +13,7 @@
 F32, BF16 = jnp.float32, jnp.bfloat16
 MIB = 1024 * 1024
 HEAD = 16
-UNROLL = 4
+UNROLL = 8
 LATE = 3
 CONV_VMEM = 64
 SUM_VMEM = 24
@@ -135,7 +135,7 @@
                 pl.when(box == index)(functools.partial(store, index))
 
     def some(step, carry):
-        slots_now = [step * UNROLL + u for u in range(UNROLL)]
+        slots_now = [step * UNROLL + u for u in range(min(UNROLL, slots))]
         for s in slots_now:
             pltpu.make_async_copy(sources[-1].at[s], local[-1].at[s], sems.at[n_in - 1 + s]).wait()
         results = [convolved(s) for s in slots_now]
@@ -143,7 +143,7 @@
             deliver(s, full)
         return carry
 
-    lax.fori_loop(0, slots // UNROLL, some, 0)
+    lax.fori_loop(0, max(1, slots // UNROLL), some, 0)
     width = patch.shape[2]
     copies = []
     for index in range(plan["sky"]):
@@ -219,10 +219,7 @@
 
 
 def band_plan(nb):
-    if nb & (nb - 1) == 0:
-        masks = sorted(range(1, nb), key=lambda m: (-m.bit_length(), m)) + [0]
-        return lambda band, phase: band ^ masks[phase]
-    shifts = sorted(range(1, nb), key=lambda k: -min(k, nb - k)) + [0]
+    shifts = list(range(1, nb)) + [0]
     return lambda band, phase: (
         (band + shifts[phase]) % nb if isinstance(band, int) else lax.rem(band + shifts[phase], nb)
     )

time: 52.9 us -> 51.5 us (0.974)
  the two profiles are of different devices: /device:TPU:0 before, /device:TPU:13 now
where the time goes in v5:
time: 51.5 us; the launch traced here: 51.2 us
  Pallas kernels  18.8 us (37%)
  waiting for transfers between devices  16.9 us (33%)
  starting transfers between devices  13 us (25%)
  local copies, waits for them, and re-layouts  1.83 us (4%)
  between operations  0.72 us (1%)
    ppermute x9, waiting for transfers between devices, per_device(): lax.ppermute(a, 'sky', [(i, i ^ r) for i in range(sky)])  10.4 us
    ppermute x9, starting transfers between devices, per_device(): lax.ppermute(a, 'sky', [(i, i ^ r) for i in range(sky)])  9.01 us
    pallas_call x1, Pallas kernels, per_device(): pl.pallas_call(functools.partial(convolve_kernel, plan), out_shape=out_sh...  8.69 us
    pallas_call x4, Pallas kernels, per_device(): pl.pallas_call(functools.partial(sum_kernel, plan, phase), grid=(1,), out...  8.17 us
    ppermute x3, waiting for transfers between devices, per_device(): lax.ppermute(extra, 'band', [(b, chunk(b, phase)) for b in range(nb)])  6.49 us
    ppermute x3, starting transfers between devices, per_device(): lax.ppermute(extra, 'band', [(b, chunk(b, phase)) for b in range(nb)])  3.94 us
    pallas_call x1, Pallas kernels, per_device(): pl.pallas_call(accumulate_kernel, grid=(1,), out_shape=jax.ShapeDtypeStru...  1.94 us
    unnamed x12, local copies, waits for them, and re-layouts  1.83 us
  transfers between devices with their start and end apart: 12, of which 8 were waited for; matrix products, arithmetic and copies ran while one was open for 0% of the time, Pallas kernels for 16%

profile of v5, /device:TPU:13, one launch (start us, length us, event | category | flops | bytes accessed | tf_op | source)
XLA Modules:
  0.0 51.2 jit_solution(10402346118378822632)
XLA Ops:
  0.6 8.7 %convolve.1 = (bf16[1,1040,256]{2,1,0:T(8,128)(2,1)}, bf16[1,272,256]{2,1,0:T(8,128)(2,1)}, bf16[1,272,256]{2,1,0:T(8,128)(2,1)}, bf16[1,272,256]{2,1,0:T(8,128)...) custom-call(s32[1,8]{1,0:T(1,128)} %bitcast.7, ...), custom_call_target="tpu_custom_call" | custom-call | flops 2952790016 | bytes 3145728 | tf_op jit(solution)/shard_map/convolve/pallas_call | solution.py:275
  9.3 0.7 %collective-permute-start = (bf16[1,1040,256]{2,1,0:T(8,128)(2,1)}, bf16[1,1040,256]{2,1,0:T(8,128)(2,1)S(1)}, u32[]{:S(2)}, u32[]{:S(2)}) collective-permute-start(bf16[1,1040,256]{2,1,0:T(8,128)(2,1)} %get-tuple-element.30), channel_id=1, source_target_pairs={{0,4},{4,0},{8,12},{12,8},{1,5},{5,1},{9,13},{13,9},{2,6},{6,2},{1... | collective-permute-start | bytes 1597448 | tf_op jit(solution)/shard_map/ppermute | solution.py:292
  10.1 1.2 %collective-permute-start.3 = (bf16[1,272,256]{2,1,0:T(8,128)(2,1)}, bf16[1,272,256]{2,1,0:T(8,128)(2,1)S(1)}, u32[]{:S(2)}, u32[]{:S(2)}) collective-permute-start(bf16[1,272,256]{2,1,0:T(8,128)(2,1)} %get-tuple-element.34), channel_id=1, source_target_pairs={{0,8},{4,12},{8,0},{12,4},{1,9},{5,13},{9,1},{13,5},{2,10},{6,14},... | collective-permute-start | bytes 417800 | tf_op jit(solution)/shard_map/ppermute | solution.py:292
  11.8 1.2 %collective-permute-start.7 = (bf16[1,256,256]{2,1,0:T(8,128)(2,1)}, bf16[1,256,256]{2,1,0:T(8,128)(2,1)S(1)}, u32[]{:S(2)}, u32[]{:S(2)}) collective-permute-start(bf16[1,256,256]{2,1,0:T(8,128)(2,1)} %get-tuple-element.42), channel_id=1, source_target_pairs={{0,8},{4,12},{8,0},{12,4},{1,9},{5,13},{9,1},{13,5},{2,10},{6,14},... | collective-permute-start | bytes 393224 | tf_op jit(solution)/shard_map/ppermute | solution.py:292
  13.0 0.6 %collective-permute-start.8 = (bf16[1,256,256]{2,1,0:T(8,128)(2,1)}, bf16[1,256,256]{2,1,0:T(8,128)(2,1)S(1)}, u32[]{:S(2)}, u32[]{:S(2)}) collective-permute-start(bf16[1,256,256]{2,1,0:T(8,128)(2,1)} %get-tuple-element.43), channel_id=1, source_target_pairs={{0,12},{4,8},{8,4},{12,0},{1,13},{5,9},{9,5},{13,1},{2,14},{6,10},... | collective-permute-start | bytes 393224 | tf_op jit(solution)/shard_map/ppermute | solution.py:292
  13.6 2.0 %collective-permute-done.3.refs_2_.refs_6_ = bf16[1,272,256]{2,1,0:T(8,128)(2,1)S(1)} collective-permute-done((bf16[1,272,256]{2,1,0:T(8,128)(2,1)}, bf16[1,272,256]{2,1,0:T(8,128)(2,1)S(1)}, u32[]{:S(2)}, u32[]{:S(2)}) %collective-permute-start.3) | collective-permute-done | bytes 139296 | tf_op jit(solution)/shard_map/ppermute | solution.py:292
  15.5 1.2 %collective-permute-start.5 = (bf16[1,256,256]{2,1,0:T(8,128)(2,1)}, bf16[1,256,256]{2,1,0:T(8,128)(2,1)S(1)}, u32[]{:S(2)}, u32[]{:S(2)}) collective-permute-start(bf16[1,256,256]{2,1,0:T(8,128)(2,1)} %get-tuple-element.39), channel_id=1, source_target_pairs={{0,8},{4,12},{8,0},{12,4},{1,9},{5,13},{9,1},{13,5},{2,10},{6,14},... | collective-permute-start | bytes 393224 | tf_op jit(solution)/shard_map/ppermute | solution.py:292
  16.7 2.4 %collective-permute-done.4.refs_3_.refs_7_ = bf16[1,272,256]{2,1,0:T(8,128)(2,1)S(1)} collective-permute-done((bf16[1,272,256]{2,1,0:T(8,128)(2,1)}, bf16[1,272,256]{2,1,0:T(8,128)(2,1)S(1)}, u32[]{:S(2)}, u32[]{:S(2)}) %collective-permute-start.4) | collective-permute-done | bytes 139296 | tf_op jit(solution)/shard_map/ppermute | solution.py:292
  19.1 0.9 %collective-permute-start.6 = (bf16[1,256,256]{2,1,0:T(8,128)(2,1)}, bf16[1,256,256]{2,1,0:T(8,128)(2,1)S(1)}, u32[]{:S(2)}, u32[]{:S(2)}) collective-permute-start(bf16[1,256,256]{2,1,0:T(8,128)(2,1)} %get-tuple-element.40), channel_id=1, source_target_pairs={{0,12},{4,8},{8,4},{12,0},{1,13},{5,9},{9,5},{13,1},{2,14},{6,10},... | collective-permute-start | bytes 393224 | tf_op jit(solution)/shard_map/ppermute | solution.py:292
  20.0 0.9 %copy-done = bf16[1,272,256]{2,1,0:T(8,128)(2,1)S(1)} copy-done((bf16[1,272,256]{2,1,0:T(8,128)(2,1)S(1)}, bf16[1,272,256]{2,1,0:T(8,128)(2,1)}, u32[]{:S(2)}) %copy-start) | copy-done | bytes 139288
  20.9 2.3 %add_up.4 = (f32[8,256,256]{2,1,0:T(8,128)}, bf16[8,64,256]{2,1,0:T(8,128)(2,1)S(1)}, s32[4,128]{1,0:T(4,128)S(1)}, f32[4,128]{1,0:T(4,128)S(1)}) custom-call(bf16[1,272,256]{2,1,0:T(8,128)(2,1)S(1)} %copy-done, bf16[1,1040,256]{2,1,0:T(8,128)(2,1)S(1)} %collective-permute-done.refs_1_.refs_5_, ...), custom_call_target="tpu_custom_call" | custom-call | flops 524288 | bytes 1572864 | tf_op jit(solution)/shard_map/add_up/pallas_call | solution.py:330
  23.2 1.4 %collective-permute-start.9 = (bf16[8,64,256]{2,1,0:T(8,128)(2,1)S(1)}, bf16[8,64,256]{2,1,0:T(8,128)(2,1)S(1)}, u32[]{:S(2)}, u32[]{:S(2)}) collective-permute-start(bf16[8,64,256]{2,1,0:T(8,128)(2,1)S(1)} %get-tuple-element.49), channel_id=1, source_target_pairs={{0,1},{1,2},{2,3},{3,0},{4,5},{5,6},{6,7},{7,4},{8,9},{9,10},{10,1... | collective-permute-start | bytes 786440 | tf_op jit(solution)/shard_map/ppermute | solution.py:346
  24.7 0.9 %copy-done.3 = bf16[1,256,256]{2,1,0:T(8,128)(2,1)S(1)} copy-done((bf16[1,256,256]{2,1,0:T(8,128)(2,1)S(1)}, bf16[1,256,256]{2,1,0:T(8,128)(2,1)}, u32[]{:S(2)}) %copy-start.3) | copy-done | bytes 131096
  25.7 1.7 %add_up.5 = (f32[8,256,256]{2,1,0:T(8,128)}, bf16[8,64,256]{2,1,0:T(8,128)(2,1)S(1)}) custom-call(bf16[1,256,256]{2,1,0:T(8,128)(2,1)S(1)} %copy-done.3, bf16[1,1040,256]{2,1,0:T(8,128)(2,1)S(1)} %collective-permute-done.refs_1_.refs_5_, bf16[1,256,256]{2,1,0:T(8,128)(2,1)S(1)} %collective-permute-done.7.refs_2_, ...), custom_call_target="tpu_custom_call", output_to_operand_aliasing={{0}: (6, {})} | custom-call | flops 524288 | bytes 1572864 | tf_op jit(solution)/shard_map/add_up/pallas_call | solution.py:330
  27.4 2.4 %collective-permute-start.10 = (bf16[8,64,256]{2,1,0:T(8,128)(2,1)S(1)}, bf16[8,64,256]{2,1,0:T(8,128)(2,1)S(1)}, u32[]{:S(2)}, u32[]{:S(2)}) collective-permute-start(bf16[8,64,256]{2,1,0:T(8,128)(2,1)S(1)} %get-tuple-element.51), channel_id=1, source_target_pairs={{0,2},{1,3},{2,0},{3,1},{4,6},{5,7},{6,4},{7,5},{8,10},{9,11},{10,... | collective-permute-start | bytes 786440 | tf_op jit(solution)/shard_map/ppermute | solution.py:346
  30.2 1.7 %add_up.6 = (f32[8,256,256]{2,1,0:T(8,128)}, bf16[8,64,256]{2,1,0:T(8,128)(2,1)S(1)}) custom-call(bf16[1,256,256]{2,1,0:T(8,128)(2,1)S(1)} %copy-done.2, bf16[1,1040,256]{2,1,0:T(8,128)(2,1)S(1)} %collective-permute-done.refs_1_.refs_5_, bf16[1,256,256]{2,1,0:T(8,128)(2,1)S(1)} %collective-permute-done.5.refs_2_, ...), custom_call_target="tpu_custom_call", output_to_operand_aliasing={{0}: (6, {})} | custom-call | flops 524288 | bytes 1572864 | tf_op jit(solution)/shard_map/add_up/pallas_call | solution.py:330
  32.1 1.2 %collective-permute-start.1 = (bf16[1,256,256]{2,1,0:T(8,128)(2,1)S(1)}, bf16[1,256,256]{2,1,0:T(8,128)(2,1)S(1)}, u32[]{:S(2)}, u32[]{:S(2)}) collective-permute-start(bf16[1,256,256]{2,1,0:T(8,128)(2,1)S(1)} %copy-done.5), channel_id=1, source_target_pairs={{0,8},{4,12},{8,0},{12,4},{1,9},{5,13},{9,1},{13,5},{2,10},{6,14},... | collective-permute-start | bytes 393224 | tf_op jit(solution)/shard_map/ppermute | solution.py:292
  33.3 1.5 %collective-permute-start.2 = (bf16[1,256,256]{2,1,0:T(8,128)(2,1)S(1)}, bf16[1,256,256]{2,1,0:T(8,128)(2,1)S(1)}, u32[]{:S(2)}, u32[]{:S(2)}) collective-permute-start(bf16[1,256,256]{2,1,0:T(8,128)(2,1)S(1)} %copy-done.4), channel_id=1, source_target_pairs={{0,12},{4,8},{8,4},{12,0},{1,13},{5,9},{9,5},{13,1},{2,14},{6,10},... | collective-permute-start | bytes 393224 | tf_op jit(solution)/shard_map/ppermute | solution.py:292
  34.9 1.4 %collective-permute-done.1.refs_2_ = bf16[1,256,256]{2,1,0:T(8,128)(2,1)S(1)} collective-permute-done((bf16[1,256,256]{2,1,0:T(8,128)(2,1)S(1)}, bf16[1,256,256]{2,1,0:T(8,128)(2,1)S(1)}, u32[]{:S(2)}, u32[]{:S(2)}) %collective-permute-start.1) | collective-permute-done | bytes 131104 | tf_op jit(solution)/shard_map/ppermute | solution.py:292
  36.2 4.1 %collective-permute-done.2.refs_3_ = bf16[1,256,256]{2,1,0:T(8,128)(2,1)S(1)} collective-permute-done((bf16[1,256,256]{2,1,0:T(8,128)(2,1)S(1)}, bf16[1,256,256]{2,1,0:T(8,128)(2,1)S(1)}, u32[]{:S(2)}, u32[]{:S(2)}) %collective-permute-start.2) | collective-permute-done | bytes 131104 | tf_op jit(solution)/shard_map/ppermute | solution.py:292
  40.3 2.5 %add_up.7 = (f32[8,256,256]{2,1,0:T(8,128)}, f32[8,64,256]{2,1,0:T(8,128)}) custom-call(bf16[1,256,256]{2,1,0:T(8,128)(2,1)S(1)} %copy-done.1, bf16[1,1040,256]{2,1,0:T(8,128)(2,1)S(1)} %collective-permute-done.refs_1_.refs_5_, bf16[1,256,256]{2,1,0:T(8,128)(2,1)S(1)} %collective-permute-done.1.refs_2_, ...), custom_call_target="tpu_custom_call", output_to_operand_aliasing={{0}: (6, {})} | custom-call | flops 524288 | bytes 1572864 | tf_op jit(solution)/shard_map/add_up/pallas_call | solution.py:330
  42.8 4.3 %collective-permute-done.10.refs_2_ = bf16[8,64,256]{2,1,0:T(8,128)(2,1)S(1)} collective-permute-done((bf16[8,64,256]{2,1,0:T(8,128)(2,1)S(1)}, bf16[8,64,256]{2,1,0:T(8,128)(2,1)S(1)}, u32[]{:S(2)}, u32[]{:S(2)}) %collective-permute-start.10) | collective-permute-done | bytes 262176 | tf_op jit(solution)/shard_map/ppermute | solution.py:346
  47.1 2.2 %collective-permute-done.11.refs_3_ = bf16[8,64,256]{2,1,0:T(8,128)(2,1)S(1)} collective-permute-done((bf16[8,64,256]{2,1,0:T(8,128)(2,1)S(1)}, bf16[8,64,256]{2,1,0:T(8,128)(2,1)S(1)}, u32[]{:S(2)}, u32[]{:S(2)}) %collective-permute-start.11) | collective-permute-done | bytes 262176 | tf_op jit(solution)/shard_map/ppermute | solution.py:346
  49.3 1.9 %accumulate.1 = f32[8,64,256]{2,1,0:T(8,128)} custom-call(f32[8,64,256]{2,1,0:T(8,128)} %get-tuple-element.52.refs_0_, bf16[8,64,256]{2,1,0:T(8,128)(2,1)S(1)} %collective-permute-done.9.refs_1_, bf16[8,64,256]{2,1,0:T(8,128)(2,1)S(1)} %collective-permute-done.10.refs_2_, ...), custom_call_target="tpu_custom_call", output_to_operand_aliasing={{}: (0, {})} | custom-call | tf_op jit(solution)/shard_map/accumulate/pallas_call | solution.py:351
  (18 shorter events, 1.4 us)
Async XLA Ops:
  9.3 10.7 %collective-permute-start = (bf16[1,1040,256]{2,1,0:T(8,128)(2,1)}, bf16[1,1040,256]{2,1,0:T(8,128)(2,1)S(1)}, u32[]{:S(2)}, u32[]{:S(2)}) collective-permute-start(bf16[1,1040,256]{2,1,0:T(8,128)(2,1)} %get-tuple-element.30), channel_id=1, source_target_pairs={{0,4},{4,0},{8,12},{12,8},{1,5},{5,1},{9,13},{13,9},{2,6},{6,2},{1... | collective-permute-start | bytes 1597448 | tf_op jit(solution)/shard_map/ppermute | solution.py:292
  10.1 5.5 %collective-permute-start.3 = (bf16[1,272,256]{2,1,0:T(8,128)(2,1)}, bf16[1,272,256]{2,1,0:T(8,128)(2,1)S(1)}, u32[]{:S(2)}, u32[]{:S(2)}) collective-permute-start(bf16[1,272,256]{2,1,0:T(8,128)(2,1)} %get-tuple-element.34), channel_id=1, source_target_pairs={{0,8},{4,12},{8,0},{12,4},{1,9},{5,13},{9,1},{13,5},{2,10},{6,14},... | collective-permute-start | bytes 417800 | tf_op jit(solution)/shard_map/ppermute | solution.py:292
  11.3 7.9 %collective-permute-start.4 = (bf16[1,272,256]{2,1,0:T(8,128)(2,1)}, bf16[1,272,256]{2,1,0:T(8,128)(2,1)S(1)}, u32[]{:S(2)}, u32[]{:S(2)}) collective-permute-start(bf16[1,272,256]{2,1,0:T(8,128)(2,1)} %get-tuple-element.35), channel_id=1, source_target_pairs={{0,12},{4,8},{8,4},{12,0},{1,13},{5,9},{9,5},{13,1},{2,14},{6,10},... | collective-permute-start | bytes 417800 | tf_op jit(solution)/shard_map/ppermute | solution.py:292
  11.8 12.8 %collective-permute-start.7 = (bf16[1,256,256]{2,1,0:T(8,128)(2,1)}, bf16[1,256,256]{2,1,0:T(8,128)(2,1)S(1)}, u32[]{:S(2)}, u32[]{:S(2)}) collective-permute-start(bf16[1,256,256]{2,1,0:T(8,128)(2,1)} %get-tuple-element.42), channel_id=1, source_target_pairs={{0,8},{4,12},{8,0},{12,4},{1,9},{5,13},{9,1},{13,5},{2,10},{6,14},... | collective-permute-start | bytes 393224 | tf_op jit(solution)/shard_map/ppermute | solution.py:292
  13.0 11.8 %collective-permute-start.8 = (bf16[1,256,256]{2,1,0:T(8,128)(2,1)}, bf16[1,256,256]{2,1,0:T(8,128)(2,1)S(1)}, u32[]{:S(2)}, u32[]{:S(2)}) collective-permute-start(bf16[1,256,256]{2,1,0:T(8,128)(2,1)} %get-tuple-element.43), channel_id=1, source_target_pairs={{0,12},{4,8},{8,4},{12,0},{1,13},{5,9},{9,5},{13,1},{2,14},{6,10},... | collective-permute-start | bytes 393224 | tf_op jit(solution)/shard_map/ppermute | solution.py:292
  15.5 14.2 %collective-permute-start.5 = (bf16[1,256,256]{2,1,0:T(8,128)(2,1)}, bf16[1,256,256]{2,1,0:T(8,128)(2,1)S(1)}, u32[]{:S(2)}, u32[]{:S(2)}) collective-permute-start(bf16[1,256,256]{2,1,0:T(8,128)(2,1)} %get-tuple-element.39), channel_id=1, source_target_pairs={{0,8},{4,12},{8,0},{12,4},{1,9},{5,13},{9,1},{13,5},{2,10},{6,14},... | collective-permute-start | bytes 393224 | tf_op jit(solution)/shard_map/ppermute | solution.py:292
  19.1 11.1 %collective-permute-start.6 = (bf16[1,256,256]{2,1,0:T(8,128)(2,1)}, bf16[1,256,256]{2,1,0:T(8,128)(2,1)S(1)}, u32[]{:S(2)}, u32[]{:S(2)}) collective-permute-start(bf16[1,256,256]{2,1,0:T(8,128)(2,1)} %get-tuple-element.40), channel_id=1, source_target_pairs={{0,12},{4,8},{8,4},{12,0},{1,13},{5,9},{9,5},{13,1},{2,14},{6,10},... | collective-permute-start | bytes 393224 | tf_op jit(solution)/shard_map/ppermute | solution.py:292
  20.0 0.9 %copy-start = (bf16[1,272,256]{2,1,0:T(8,128)(2,1)S(1)}, bf16[1,272,256]{2,1,0:T(8,128)(2,1)}, u32[]{:S(2)}) copy-start(bf16[1,272,256]{2,1,0:T(8,128)(2,1)} %get-tuple-element.33.refs_0_.refs_4_) | copy-start | bytes 417796
  20.9 9.3 %copy-start.2 = (bf16[1,256,256]{2,1,0:T(8,128)(2,1)S(1)}, bf16[1,256,256]{2,1,0:T(8,128)(2,1)}, u32[]{:S(2)}) copy-start(bf16[1,256,256]{2,1,0:T(8,128)(2,1)} %get-tuple-element.38.refs_0_) | copy-start | bytes 393220
  23.2 19.6 %collective-permute-start.9 = (bf16[8,64,256]{2,1,0:T(8,128)(2,1)S(1)}, bf16[8,64,256]{2,1,0:T(8,128)(2,1)S(1)}, u32[]{:S(2)}, u32[]{:S(2)}) collective-permute-start(bf16[8,64,256]{2,1,0:T(8,128)(2,1)S(1)} %get-tuple-element.49), channel_id=1, source_target_pairs={{0,1},{1,2},{2,3},{3,0},{4,5},{5,6},{6,7},{7,4},{8,9},{9,10},{10,1... | collective-permute-start | bytes 786440 | tf_op jit(solution)/shard_map/ppermute | solution.py:346
  24.7 0.9 %copy-start.3 = (bf16[1,256,256]{2,1,0:T(8,128)(2,1)S(1)}, bf16[1,256,256]{2,1,0:T(8,128)(2,1)}, u32[]{:S(2)}) copy-start(bf16[1,256,256]{2,1,0:T(8,128)(2,1)} %get-tuple-element.41.refs_0_) | copy-start | bytes 393220
  27.3 4.8 %copy-start.5 = (bf16[1,256,256]{2,1,0:T(8,128)(2,1)S(1)}, bf16[1,256,256]{2,1,0:T(8,128)(2,1)}, u32[]{:S(2)}) copy-start(bf16[1,256,256]{2,1,0:T(8,128)(2,1)} %get-tuple-element.31) | copy-start | bytes 393220
  27.3 6.0 %copy-start.4 = (bf16[1,256,256]{2,1,0:T(8,128)(2,1)S(1)}, bf16[1,256,256]{2,1,0:T(8,128)(2,1)}, u32[]{:S(2)}) copy-start(bf16[1,256,256]{2,1,0:T(8,128)(2,1)} %get-tuple-element.32) | copy-start | bytes 393220
  27.4 13.0 %copy-start.1 = (bf16[1,256,256]{2,1,0:T(8,128)(2,1)S(1)}, bf16[1,256,256]{2,1,0:T(8,128)(2,1)}, u32[]{:S(2)}) copy-start(bf16[1,256,256]{2,1,0:T(8,128)(2,1)} %get-tuple-element.29.refs_0_) | copy-start | bytes 393220
  27.4 19.8 %collective-permute-start.10 = (bf16[8,64,256]{2,1,0:T(8,128)(2,1)S(1)}, bf16[8,64,256]{2,1,0:T(8,128)(2,1)S(1)}, u32[]{:S(2)}, u32[]{:S(2)}) collective-permute-start(bf16[8,64,256]{2,1,0:T(8,128)(2,1)S(1)} %get-tuple-element.51), channel_id=1, source_target_pairs={{0,2},{1,3},{2,0},{3,1},{4,6},{5,7},{6,4},{7,5},{8,10},{9,11},{10,... | collective-permute-start | bytes 786440 | tf_op jit(solution)/shard_map/ppermute | solution.py:346
  31.9 17.4 %collective-permute-start.11 = (bf16[8,64,256]{2,1,0:T(8,128)(2,1)S(1)}, bf16[8,64,256]{2,1,0:T(8,128)(2,1)S(1)}, u32[]{:S(2)}, u32[]{:S(2)}) collective-permute-start(bf16[8,64,256]{2,1,0:T(8,128)(2,1)S(1)} %get-tuple-element.55), channel_id=1, source_target_pairs={{0,3},{1,0},{2,1},{3,2},{4,7},{5,4},{6,5},{7,6},{8,11},{9,8},{10,9... | collective-permute-start | bytes 786440 | tf_op jit(solution)/shard_map/ppermute | solution.py:346
  32.1 4.1 %collective-permute-start.1 = (bf16[1,256,256]{2,1,0:T(8,128)(2,1)S(1)}, bf16[1,256,256]{2,1,0:T(8,128)(2,1)S(1)}, u32[]{:S(2)}, u32[]{:S(2)}) collective-permute-start(bf16[1,256,256]{2,1,0:T(8,128)(2,1)S(1)} %copy-done.5), channel_id=1, source_target_pairs={{0,8},{4,12},{8,0},{12,4},{1,9},{5,13},{9,1},{13,5},{2,10},{6,14},... | collective-permute-start | bytes 393224 | tf_op jit(solution)/shard_map/ppermute | solution.py:292
  33.3 7.0 %collective-permute-start.2 = (bf16[1,256,256]{2,1,0:T(8,128)(2,1)S(1)}, bf16[1,256,256]{2,1,0:T(8,128)(2,1)S(1)}, u32[]{:S(2)}, u32[]{:S(2)}) collective-permute-start(bf16[1,256,256]{2,1,0:T(8,128)(2,1)S(1)} %copy-done.4), channel_id=1, source_target_pairs={{0,12},{4,8},{8,4},{12,0},{1,13},{5,9},{9,5},{13,1},{2,14},{6,10},... | collective-permute-start | bytes 393224 | tf_op jit(solution)/shard_map/ppermute | solution.py:292

commit v6 on v5

--- a/solution.py
+++ b/solution.py
@@ -13,8 +13,8 @@
 F32, BF16 = jnp.float32, jnp.bfloat16
 MIB = 1024 * 1024
 HEAD = 16
-UNROLL = 8
-LATE = 3
+STAGE = True
+BATCH = 4
 CONV_VMEM = 64
 SUM_VMEM = 24
 
@@ -54,11 +54,10 @@
     return lax.dot_general(a, b, (contract, ((), ())), preferred_element_type=F32)
 
 
-def weigh(rows, tables):
-    lane = rows[0].shape[1] // 2
-    (c, s), (tc, ts) = rows, tables
-    cc, cs, sc, ss = c[:, :lane], c[:, lane:], s[:, :lane], s[:, lane:]
-    pa, pb, qa, qb = tc[:, :lane], tc[:, lane:], ts[:, :lane], ts[:, lane:]
+def weigh(waves, tables):
+    sub, lane = tables.shape[0] // 2, tables.shape[1] // 2
+    (cc, cs), (sc, ss) = [(a[:, :lane], a[:, lane:]) for a in waves]
+    pa, pb, qa, qb = tables[:sub, :lane], tables[:sub, lane:], tables[sub:, :lane], tables[sub:, lane:]
     return (
         (pa * cc + pb * cs + qa * sc + qb * ss).astype(BF16),
         (pa * cs - pb * cc + qa * ss - qb * sc).astype(BF16),
@@ -93,20 +92,12 @@
     basis = kx.shape[0]
     lanes = lax.broadcasted_iota(jnp.int32, (1, 128), 1)
 
-    def convolved(slot):
+    row_ids = lax.broadcasted_iota(jnp.int32, (side, side), 0)
+
+    def mixing(slot):
         seen = visit[0, slot]
         weight = jnp.full((1, basis), inv_var[0, seen], F32).astype(BF16).astype(F32)
-        mixing = (weight * coef[seen].astype(BF16).astype(F32)).astype(BF16).astype(F32)
-        row_ids = lax.broadcasted_iota(jnp.int32, (side, side), 0)
-        masked = jnp.where(row_ids < valid[0, slot], patch[slot], 0.0).astype(BF16)
-        col = dot(masked, to_col[...]).astype(BF16)
-        mixed = (row_waves[...] * mixing).astype(BF16)
-        parts = (dot(to_row[:sub, :], col), dot(to_row[sub:, :], col))
-        tables = (dot(mixed[:sub], col_waves[...]), dot(mixed[sub:], col_waves[...]))
-        y_cc, y_cs, y_sc, y_ss = weigh(parts, tables)
-        z_c = dot(y_cc, from_col[:lane, :]) + dot(y_cs, from_col[lane:, :])
-        z_s = dot(y_sc, from_col[:lane, :]) + dot(y_ss, from_col[lane:, :])
-        return (dot(back[:, :sub], z_c.astype(BF16)) + dot(back[:, sub:], z_s.astype(BF16))).astype(BF16)
+        return (weight * coef[seen].astype(BF16).astype(F32)).astype(BF16).astype(F32)
 
     def sent(slot, phase, ref):
         return pltpu.make_async_copy(done.at[slot, phase * rows : (phase + 1) * rows, :], ref, out_sems.at[slot, phase])
@@ -134,16 +125,26 @@
             for index in range(plan["sky"]):
                 pl.when(box == index)(functools.partial(store, index))
 
-    def some(step, carry):
-        slots_now = [step * UNROLL + u for u in range(min(UNROLL, slots))]
-        for s in slots_now:
-            pltpu.make_async_copy(sources[-1].at[s], local[-1].at[s], sems.at[n_in - 1 + s]).wait()
-        results = [convolved(s) for s in slots_now]
-        for s, full in zip(slots_now, results):
-            deliver(s, full)
-        return carry
-
-    lax.fori_loop(0, max(1, slots // UNROLL), some, 0)
+    for batch in range(0, slots, BATCH):
+        group = range(batch, min(batch + BATCH, slots))
+        for s in group:
+            tiles[s].wait()
+        masked = [jnp.where(row_ids < valid[0, s], patch[s], 0.0).astype(BF16) for s in group]
+        mixed = [(row_waves[...] * mixing(s)).astype(BF16) for s in group]
+        col = dot(jnp.concatenate(masked, axis=0), to_col[...]).astype(BF16)
+        tables = dot(jnp.concatenate(mixed, axis=0), col_waves[...])
+        cos, sin = [], []
+        for n, s in enumerate(group):
+            mine = col[n * side : (n + 1) * side]
+            both = dot(to_row[...], mine)
+            y_cc, y_cs, y_sc, y_ss = weigh((both[:sub], both[sub:]), tables[n * 2 * sub : (n + 1) * 2 * sub])
+            cos, sin = cos + [y_cc, y_sc], sin + [y_cs, y_ss]
+        half = dot(jnp.concatenate(cos, axis=0), from_col[:lane, :])
+        half = half + dot(jnp.concatenate(sin, axis=0), from_col[lane:, :])
+        half = half.astype(BF16)
+        for n, s in enumerate(group):
+            full = dot(back[...], half[n * 2 * sub : (n + 1) * 2 * sub])
+            deliver(s, full.astype(BF16))
     width = patch.shape[2]
     copies = []
     for index in range(plan["sky"]):
@@ -225,6 +226,17 @@
     )
 
 
+def copy_kernel(source, out):
+    out[...] = source[...]
+
+
+def brought(array):
+    return pl.pallas_call(
+        copy_kernel, out_shape=jax.ShapeDtypeStruct(array.shape, array.dtype),
+        compiler_params=pltpu.CompilerParams(vmem_limit_bytes=SUM_VMEM * MIB), name="bring",
+    )(array)
+
+
 def accumulate_kernel(*refs):
     total, *terms, out = refs
     value = total[...]
@@ -243,7 +255,7 @@
     tables = wave_tables(side, kernel_x.shape[1])
     sub, lane = tables["sub"], tables["lane"]
     chunk = band_plan(nb)
-    late = min(LATE, nb - 1)
+    late = min(3, nb - 1)
     adds = [[]] * (nb - 1) + [list(range(nb - 1 - late))]
     box = cap * rows
     shaped = lambda count, height: jax.ShapeDtypeStruct((count, height, width), BF16)
@@ -252,16 +264,14 @@
         place = lambda outs, dest, phase: (outs[phase], dest, 0)
         head = lambda outs, dest: (outs[0], dest, box)
     else:
-        cut = lambda phase: shaped(1, box + (HEAD if phase == 0 else 0))
-        out_shapes = [shaped(1, nb * box + HEAD)] + [cut(phase) for phase in range(nb) for _ in range(3)]
+        far = lambda phase: shaped(1, box + (HEAD if phase == 0 else 0))
+        out_shapes = [shaped(1, nb * box + HEAD)] * 2 + [far(phase) for phase in range(nb) for _ in range(2)]
 
         def place(outs, dest, phase):
-            if dest == 1:
-                return outs[0], 0, phase * box
-            return outs[1 + 3 * phase + max(0, dest - 1)], 0, 0
+            return (outs[dest], 0, phase * box) if dest < 2 else (outs[2 * phase + dest], 0, 0)
 
         def head(outs, dest):
-            return place(outs, dest, 0)[0], 0, nb * box if dest == 1 else box
+            return outs[dest], 0, nb * box if dest < 2 else box
 
     plan = dict(sub=sub, lane=lane, rows=rows, nb=nb, scale=tables["scale"], slots=slots, cap=cap, sky=sky, per=PATCH_DEV,
                 single=single, n_boxes=1 if single else sky, place=place, head=head, chunk=chunk, adds=adds)
@@ -294,12 +304,15 @@
         moved = [lax.all_to_all(s, "sky", split_axis=0, concat_axis=0, tiled=True) for s in sent]
         pieces = lambda phase: [(moved[phase], sky, 0, 0, box)]
     else:
-        near = swap(sent[0], 1)
-        cuts = [swap(a, (0, 2, 3)[i % 3]) for i, a in enumerate(sent[1:])]
+        own, near, far = sent[0], swap(sent[1], 1), []
+        for i, array in enumerate(sent[2:]):
+            if i == 2 and STAGE:
+                own, array = lax.optimization_barrier((brought(own), array))
+            far.append(swap(array, 2 + i % 2))
 
         def pieces(phase):
-            mine, *others = cuts[3 * phase : 3 * phase + 3]
-            return [(mine, 1, 0, 0, box), (near, 1, 0, phase, nb * box)] + [(a, 1, 0, 0, box) for a in others]
+            here = [(a, 1, 0, phase, nb * box) for a in (own, near)]
+            return here + [(a, 1, 0, 0, box) for a in far[2 * phase : 2 * phase + 2]]
 
     band_buf, facts, arrived = None, None, []
     band_shape = jax.ShapeDtypeStruct((PATCH_DEV, side, width), F32)

time: 51.5 us -> 49.3 us (0.957)
  the two profiles are of different devices: /device:TPU:13 before, /device:TPU:9 now
where the time goes in v6:
time: 49.3 us; the launch traced here: 49.1 us
  Pallas kernels  17.6 us (36%)
  waiting for transfers between devices  17.5 us (35%)
  starting transfers between devices  12.1 us (25%)
  local copies, waits for them, and re-layouts  1.05 us (2%)
  between operations  0.73 us (1%)
    ppermute x9, waiting for transfers between devices, per_device(): lax.ppermute(a, 'sky', [(i, i ^ r) for i in range(sky)])  11.7 us
    pallas_call x4, Pallas kernels, per_device(): pl.pallas_call(functools.partial(sum_kernel, plan, phase), grid=(1,), out...  8.32 us
    ppermute x9, starting transfers between devices, per_device(): lax.ppermute(a, 'sky', [(i, i ^ r) for i in range(sky)])  8.3 us
    pallas_call x1, Pallas kernels, per_device(): pl.pallas_call(functools.partial(convolve_kernel, plan), out_shape=out_sh...  7.34 us
    ppermute x3, waiting for transfers between devices, per_device(): lax.ppermute(extra, 'band', [(b, chunk(b, phase)) for b in range(nb)])  5.87 us
    ppermute x3, starting transfers between devices, per_device(): lax.ppermute(extra, 'band', [(b, chunk(b, phase)) for b in range(nb)])  3.83 us
    pallas_call x1, Pallas kernels, per_device(): pl.pallas_call(accumulate_kernel, grid=(1,), out_shape=jax.ShapeDtypeStru...  1.94 us
    unnamed x6, local copies, waits for them, and re-layouts  1.05 us
  transfers between devices with their start and end apart: 12, of which 8 were waited for; matrix products, arithmetic and copies ran while one was open for 0% of the time, Pallas kernels for 17%

profile of v6, /device:TPU:9, one launch (start us, length us, event | category | flops | bytes accessed | tf_op | source)
XLA Modules:
  0.0 49.1 jit_solution(10473462749051475967)
XLA Ops:
  0.6 7.3 %convolve.1 = (bf16[1,1040,256]{2,1,0:T(8,128)(2,1)}, bf16[1,1040,256]{2,1,0:T(8,128)(2,1)}, bf16[1,272,256]{2,1,0:T(8,128)(2,1)}, bf16[1,272,256]{2,1,0:T(8,128...) custom-call(s32[1,8]{1,0:T(1,128)} %bitcast.7, ...), custom_call_target="tpu_custom_call" | custom-call | flops 2952790016 | bytes 3145728 | tf_op jit(solution)/shard_map/convolve/pallas_call | solution.py:285
  8.0 0.7 %collective-permute-start = (bf16[1,1040,256]{2,1,0:T(8,128)(2,1)}, bf16[1,1040,256]{2,1,0:T(8,128)(2,1)S(1)}, u32[]{:S(2)}, u32[]{:S(2)}) collective-permute-start(bf16[1,1040,256]{2,1,0:T(8,128)(2,1)} %get-tuple-element.31), channel_id=1, source_target_pairs={{0,4},{4,0},{8,12},{12,8},{1,5},{5,1},{9,13},{13,9},{2,6},{6,2},{1... | collective-permute-start | bytes 1597448 | tf_op jit(solution)/shard_map/ppermute | solution.py:302
  8.7 1.2 %collective-permute-start.3 = (bf16[1,272,256]{2,1,0:T(8,128)(2,1)}, bf16[1,272,256]{2,1,0:T(8,128)(2,1)S(1)}, u32[]{:S(2)}, u32[]{:S(2)}) collective-permute-start(bf16[1,272,256]{2,1,0:T(8,128)(2,1)} %get-tuple-element.34), channel_id=1, source_target_pairs={{0,8},{4,12},{8,0},{12,4},{1,9},{5,13},{9,1},{13,5},{2,10},{6,14},... | collective-permute-start | bytes 417800 | tf_op jit(solution)/shard_map/ppermute | solution.py:302
  10.4 1.0 %copy-done = bf16[1,1040,256]{2,1,0:T(8,128)(2,1)S(1)} copy-done((bf16[1,1040,256]{2,1,0:T(8,128)(2,1)S(1)}, bf16[1,1040,256]{2,1,0:T(8,128)(2,1)}, u32[]{:S(2)}) %copy-start) | copy-done | bytes 532504
  11.5 1.3 %collective-permute-start.7 = (bf16[1,256,256]{2,1,0:T(8,128)(2,1)}, bf16[1,256,256]{2,1,0:T(8,128)(2,1)S(1)}, u32[]{:S(2)}, u32[]{:S(2)}) collective-permute-start(bf16[1,256,256]{2,1,0:T(8,128)(2,1)} %get-tuple-element.40), channel_id=1, source_target_pairs={{0,8},{4,12},{8,0},{12,4},{1,9},{5,13},{9,1},{13,5},{2,10},{6,14},... | collective-permute-start | bytes 393224 | tf_op jit(solution)/shard_map/ppermute | solution.py:302
  12.8 0.6 %collective-permute-start.8 = (bf16[1,256,256]{2,1,0:T(8,128)(2,1)}, bf16[1,256,256]{2,1,0:T(8,128)(2,1)S(1)}, u32[]{:S(2)}, u32[]{:S(2)}) collective-permute-start(bf16[1,256,256]{2,1,0:T(8,128)(2,1)} %get-tuple-element.41), channel_id=1, source_target_pairs={{0,12},{4,8},{8,4},{12,0},{1,13},{5,9},{9,5},{13,1},{2,14},{6,10},... | collective-permute-start | bytes 393224 | tf_op jit(solution)/shard_map/ppermute | solution.py:302
  13.4 0.8 %collective-permute-done.3.refs_2_.refs_6_ = bf16[1,272,256]{2,1,0:T(8,128)(2,1)S(1)} collective-permute-done((bf16[1,272,256]{2,1,0:T(8,128)(2,1)}, bf16[1,272,256]{2,1,0:T(8,128)(2,1)S(1)}, u32[]{:S(2)}, u32[]{:S(2)}) %collective-permute-start.3) | collective-permute-done | bytes 139296 | tf_op jit(solution)/shard_map/ppermute | solution.py:302
  14.2 1.2 %collective-permute-start.5 = (bf16[1,256,256]{2,1,0:T(8,128)(2,1)}, bf16[1,256,256]{2,1,0:T(8,128)(2,1)S(1)}, u32[]{:S(2)}, u32[]{:S(2)}) collective-permute-start(bf16[1,256,256]{2,1,0:T(8,128)(2,1)} %get-tuple-element.38), channel_id=1, source_target_pairs={{0,8},{4,12},{8,0},{12,4},{1,9},{5,13},{9,1},{13,5},{2,10},{6,14},... | collective-permute-start | bytes 393224 | tf_op jit(solution)/shard_map/ppermute | solution.py:302
  15.4 2.4 %collective-permute-done.4.refs_3_.refs_7_ = bf16[1,272,256]{2,1,0:T(8,128)(2,1)S(1)} collective-permute-done((bf16[1,272,256]{2,1,0:T(8,128)(2,1)}, bf16[1,272,256]{2,1,0:T(8,128)(2,1)S(1)}, u32[]{:S(2)}, u32[]{:S(2)}) %collective-permute-start.4) | collective-permute-done | bytes 139296 | tf_op jit(solution)/shard_map/ppermute | solution.py:302
  17.8 0.9 %collective-permute-start.6 = (bf16[1,256,256]{2,1,0:T(8,128)(2,1)}, bf16[1,256,256]{2,1,0:T(8,128)(2,1)S(1)}, u32[]{:S(2)}, u32[]{:S(2)}) collective-permute-start(bf16[1,256,256]{2,1,0:T(8,128)(2,1)} %get-tuple-element.39), channel_id=1, source_target_pairs={{0,12},{4,8},{8,4},{12,0},{1,13},{5,9},{9,5},{13,1},{2,14},{6,10},... | collective-permute-start | bytes 393224 | tf_op jit(solution)/shard_map/ppermute | solution.py:302
  18.7 2.4 %add_up.4 = (f32[8,256,256]{2,1,0:T(8,128)}, bf16[8,64,256]{2,1,0:T(8,128)(2,1)S(1)}, s32[4,128]{1,0:T(4,128)S(1)}, f32[4,128]{1,0:T(4,128)S(1)}) custom-call(bf16[1,1040,256]{2,1,0:T(8,128)(2,1)S(1)} %bring.1.refs_0_.refs_4_, bf16[1,1040,256]{2,1,0:T(8,128)(2,1)S(1)} %collective-permute-done.refs_1_.refs_5_, ...), custom_call_target="tpu_custom_call" | custom-call | flops 524288 | bytes 1572864 | tf_op jit(solution)/shard_map/add_up/pallas_call | solution.py:343
  21.0 1.4 %collective-permute-start.9 = (bf16[8,64,256]{2,1,0:T(8,128)(2,1)S(1)}, bf16[8,64,256]{2,1,0:T(8,128)(2,1)S(1)}, u32[]{:S(2)}, u32[]{:S(2)}) collective-permute-start(bf16[8,64,256]{2,1,0:T(8,128)(2,1)S(1)} %get-tuple-element.47), channel_id=1, source_target_pairs={{0,1},{1,2},{2,3},{3,0},{4,5},{5,6},{6,7},{7,4},{8,9},{9,10},{10,1... | collective-permute-start | bytes 786440 | tf_op jit(solution)/shard_map/ppermute | solution.py:359
  22.4 1.0 %collective-permute-done.8.refs_3_ = bf16[1,256,256]{2,1,0:T(8,128)(2,1)S(1)} collective-permute-done((bf16[1,256,256]{2,1,0:T(8,128)(2,1)}, bf16[1,256,256]{2,1,0:T(8,128)(2,1)S(1)}, u32[]{:S(2)}, u32[]{:S(2)}) %collective-permute-start.8) | collective-permute-done | bytes 131104 | tf_op jit(solution)/shard_map/ppermute | solution.py:302
  23.4 1.7 %add_up.5 = (f32[8,256,256]{2,1,0:T(8,128)}, bf16[8,64,256]{2,1,0:T(8,128)(2,1)S(1)}) custom-call(bf16[1,1040,256]{2,1,0:T(8,128)(2,1)S(1)} %bring.1.refs_0_.refs_4_, bf16[1,1040,256]{2,1,0:T(8,128)(2,1)S(1)} %collective-permute-done.refs_1_.refs_5_, bf16[1,256,256]{2,1,0:T(8,128)(2,1)S(1)} %collective-permute-done.7.refs_2_, ...), custom_call_target="tpu_custom_call", output_to_operand_aliasing={{0}: (6, {})} | custom-call | flops 524288 | bytes 1572864 | tf_op jit(solution)/shard_map/add_up/pallas_call | solution.py:343
  25.1 2.4 %collective-permute-start.10 = (bf16[8,64,256]{2,1,0:T(8,128)(2,1)S(1)}, bf16[8,64,256]{2,1,0:T(8,128)(2,1)S(1)}, u32[]{:S(2)}, u32[]{:S(2)}) collective-permute-start(bf16[8,64,256]{2,1,0:T(8,128)(2,1)S(1)} %get-tuple-element.49), channel_id=1, source_target_pairs={{0,2},{1,3},{2,0},{3,1},{4,6},{5,7},{6,4},{7,5},{8,10},{9,11},{10,... | collective-permute-start | bytes 786440 | tf_op jit(solution)/shard_map/ppermute | solution.py:359
  27.5 1.3 %collective-permute-done.6.refs_3_ = bf16[1,256,256]{2,1,0:T(8,128)(2,1)S(1)} collective-permute-done((bf16[1,256,256]{2,1,0:T(8,128)(2,1)}, bf16[1,256,256]{2,1,0:T(8,128)(2,1)S(1)}, u32[]{:S(2)}, u32[]{:S(2)}) %collective-permute-start.6) | collective-permute-done | bytes 131104 | tf_op jit(solution)/shard_map/ppermute | solution.py:302
  28.8 1.7 %add_up.6 = (f32[8,256,256]{2,1,0:T(8,128)}, bf16[8,64,256]{2,1,0:T(8,128)(2,1)S(1)}) custom-call(bf16[1,1040,256]{2,1,0:T(8,128)(2,1)S(1)} %bring.1.refs_0_.refs_4_, bf16[1,1040,256]{2,1,0:T(8,128)(2,1)S(1)} %collective-permute-done.refs_1_.refs_5_, bf16[1,256,256]{2,1,0:T(8,128)(2,1)S(1)} %collective-permute-done.5.refs_2_, ...), custom_call_target="tpu_custom_call", output_to_operand_aliasing={{0}: (6, {})} | custom-call | flops 524288 | bytes 1572864 | tf_op jit(solution)/shard_map/add_up/pallas_call | solution.py:343
  30.6 1.4 %collective-permute-start.1 = (bf16[1,256,256]{2,1,0:T(8,128)(2,1)S(1)}, bf16[1,256,256]{2,1,0:T(8,128)(2,1)S(1)}, u32[]{:S(2)}, u32[]{:S(2)}) collective-permute-start(bf16[1,256,256]{2,1,0:T(8,128)(2,1)S(1)} %copy-done.2), channel_id=1, source_target_pairs={{0,8},{4,12},{8,0},{12,4},{1,9},{5,13},{9,1},{13,5},{2,10},{6,14},... | collective-permute-start | bytes 393224 | tf_op jit(solution)/shard_map/ppermute | solution.py:302
  32.5 3.1 %collective-permute-done.1.refs_2_ = bf16[1,256,256]{2,1,0:T(8,128)(2,1)S(1)} collective-permute-done((bf16[1,256,256]{2,1,0:T(8,128)(2,1)S(1)}, bf16[1,256,256]{2,1,0:T(8,128)(2,1)S(1)}, u32[]{:S(2)}, u32[]{:S(2)}) %collective-permute-start.1) | collective-permute-done | bytes 131104 | tf_op jit(solution)/shard_map/ppermute | solution.py:302
  35.6 3.1 %collective-permute-done.2.refs_3_ = bf16[1,256,256]{2,1,0:T(8,128)(2,1)S(1)} collective-permute-done((bf16[1,256,256]{2,1,0:T(8,128)(2,1)S(1)}, bf16[1,256,256]{2,1,0:T(8,128)(2,1)S(1)}, u32[]{:S(2)}, u32[]{:S(2)}) %collective-permute-start.2) | collective-permute-done | bytes 131104 | tf_op jit(solution)/shard_map/ppermute | solution.py:302
  38.7 2.5 %add_up.7 = (f32[8,256,256]{2,1,0:T(8,128)}, f32[8,64,256]{2,1,0:T(8,128)}) custom-call(bf16[1,1040,256]{2,1,0:T(8,128)(2,1)S(1)} %bring.1.refs_0_.refs_4_, bf16[1,1040,256]{2,1,0:T(8,128)(2,1)S(1)} %collective-permute-done.refs_1_.refs_5_, bf16[1,256,256]{2,1,0:T(8,128)(2,1)S(1)} %collective-permute-done.1.refs_2_, ...), custom_call_target="tpu_custom_call", output_to_operand_aliasing={{0}: (6, {})} | custom-call | flops 524288 | bytes 1572864 | tf_op jit(solution)/shard_map/add_up/pallas_call | solution.py:343
  41.3 3.6 %collective-permute-done.10.refs_2_ = bf16[8,64,256]{2,1,0:T(8,128)(2,1)S(1)} collective-permute-done((bf16[8,64,256]{2,1,0:T(8,128)(2,1)S(1)}, bf16[8,64,256]{2,1,0:T(8,128)(2,1)S(1)}, u32[]{:S(2)}, u32[]{:S(2)}) %collective-permute-start.10) | collective-permute-done | bytes 262176 | tf_op jit(solution)/shard_map/ppermute | solution.py:359
  44.9 2.2 %collective-permute-done.11.refs_3_ = bf16[8,64,256]{2,1,0:T(8,128)(2,1)S(1)} collective-permute-done((bf16[8,64,256]{2,1,0:T(8,128)(2,1)S(1)}, bf16[8,64,256]{2,1,0:T(8,128)(2,1)S(1)}, u32[]{:S(2)}, u32[]{:S(2)}) %collective-permute-start.11) | collective-permute-done | bytes 262176 | tf_op jit(solution)/shard_map/ppermute | solution.py:359
  47.1 1.9 %accumulate.1 = f32[8,64,256]{2,1,0:T(8,128)} custom-call(f32[8,64,256]{2,1,0:T(8,128)} %get-tuple-element.50.refs_0_, bf16[8,64,256]{2,1,0:T(8,128)(2,1)S(1)} %collective-permute-done.9.refs_1_, bf16[8,64,256]{2,1,0:T(8,128)(2,1)S(1)} %collective-permute-done.10.refs_2_, ...), custom_call_target="tpu_custom_call", output_to_operand_aliasing={{}: (0, {})} | custom-call | tf_op jit(solution)/shard_map/accumulate/pallas_call | solution.py:364
  (13 shorter events, 1.1 us)
Async XLA Ops:
  8.0 10.7 %collective-permute-start = (bf16[1,1040,256]{2,1,0:T(8,128)(2,1)}, bf16[1,1040,256]{2,1,0:T(8,128)(2,1)S(1)}, u32[]{:S(2)}, u32[]{:S(2)}) collective-permute-start(bf16[1,1040,256]{2,1,0:T(8,128)(2,1)} %get-tuple-element.31), channel_id=1, source_target_pairs={{0,4},{4,0},{8,12},{12,8},{1,5},{5,1},{9,13},{13,9},{2,6},{6,2},{1... | collective-permute-start | bytes 1597448 | tf_op jit(solution)/shard_map/ppermute | solution.py:302
  8.7 5.5 %collective-permute-start.3 = (bf16[1,272,256]{2,1,0:T(8,128)(2,1)}, bf16[1,272,256]{2,1,0:T(8,128)(2,1)S(1)}, u32[]{:S(2)}, u32[]{:S(2)}) collective-permute-start(bf16[1,272,256]{2,1,0:T(8,128)(2,1)} %get-tuple-element.34), channel_id=1, source_target_pairs={{0,8},{4,12},{8,0},{12,4},{1,9},{5,13},{9,1},{13,5},{2,10},{6,14},... | collective-permute-start | bytes 417800 | tf_op jit(solution)/shard_map/ppermute | solution.py:302
  9.9 7.8 %collective-permute-start.4 = (bf16[1,272,256]{2,1,0:T(8,128)(2,1)}, bf16[1,272,256]{2,1,0:T(8,128)(2,1)S(1)}, u32[]{:S(2)}, u32[]{:S(2)}) collective-permute-start(bf16[1,272,256]{2,1,0:T(8,128)(2,1)} %get-tuple-element.35), channel_id=1, source_target_pairs={{0,12},{4,8},{8,4},{12,0},{1,13},{5,9},{9,5},{13,1},{2,14},{6,10},... | collective-permute-start | bytes 417800 | tf_op jit(solution)/shard_map/ppermute | solution.py:302
  10.4 1.0 %copy-start = (bf16[1,1040,256]{2,1,0:T(8,128)(2,1)S(1)}, bf16[1,1040,256]{2,1,0:T(8,128)(2,1)}, u32[]{:S(2)}) copy-start(bf16[1,1040,256]{2,1,0:T(8,128)(2,1)} %get-tuple-element.28.source) | copy-start | bytes 1597444
  11.5 10.9 %collective-permute-start.7 = (bf16[1,256,256]{2,1,0:T(8,128)(2,1)}, bf16[1,256,256]{2,1,0:T(8,128)(2,1)S(1)}, u32[]{:S(2)}, u32[]{:S(2)}) collective-permute-start(bf16[1,256,256]{2,1,0:T(8,128)(2,1)} %get-tuple-element.40), channel_id=1, source_target_pairs={{0,8},{4,12},{8,0},{12,4},{1,9},{5,13},{9,1},{13,5},{2,10},{6,14},... | collective-permute-start | bytes 393224 | tf_op jit(solution)/shard_map/ppermute | solution.py:302
  12.8 10.6 %collective-permute-start.8 = (bf16[1,256,256]{2,1,0:T(8,128)(2,1)}, bf16[1,256,256]{2,1,0:T(8,128)(2,1)S(1)}, u32[]{:S(2)}, u32[]{:S(2)}) collective-permute-start(bf16[1,256,256]{2,1,0:T(8,128)(2,1)} %get-tuple-element.41), channel_id=1, source_target_pairs={{0,12},{4,8},{8,4},{12,0},{1,13},{5,9},{9,5},{13,1},{2,14},{6,10},... | collective-permute-start | bytes 393224 | tf_op jit(solution)/shard_map/ppermute | solution.py:302
  14.2 13.3 %collective-permute-start.5 = (bf16[1,256,256]{2,1,0:T(8,128)(2,1)}, bf16[1,256,256]{2,1,0:T(8,128)(2,1)S(1)}, u32[]{:S(2)}, u32[]{:S(2)}) collective-permute-start(bf16[1,256,256]{2,1,0:T(8,128)(2,1)} %get-tuple-element.38), channel_id=1, source_target_pairs={{0,8},{4,12},{8,0},{12,4},{1,9},{5,13},{9,1},{13,5},{2,10},{6,14},... | collective-permute-start | bytes 393224 | tf_op jit(solution)/shard_map/ppermute | solution.py:302
  17.8 11.1 %collective-permute-start.6 = (bf16[1,256,256]{2,1,0:T(8,128)(2,1)}, bf16[1,256,256]{2,1,0:T(8,128)(2,1)S(1)}, u32[]{:S(2)}, u32[]{:S(2)}) collective-permute-start(bf16[1,256,256]{2,1,0:T(8,128)(2,1)} %get-tuple-element.39), channel_id=1, source_target_pairs={{0,12},{4,8},{8,4},{12,0},{1,13},{5,9},{9,5},{13,1},{2,14},{6,10},... | collective-permute-start | bytes 393224 | tf_op jit(solution)/shard_map/ppermute | solution.py:302
  21.0 20.2 %collective-permute-start.9 = (bf16[8,64,256]{2,1,0:T(8,128)(2,1)S(1)}, bf16[8,64,256]{2,1,0:T(8,128)(2,1)S(1)}, u32[]{:S(2)}, u32[]{:S(2)}) collective-permute-start(bf16[8,64,256]{2,1,0:T(8,128)(2,1)S(1)} %get-tuple-element.47), channel_id=1, source_target_pairs={{0,1},{1,2},{2,3},{3,0},{4,5},{5,6},{6,7},{7,4},{8,9},{9,10},{10,1... | collective-permute-start | bytes 786440 | tf_op jit(solution)/shard_map/ppermute | solution.py:359
  25.1 5.5 %copy-start.2 = (bf16[1,256,256]{2,1,0:T(8,128)(2,1)S(1)}, bf16[1,256,256]{2,1,0:T(8,128)(2,1)}, u32[]{:S(2)}) copy-start(bf16[1,256,256]{2,1,0:T(8,128)(2,1)} %get-tuple-element.32) | copy-start | bytes 393220
  25.1 6.9 %copy-start.1 = (bf16[1,256,256]{2,1,0:T(8,128)(2,1)S(1)}, bf16[1,256,256]{2,1,0:T(8,128)(2,1)}, u32[]{:S(2)}) copy-start(bf16[1,256,256]{2,1,0:T(8,128)(2,1)} %get-tuple-element.33) | copy-start | bytes 393220
  25.1 19.8 %collective-permute-start.10 = (bf16[8,64,256]{2,1,0:T(8,128)(2,1)S(1)}, bf16[8,64,256]{2,1,0:T(8,128)(2,1)S(1)}, u32[]{:S(2)}, u32[]{:S(2)}) collective-permute-start(bf16[8,64,256]{2,1,0:T(8,128)(2,1)S(1)} %get-tuple-element.49), channel_id=1, source_target_pairs={{0,2},{1,3},{2,0},{3,1},{4,6},{5,7},{6,4},{7,5},{8,10},{9,11},{10,... | collective-permute-start | bytes 786440 | tf_op jit(solution)/shard_map/ppermute | solution.py:359
  30.6 16.6 %collective-permute-start.11 = (bf16[8,64,256]{2,1,0:T(8,128)(2,1)S(1)}, bf16[8,64,256]{2,1,0:T(8,128)(2,1)S(1)}, u32[]{:S(2)}, u32[]{:S(2)}) collective-permute-start(bf16[8,64,256]{2,1,0:T(8,128)(2,1)S(1)} %get-tuple-element.53), channel_id=1, source_target_pairs={{0,3},{1,0},{2,1},{3,2},{4,7},{5,4},{6,5},{7,6},{8,11},{9,8},{10,9... | collective-permute-start | bytes 786440 | tf_op jit(solution)/shard_map/ppermute | solution.py:359
  30.6 5.0 %collective-permute-start.1 = (bf16[1,256,256]{2,1,0:T(8,128)(2,1)S(1)}, bf16[1,256,256]{2,1,0:T(8,128)(2,1)S(1)}, u32[]{:S(2)}, u32[]{:S(2)}) collective-permute-start(bf16[1,256,256]{2,1,0:T(8,128)(2,1)S(1)} %copy-done.2), channel_id=1, source_target_pairs={{0,8},{4,12},{8,0},{12,4},{1,9},{5,13},{9,1},{13,5},{2,10},{6,14},... | collective-permute-start | bytes 393224 | tf_op jit(solution)/shard_map/ppermute | solution.py:302
  32.0 6.7 %collective-permute-start.2 = (bf16[1,256,256]{2,1,0:T(8,128)(2,1)S(1)}, bf16[1,256,256]{2,1,0:T(8,128)(2,1)S(1)}, u32[]{:S(2)}, u32[]{:S(2)}) collective-permute-start(bf16[1,256,256]{2,1,0:T(8,128)(2,1)S(1)} %copy-done.1), channel_id=1, source_target_pairs={{0,12},{4,8},{8,4},{12,0},{1,13},{5,9},{9,5},{13,1},{2,14},{6,10},... | collective-permute-start | bytes 393224 | tf_op jit(solution)/shard_map/ppermute | solution.py:302

commit v7 on v6

--- a/solution.py
+++ b/solution.py
@@ -13,7 +13,6 @@
 F32, BF16 = jnp.float32, jnp.bfloat16
 MIB = 1024 * 1024
 HEAD = 16
-STAGE = True
 BATCH = 4
 CONV_VMEM = 64
 SUM_VMEM = 24
@@ -238,11 +237,17 @@
 
 
 def accumulate_kernel(*refs):
-    total, *terms, out = refs
-    value = total[...]
-    for term in terms:
-        value = value + term[...].astype(F32)
-    out[...] = value
+    total, *terms, out, held, sems = refs
+    copies = []
+    for patch in range(total.shape[0]):
+        value = total[patch]
+        for term in terms:
+            value = value + term[patch].astype(F32)
+        held[patch] = value
+        copies.append(pltpu.make_async_copy(held.at[patch], out.at[patch], sems.at[patch]))
+        copies[-1].start()
+    for copy in copies:
+        copy.wait()
 
 
 def per_device(patches, valid_rows, slot_owner, slot_local, slot_visit, basis_coef, inv_var, kernel_x, kernel_y):
@@ -304,11 +309,9 @@
         moved = [lax.all_to_all(s, "sky", split_axis=0, concat_axis=0, tiled=True) for s in sent]
         pieces = lambda phase: [(moved[phase], sky, 0, 0, box)]
     else:
-        own, near, far = sent[0], swap(sent[1], 1), []
-        for i, array in enumerate(sent[2:]):
-            if i == 2 and STAGE:
-                own, array = lax.optimization_barrier((brought(own), array))
-            far.append(swap(array, 2 + i % 2))
+        own, second = lax.optimization_barrier((brought(sent[0]), sent[4]))
+        near = swap(sent[1], 1)
+        far = [swap(a, 2 + i % 2) for i, a in enumerate([*sent[2:4], second, *sent[5:]])]
 
         def pieces(phase):
             here = [(a, 1, 0, phase, nb * box) for a in (own, near)]
@@ -363,7 +366,8 @@
             extra, terms[i] = lax.optimization_barrier((extra, terms[i]))
         extra = pl.pallas_call(
             accumulate_kernel, grid=(1,), out_shape=jax.ShapeDtypeStruct(chunk_shape, F32),
-            in_specs=[whole(chunk_shape)] * (1 + late), out_specs=whole(chunk_shape), input_output_aliases={0: 0},
+            in_specs=[whole(chunk_shape)] * (1 + late), out_specs=hbm,
+            scratch_shapes=[pltpu.VMEM(chunk_shape, F32), pltpu.SemaphoreType.DMA((PATCH_DEV,))],
             compiler_params=pltpu.CompilerParams(vmem_limit_bytes=SUM_VMEM * MIB), name="accumulate",
         )(extra, *terms)
     return (band_buf[None], extra)

time: 49.3 us -> 48.2 us (0.978)
  the two profiles are of different devices: /device:TPU:9 before, /device:TPU:13 now
where the time goes in v7:
time: 48.2 us; the launch traced here: 48 us
  waiting for transfers between devices  18.4 us (38%)
  Pallas kernels  15.7 us (33%)
  starting transfers between devices  12.2 us (25%)
  local copies, waits for them, and re-layouts  1.05 us (2%)
  between operations  0.71 us (1%)
    ppermute x9, waiting for transfers between devices, per_device(): lax.ppermute(a, 'sky', [(i, i ^ r) for i in range(sky)])  11.8 us
    ppermute x9, starting transfers between devices, per_device(): lax.ppermute(a, 'sky', [(i, i ^ r) for i in range(sky)])  8.25 us
    pallas_call x4, Pallas kernels, per_device(): pl.pallas_call(functools.partial(sum_kernel, plan, phase), grid=(1,), out...  7.4 us
    pallas_call x1, Pallas kernels, per_device(): pl.pallas_call(functools.partial(convolve_kernel, plan), out_shape=out_sh...  7.36 us
    ppermute x3, waiting for transfers between devices, per_device(): lax.ppermute(extra, 'band', [(b, chunk(b, phase)) for b in range(nb)])  6.58 us
    ppermute x3, starting transfers between devices, per_device(): lax.ppermute(extra, 'band', [(b, chunk(b, phase)) for b in range(nb)])  3.91 us
    unnamed x6, local copies, waits for them, and re-layouts  1.05 us
  transfers between devices with their start and end apart: 12, of which 8 were waited for; matrix products, arithmetic and copies ran while one was open for 0% of the time, Pallas kernels for 15%

profile of v7, /device:TPU:13, one launch (start us, length us, event | category | flops | bytes accessed | tf_op | source)
XLA Modules:
  0.0 48.0 jit_solution(7100541200848989954)
XLA Ops:
  0.6 7.4 %convolve.1 = (bf16[1,1040,256]{2,1,0:T(8,128)(2,1)}, bf16[1,1040,256]{2,1,0:T(8,128)(2,1)}, bf16[1,272,256]{2,1,0:T(8,128)(2,1)}, bf16[1,272,256]{2,1,0:T(8,128...) custom-call(s32[1,8]{1,0:T(1,128)} %bitcast.7, ...), custom_call_target="tpu_custom_call" | custom-call | flops 2952790016 | bytes 3145728 | tf_op jit(solution)/shard_map/convolve/pallas_call | solution.py:290
  8.0 0.7 %collective-permute-start = (bf16[1,1040,256]{2,1,0:T(8,128)(2,1)}, bf16[1,1040,256]{2,1,0:T(8,128)(2,1)S(1)}, u32[]{:S(2)}, u32[]{:S(2)}) collective-permute-start(bf16[1,1040,256]{2,1,0:T(8,128)(2,1)} %get-tuple-element.31), channel_id=1, source_target_pairs={{0,4},{4,0},{8,12},{12,8},{1,5},{5,1},{9,13},{13,9},{2,6},{6,2},{1... | collective-permute-start | bytes 1597448 | tf_op jit(solution)/shard_map/ppermute | solution.py:307
  8.7 1.2 %collective-permute-start.3 = (bf16[1,272,256]{2,1,0:T(8,128)(2,1)}, bf16[1,272,256]{2,1,0:T(8,128)(2,1)S(1)}, u32[]{:S(2)}, u32[]{:S(2)}) collective-permute-start(bf16[1,272,256]{2,1,0:T(8,128)(2,1)} %get-tuple-element.34), channel_id=1, source_target_pairs={{0,8},{4,12},{8,0},{12,4},{1,9},{5,13},{9,1},{13,5},{2,10},{6,14},... | collective-permute-start | bytes 417800 | tf_op jit(solution)/shard_map/ppermute | solution.py:307
  10.5 1.0 %copy-done = bf16[1,1040,256]{2,1,0:T(8,128)(2,1)S(1)} copy-done((bf16[1,1040,256]{2,1,0:T(8,128)(2,1)S(1)}, bf16[1,1040,256]{2,1,0:T(8,128)(2,1)}, u32[]{:S(2)}) %copy-start) | copy-done | bytes 532504
  11.5 1.3 %collective-permute-start.7 = (bf16[1,256,256]{2,1,0:T(8,128)(2,1)}, bf16[1,256,256]{2,1,0:T(8,128)(2,1)S(1)}, u32[]{:S(2)}, u32[]{:S(2)}) collective-permute-start(bf16[1,256,256]{2,1,0:T(8,128)(2,1)} %get-tuple-element.40), channel_id=1, source_target_pairs={{0,8},{4,12},{8,0},{12,4},{1,9},{5,13},{9,1},{13,5},{2,10},{6,14},... | collective-permute-start | bytes 393224 | tf_op jit(solution)/shard_map/ppermute | solution.py:307
  13.4 0.8 %collective-permute-done.3.refs_2_.refs_6_ = bf16[1,272,256]{2,1,0:T(8,128)(2,1)S(1)} collective-permute-done((bf16[1,272,256]{2,1,0:T(8,128)(2,1)}, bf16[1,272,256]{2,1,0:T(8,128)(2,1)S(1)}, u32[]{:S(2)}, u32[]{:S(2)}) %collective-permute-start.3) | collective-permute-done | bytes 139296 | tf_op jit(solution)/shard_map/ppermute | solution.py:307
  14.2 1.2 %collective-permute-start.5 = (bf16[1,256,256]{2,1,0:T(8,128)(2,1)}, bf16[1,256,256]{2,1,0:T(8,128)(2,1)S(1)}, u32[]{:S(2)}, u32[]{:S(2)}) collective-permute-start(bf16[1,256,256]{2,1,0:T(8,128)(2,1)} %get-tuple-element.38), channel_id=1, source_target_pairs={{0,8},{4,12},{8,0},{12,4},{1,9},{5,13},{9,1},{13,5},{2,10},{6,14},... | collective-permute-start | bytes 393224 | tf_op jit(solution)/shard_map/ppermute | solution.py:307
  15.4 2.4 %collective-permute-done.4.refs_3_.refs_7_ = bf16[1,272,256]{2,1,0:T(8,128)(2,1)S(1)} collective-permute-done((bf16[1,272,256]{2,1,0:T(8,128)(2,1)}, bf16[1,272,256]{2,1,0:T(8,128)(2,1)S(1)}, u32[]{:S(2)}, u32[]{:S(2)}) %collective-permute-start.4) | collective-permute-done | bytes 139296 | tf_op jit(solution)/shard_map/ppermute | solution.py:307
  17.8 0.9 %collective-permute-start.6 = (bf16[1,256,256]{2,1,0:T(8,128)(2,1)}, bf16[1,256,256]{2,1,0:T(8,128)(2,1)S(1)}, u32[]{:S(2)}, u32[]{:S(2)}) collective-permute-start(bf16[1,256,256]{2,1,0:T(8,128)(2,1)} %get-tuple-element.39), channel_id=1, source_target_pairs={{0,12},{4,8},{8,4},{12,0},{1,13},{5,9},{9,5},{13,1},{2,14},{6,10},... | collective-permute-start | bytes 393224 | tf_op jit(solution)/shard_map/ppermute | solution.py:307
  18.7 2.3 %add_up.4 = (f32[8,256,256]{2,1,0:T(8,128)}, bf16[8,64,256]{2,1,0:T(8,128)(2,1)S(1)}, s32[4,128]{1,0:T(4,128)S(1)}, f32[4,128]{1,0:T(4,128)S(1)}) custom-call(bf16[1,1040,256]{2,1,0:T(8,128)(2,1)S(1)} %bring.1.refs_0_.refs_4_, bf16[1,1040,256]{2,1,0:T(8,128)(2,1)S(1)} %collective-permute-done.refs_1_.refs_5_, ...), custom_call_target="tpu_custom_call" | custom-call | flops 524288 | bytes 1572864 | tf_op jit(solution)/shard_map/add_up/pallas_call | solution.py:346
  21.0 1.3 %collective-permute-start.9 = (bf16[8,64,256]{2,1,0:T(8,128)(2,1)S(1)}, bf16[8,64,256]{2,1,0:T(8,128)(2,1)S(1)}, u32[]{:S(2)}, u32[]{:S(2)}) collective-permute-start(bf16[8,64,256]{2,1,0:T(8,128)(2,1)S(1)} %get-tuple-element.47), channel_id=1, source_target_pairs={{0,1},{1,2},{2,3},{3,0},{4,5},{5,6},{6,7},{7,4},{8,9},{9,10},{10,1... | collective-permute-start | bytes 786440 | tf_op jit(solution)/shard_map/ppermute | solution.py:362
  22.4 1.0 %collective-permute-done.8.refs_3_ = bf16[1,256,256]{2,1,0:T(8,128)(2,1)S(1)} collective-permute-done((bf16[1,256,256]{2,1,0:T(8,128)(2,1)}, bf16[1,256,256]{2,1,0:T(8,128)(2,1)S(1)}, u32[]{:S(2)}, u32[]{:S(2)}) %collective-permute-start.8) | collective-permute-done | bytes 131104 | tf_op jit(solution)/shard_map/ppermute | solution.py:307
  23.4 1.7 %add_up.5 = (f32[8,256,256]{2,1,0:T(8,128)}, bf16[8,64,256]{2,1,0:T(8,128)(2,1)S(1)}) custom-call(bf16[1,1040,256]{2,1,0:T(8,128)(2,1)S(1)} %bring.1.refs_0_.refs_4_, bf16[1,1040,256]{2,1,0:T(8,128)(2,1)S(1)} %collective-permute-done.refs_1_.refs_5_, bf16[1,256,256]{2,1,0:T(8,128)(2,1)S(1)} %collective-permute-done.7.refs_2_, ...), custom_call_target="tpu_custom_call", output_to_operand_aliasing={{0}: (6, {})} | custom-call | flops 524288 | bytes 1572864 | tf_op jit(solution)/shard_map/add_up/pallas_call | solution.py:346
  25.1 2.4 %collective-permute-start.10 = (bf16[8,64,256]{2,1,0:T(8,128)(2,1)S(1)}, bf16[8,64,256]{2,1,0:T(8,128)(2,1)S(1)}, u32[]{:S(2)}, u32[]{:S(2)}) collective-permute-start(bf16[8,64,256]{2,1,0:T(8,128)(2,1)S(1)} %get-tuple-element.49), channel_id=1, source_target_pairs={{0,2},{1,3},{2,0},{3,1},{4,6},{5,7},{6,4},{7,5},{8,10},{9,11},{10,... | collective-permute-start | bytes 786440 | tf_op jit(solution)/shard_map/ppermute | solution.py:362
  27.5 1.4 %collective-permute-done.6.refs_3_ = bf16[1,256,256]{2,1,0:T(8,128)(2,1)S(1)} collective-permute-done((bf16[1,256,256]{2,1,0:T(8,128)(2,1)}, bf16[1,256,256]{2,1,0:T(8,128)(2,1)S(1)}, u32[]{:S(2)}, u32[]{:S(2)}) %collective-permute-start.6) | collective-permute-done | bytes 131104 | tf_op jit(solution)/shard_map/ppermute | solution.py:307
  28.9 1.7 %add_up.6 = (f32[8,256,256]{2,1,0:T(8,128)}, bf16[8,64,256]{2,1,0:T(8,128)(2,1)S(1)}) custom-call(bf16[1,1040,256]{2,1,0:T(8,128)(2,1)S(1)} %bring.1.refs_0_.refs_4_, bf16[1,1040,256]{2,1,0:T(8,128)(2,1)S(1)} %collective-permute-done.refs_1_.refs_5_, bf16[1,256,256]{2,1,0:T(8,128)(2,1)S(1)} %collective-permute-done.5.refs_2_, ...), custom_call_target="tpu_custom_call", output_to_operand_aliasing={{0}: (6, {})} | custom-call | flops 524288 | bytes 1572864 | tf_op jit(solution)/shard_map/add_up/pallas_call | solution.py:346
  30.8 1.2 %collective-permute-start.1 = (bf16[1,256,256]{2,1,0:T(8,128)(2,1)S(1)}, bf16[1,256,256]{2,1,0:T(8,128)(2,1)S(1)}, u32[]{:S(2)}, u32[]{:S(2)}) collective-permute-start(bf16[1,256,256]{2,1,0:T(8,128)(2,1)S(1)} %copy-done.2), channel_id=1, source_target_pairs={{0,8},{4,12},{8,0},{12,4},{1,9},{5,13},{9,1},{13,5},{2,10},{6,14},... | collective-permute-start | bytes 393224 | tf_op jit(solution)/shard_map/ppermute | solution.py:307
  32.0 0.7 %collective-permute-start.2 = (bf16[1,256,256]{2,1,0:T(8,128)(2,1)S(1)}, bf16[1,256,256]{2,1,0:T(8,128)(2,1)S(1)}, u32[]{:S(2)}, u32[]{:S(2)}) collective-permute-start(bf16[1,256,256]{2,1,0:T(8,128)(2,1)S(1)} %copy-done.1), channel_id=1, source_target_pairs={{0,12},{4,8},{8,4},{12,0},{1,13},{5,9},{9,5},{13,1},{2,14},{6,10},... | collective-permute-start | bytes 393224 | tf_op jit(solution)/shard_map/ppermute | solution.py:307
  32.6 3.0 %collective-permute-done.1.refs_2_ = bf16[1,256,256]{2,1,0:T(8,128)(2,1)S(1)} collective-permute-done((bf16[1,256,256]{2,1,0:T(8,128)(2,1)S(1)}, bf16[1,256,256]{2,1,0:T(8,128)(2,1)S(1)}, u32[]{:S(2)}, u32[]{:S(2)}) %collective-permute-start.1) | collective-permute-done | bytes 131104 | tf_op jit(solution)/shard_map/ppermute | solution.py:307
  35.7 3.2 %collective-permute-done.2.refs_3_ = bf16[1,256,256]{2,1,0:T(8,128)(2,1)S(1)} collective-permute-done((bf16[1,256,256]{2,1,0:T(8,128)(2,1)S(1)}, bf16[1,256,256]{2,1,0:T(8,128)(2,1)S(1)}, u32[]{:S(2)}, u32[]{:S(2)}) %collective-permute-start.2) | collective-permute-done | bytes 131104 | tf_op jit(solution)/shard_map/ppermute | solution.py:307
  38.8 1.7 %add_up.7 = (f32[8,256,256]{2,1,0:T(8,128)}, f32[8,64,256]{2,1,0:T(8,128)S(1)}) custom-call(bf16[1,1040,256]{2,1,0:T(8,128)(2,1)S(1)} %bring.1.refs_0_.refs_4_, bf16[1,1040,256]{2,1,0:T(8,128)(2,1)S(1)} %collective-permute-done.refs_1_.refs_5_, bf16[1,256,256]{2,1,0:T(8,128)(2,1)S(1)} %collective-permute-done.1.refs_2_, ...), custom_call_target="tpu_custom_call", output_to_operand_aliasing={{0}: (6, {})} | custom-call | flops 524288 | bytes 1572864 | tf_op jit(solution)/shard_map/add_up/pallas_call | solution.py:346
  40.5 4.4 %collective-permute-done.10.refs_2_ = bf16[8,64,256]{2,1,0:T(8,128)(2,1)S(1)} collective-permute-done((bf16[8,64,256]{2,1,0:T(8,128)(2,1)S(1)}, bf16[8,64,256]{2,1,0:T(8,128)(2,1)S(1)}, u32[]{:S(2)}, u32[]{:S(2)}) %collective-permute-start.10) | collective-permute-done | bytes 262176 | tf_op jit(solution)/shard_map/ppermute | solution.py:362
  44.9 2.2 %collective-permute-done.11.refs_3_ = bf16[8,64,256]{2,1,0:T(8,128)(2,1)S(1)} collective-permute-done((bf16[8,64,256]{2,1,0:T(8,128)(2,1)S(1)}, bf16[8,64,256]{2,1,0:T(8,128)(2,1)S(1)}, u32[]{:S(2)}, u32[]{:S(2)}) %collective-permute-start.11) | collective-permute-done | bytes 262176 | tf_op jit(solution)/shard_map/ppermute | solution.py:362
  47.1 0.9 %accumulate.1 = f32[8,64,256]{2,1,0:T(8,128)} custom-call(f32[8,64,256]{2,1,0:T(8,128)S(1)} %get-tuple-element.50.refs_0_, bf16[8,64,256]{2,1,0:T(8,128)(2,1)S(1)} %collective-permute-done.9.refs_1_, bf16[8,64,256]{2,1,0:T(8,128)(2,1)S(1)} %collective-permute-done.10.refs_2_, bf16[8,64,256]{2,1,0:T(8,128)(2,1)S(1)} %collective-permute-done.11.refs_3_), custom_call_target="tpu_custom_call" | custom-call | tf_op jit(solution)/shard_map/accumulate/pallas_call | solution.py:367
  (13 shorter events, 1.4 us)
Async XLA Ops:
  8.0 10.7 %collective-permute-start = (bf16[1,1040,256]{2,1,0:T(8,128)(2,1)}, bf16[1,1040,256]{2,1,0:T(8,128)(2,1)S(1)}, u32[]{:S(2)}, u32[]{:S(2)}) collective-permute-start(bf16[1,1040,256]{2,1,0:T(8,128)(2,1)} %get-tuple-element.31), channel_id=1, source_target_pairs={{0,4},{4,0},{8,12},{12,8},{1,5},{5,1},{9,13},{13,9},{2,6},{6,2},{1... | collective-permute-start | bytes 1597448 | tf_op jit(solution)/shard_map/ppermute | solution.py:307
  8.7 5.5 %collective-permute-start.3 = (bf16[1,272,256]{2,1,0:T(8,128)(2,1)}, bf16[1,272,256]{2,1,0:T(8,128)(2,1)S(1)}, u32[]{:S(2)}, u32[]{:S(2)}) collective-permute-start(bf16[1,272,256]{2,1,0:T(8,128)(2,1)} %get-tuple-element.34), channel_id=1, source_target_pairs={{0,8},{4,12},{8,0},{12,4},{1,9},{5,13},{9,1},{13,5},{2,10},{6,14},... | collective-permute-start | bytes 417800 | tf_op jit(solution)/shard_map/ppermute | solution.py:307
  10.0 7.8 %collective-permute-start.4 = (bf16[1,272,256]{2,1,0:T(8,128)(2,1)}, bf16[1,272,256]{2,1,0:T(8,128)(2,1)S(1)}, u32[]{:S(2)}, u32[]{:S(2)}) collective-permute-start(bf16[1,272,256]{2,1,0:T(8,128)(2,1)} %get-tuple-element.35), channel_id=1, source_target_pairs={{0,12},{4,8},{8,4},{12,0},{1,13},{5,9},{9,5},{13,1},{2,14},{6,10},... | collective-permute-start | bytes 417800 | tf_op jit(solution)/shard_map/ppermute | solution.py:307
  10.5 1.0 %copy-start = (bf16[1,1040,256]{2,1,0:T(8,128)(2,1)S(1)}, bf16[1,1040,256]{2,1,0:T(8,128)(2,1)}, u32[]{:S(2)}) copy-start(bf16[1,1040,256]{2,1,0:T(8,128)(2,1)} %get-tuple-element.28.source) | copy-start | bytes 1597444
  11.5 10.8 %collective-permute-start.7 = (bf16[1,256,256]{2,1,0:T(8,128)(2,1)}, bf16[1,256,256]{2,1,0:T(8,128)(2,1)S(1)}, u32[]{:S(2)}, u32[]{:S(2)}) collective-permute-start(bf16[1,256,256]{2,1,0:T(8,128)(2,1)} %get-tuple-element.40), channel_id=1, source_target_pairs={{0,8},{4,12},{8,0},{12,4},{1,9},{5,13},{9,1},{13,5},{2,10},{6,14},... | collective-permute-start | bytes 393224 | tf_op jit(solution)/shard_map/ppermute | solution.py:307
  12.8 10.6 %collective-permute-start.8 = (bf16[1,256,256]{2,1,0:T(8,128)(2,1)}, bf16[1,256,256]{2,1,0:T(8,128)(2,1)S(1)}, u32[]{:S(2)}, u32[]{:S(2)}) collective-permute-start(bf16[1,256,256]{2,1,0:T(8,128)(2,1)} %get-tuple-element.41), channel_id=1, source_target_pairs={{0,12},{4,8},{8,4},{12,0},{1,13},{5,9},{9,5},{13,1},{2,14},{6,10},... | collective-permute-start | bytes 393224 | tf_op jit(solution)/shard_map/ppermute | solution.py:307
  14.2 13.3 %collective-permute-start.5 = (bf16[1,256,256]{2,1,0:T(8,128)(2,1)}, bf16[1,256,256]{2,1,0:T(8,128)(2,1)S(1)}, u32[]{:S(2)}, u32[]{:S(2)}) collective-permute-start(bf16[1,256,256]{2,1,0:T(8,128)(2,1)} %get-tuple-element.38), channel_id=1, source_target_pairs={{0,8},{4,12},{8,0},{12,4},{1,9},{5,13},{9,1},{13,5},{2,10},{6,14},... | collective-permute-start | bytes 393224 | tf_op jit(solution)/shard_map/ppermute | solution.py:307
  17.8 11.1 %collective-permute-start.6 = (bf16[1,256,256]{2,1,0:T(8,128)(2,1)}, bf16[1,256,256]{2,1,0:T(8,128)(2,1)S(1)}, u32[]{:S(2)}, u32[]{:S(2)}) collective-permute-start(bf16[1,256,256]{2,1,0:T(8,128)(2,1)} %get-tuple-element.39), channel_id=1, source_target_pairs={{0,12},{4,8},{8,4},{12,0},{1,13},{5,9},{9,5},{13,1},{2,14},{6,10},... | collective-permute-start | bytes 393224 | tf_op jit(solution)/shard_map/ppermute | solution.py:307
  21.0 19.5 %collective-permute-start.9 = (bf16[8,64,256]{2,1,0:T(8,128)(2,1)S(1)}, bf16[8,64,256]{2,1,0:T(8,128)(2,1)S(1)}, u32[]{:S(2)}, u32[]{:S(2)}) collective-permute-start(bf16[8,64,256]{2,1,0:T(8,128)(2,1)S(1)} %get-tuple-element.47), channel_id=1, source_target_pairs={{0,1},{1,2},{2,3},{3,0},{4,5},{5,6},{6,7},{7,4},{8,9},{9,10},{10,1... | collective-permute-start | bytes 786440 | tf_op jit(solution)/shard_map/ppermute | solution.py:362
  25.1 5.7 %copy-start.2 = (bf16[1,256,256]{2,1,0:T(8,128)(2,1)S(1)}, bf16[1,256,256]{2,1,0:T(8,128)(2,1)}, u32[]{:S(2)}) copy-start(bf16[1,256,256]{2,1,0:T(8,128)(2,1)} %get-tuple-element.32) | copy-start | bytes 393220
  25.1 6.9 %copy-start.1 = (bf16[1,256,256]{2,1,0:T(8,128)(2,1)S(1)}, bf16[1,256,256]{2,1,0:T(8,128)(2,1)}, u32[]{:S(2)}) copy-start(bf16[1,256,256]{2,1,0:T(8,128)(2,1)} %get-tuple-element.33) | copy-start | bytes 393220
  25.1 19.8 %collective-permute-start.10 = (bf16[8,64,256]{2,1,0:T(8,128)(2,1)S(1)}, bf16[8,64,256]{2,1,0:T(8,128)(2,1)S(1)}, u32[]{:S(2)}, u32[]{:S(2)}) collective-permute-start(bf16[8,64,256]{2,1,0:T(8,128)(2,1)S(1)} %get-tuple-element.49), channel_id=1, source_target_pairs={{0,2},{1,3},{2,0},{3,1},{4,6},{5,7},{6,4},{7,5},{8,10},{9,11},{10,... | collective-permute-start | bytes 786440 | tf_op jit(solution)/shard_map/ppermute | solution.py:362
  30.6 16.5 %collective-permute-start.11 = (bf16[8,64,256]{2,1,0:T(8,128)(2,1)S(1)}, bf16[8,64,256]{2,1,0:T(8,128)(2,1)S(1)}, u32[]{:S(2)}, u32[]{:S(2)}) collective-permute-start(bf16[8,64,256]{2,1,0:T(8,128)(2,1)S(1)} %get-tuple-element.53), channel_id=1, source_target_pairs={{0,3},{1,0},{2,1},{3,2},{4,7},{5,4},{6,5},{7,6},{8,11},{9,8},{10,9... | collective-permute-start | bytes 786440 | tf_op jit(solution)/shard_map/ppermute | solution.py:362
  30.8 4.9 %collective-permute-start.1 = (bf16[1,256,256]{2,1,0:T(8,128)(2,1)S(1)}, bf16[1,256,256]{2,1,0:T(8,128)(2,1)S(1)}, u32[]{:S(2)}, u32[]{:S(2)}) collective-permute-start(bf16[1,256,256]{2,1,0:T(8,128)(2,1)S(1)} %copy-done.2), channel_id=1, source_target_pairs={{0,8},{4,12},{8,0},{12,4},{1,9},{5,13},{9,1},{13,5},{2,10},{6,14},... | collective-permute-start | bytes 393224 | tf_op jit(solution)/shard_map/ppermute | solution.py:307
  32.0 6.8 %collective-permute-start.2 = (bf16[1,256,256]{2,1,0:T(8,128)(2,1)S(1)}, bf16[1,256,256]{2,1,0:T(8,128)(2,1)S(1)}, u32[]{:S(2)}, u32[]{:S(2)}) collective-permute-start(bf16[1,256,256]{2,1,0:T(8,128)(2,1)S(1)} %copy-done.1), channel_id=1, source_target_pairs={{0,12},{4,8},{8,4},{12,0},{1,13},{5,9},{9,5},{13,1},{2,14},{6,10},... | collective-permute-start | bytes 393224 | tf_op jit(solution)/shard_map/ppermute | solution.py:307

commit v8 on v7

--- a/solution.py
+++ b/solution.py
@@ -166,24 +166,42 @@
     take = lambda n: [refs.pop(0) for _ in range(n)]
     boxes = take(plan["n_boxes"])
     arrived = take(len(plan["adds"][phase]))
-    heads = take(plan["n_boxes"]) if first else None
     facts = None if first else take(2)
-    if not first:
-        take(1)
-    band_out, extra = take(2)
+    earlier = take(nb - 1) if last else []
+    if last:
+        band_out, extra = take(2)
+    else:
+        acc, extra = take(2)
     if first:
         facts = take(2)
-    acc, cov, sems = take(3)
+    if last:
+        acc, sems = take(2)
+    (cov,) = take(1)
+    if first:
+        (fact_sems,) = take(1)
     if first:
         whole_facts, weights = take(2)
-        rows_of = [h[d, 0:1, :128].astype(F32) for h in heads for d in range(h.shape[0])]
+        rows_of = []
+        for source in range(sky):
+            group, at = (0, source) if plan["single"] else (source, 0)
+            rows_of.append(boxes[group][at, plan["ends"][group] : plan["ends"][group] + HEAD, :128][0:1].astype(F32))
         for source, row in enumerate(rows_of):
             whole_facts[source : source + 1, :] = row.astype(jnp.int32)
             weights[source : source + 1, :] = row
-        copies = [pltpu.make_async_copy(a, b, sems.at[i]) for i, (a, b) in enumerate(((whole_facts, facts[0]), (weights, facts[1])))]
+        copies = [pltpu.make_async_copy(a, b, fact_sems.at[i]) for i, (a, b) in enumerate(((whole_facts, facts[0]), (weights, facts[1])))]
         for copy in copies:
             copy.start()
-    chunk = plan["chunk"](lax.axis_index("band"), phase)
+    band = lax.axis_index("band")
+    chunk = plan["chunk"](band, phase)
+
+    def out_rows(patch, at):
+        return band_out.at[patch, pl.ds(pl.multiple_of(plan["chunk"](band, at) * rows, rows), rows), :]
+
+    writes = []
+    for at, done in enumerate(earlier):
+        for patch in range(per):
+            writes.append(pltpu.make_async_copy(done.at[patch], out_rows(patch, at), sems.at[at, patch]))
+            writes[-1].start()
     acc[...] = jnp.zeros_like(acc)
     cov[...] = jnp.zeros_like(cov)
     row_ids = chunk * rows + lax.broadcasted_iota(jnp.int32, (rows, 128), 0)
@@ -197,12 +215,12 @@
 
             @pl.when(local >= 0)
             def _(group=group, at=at, rank=rank, source=source, local=local):
-                acc[local] += boxes[group][at, rank * rows : (rank + 1) * rows, :].astype(F32)
+                start = plan["starts"][phase][group] + rank * rows
+                acc[local] += boxes[group][at, start : start + rows, :].astype(F32)
                 weight = jnp.full((rows, 128), facts[1][source, 8 * rank + 2], F32)
                 cov[local] += jnp.where(row_ids < facts[0][source, 8 * rank + 1], weight, 0.0)
 
     width = acc.shape[2]
-    copies = []
     for patch in range(per):
         factor = 1.0 / jnp.maximum(cov[patch], 1.0)
         for at in range(0, width, 128):
@@ -211,11 +229,11 @@
             for other in arrived:
                 value = value + other[patch, :, at : at + 128].astype(F32)
             extra[patch, :, at : at + 128] = value.astype(extra.dtype)
-        copies.append(pltpu.make_async_copy(
-            acc.at[patch], band_out.at[patch, pl.ds(pl.multiple_of(chunk * rows, rows), rows), :], sems.at[patch]))
-        copies[-1].start()
-    for copy in copies:
-        copy.wait()
+        if last:
+            writes.append(pltpu.make_async_copy(acc.at[patch], out_rows(patch, phase), sems.at[phase, patch]))
+            writes[-1].start()
+    for write in writes:
+        write.wait()
 
 
 def band_plan(nb):
@@ -317,46 +335,44 @@
             here = [(a, 1, 0, phase, nb * box) for a in (own, near)]
             return here + [(a, 1, 0, 0, box) for a in far[2 * phase : 2 * phase + 2]]
 
-    band_buf, facts, arrived = None, None, []
+    facts, arrived, finished = None, [], []
     band_shape = jax.ShapeDtypeStruct((PATCH_DEV, side, width), F32)
     chunk_shape = (PATCH_DEV, rows, width)
-    whole = lambda shape: pl.BlockSpec(shape, lambda *_: (0,) * len(shape))
+    vmem = pl.BlockSpec(memory_space=pltpu.VMEM)
+    plan.update(starts=[[p[3] * box for p in pieces(phase)] for phase in range(nb)], ends=[p[4] for p in pieces(0)])
     fact_shapes = [jax.ShapeDtypeStruct((sky, 128), jnp.int32), jax.ShapeDtypeStruct((sky, 128), F32)]
     for phase in range(nb):
         first, last = phase == 0, phase == nb - 1
         inputs, specs = [], []
-        for array, count, at, row, _ in pieces(phase):
-            inputs.append(array)
-            specs.append(pl.BlockSpec((count, box, width), lambda i, at=at, row=row: (at, row, 0)))
+        inputs += [piece[0] for piece in pieces(phase)]
+        specs += [vmem] * len(inputs)
         for earlier in adds[phase]:
             inputs.append(arrived[earlier])
-            specs.append(whole(chunk_shape))
-        outs = [band_shape, jax.ShapeDtypeStruct(chunk_shape, F32 if last else BF16)]
-        out_specs, aliases, scratch = [hbm, whole(chunk_shape)], {}, []
+            specs.append(vmem)
+        outs = [band_shape if last else jax.ShapeDtypeStruct(chunk_shape, F32),
+                jax.ShapeDtypeStruct(chunk_shape, F32 if last else BF16)]
+        out_specs = [hbm if last else vmem, vmem]
+        scratch = [pltpu.VMEM(chunk_shape, F32), pltpu.SemaphoreType.DMA((nb, PATCH_DEV))] if last else []
+        scratch.append(pltpu.VMEM((PATCH_DEV, rows, 128), F32))
         if first:
-            for array, count, at, _, end in pieces(phase):
-                inputs.append(array)
-                specs.append(pl.BlockSpec((count, HEAD, width), lambda i, at=at, end=end: (at, end // HEAD, 0)))
             outs, out_specs = outs + fact_shapes, out_specs + [smem] * 2
-            scratch = [pltpu.VMEM(s.shape, s.dtype) for s in fact_shapes]
+            scratch += [pltpu.SemaphoreType.DMA((2,))] + [pltpu.VMEM(s.shape, s.dtype) for s in fact_shapes]
         else:
             inputs, specs = inputs + facts, specs + [smem] * 2
-            aliases = {len(inputs): 0}
-            inputs, specs = inputs + [band_buf], specs + [hbm]
-        band_buf, extra, *rest = pl.pallas_call(
+        if last:
+            inputs, specs = inputs + finished, specs + [vmem] * len(finished)
+        summed, extra, *rest = pl.pallas_call(
             functools.partial(sum_kernel, plan, phase),
-            grid=(1,),
             out_shape=outs,
             in_specs=specs,
             out_specs=out_specs,
-            scratch_shapes=[pltpu.VMEM(chunk_shape, F32), pltpu.VMEM((PATCH_DEV, rows, 128), F32),
-                            pltpu.SemaphoreType.DMA((PATCH_DEV,))] + scratch,
-            input_output_aliases=aliases,
+            scratch_shapes=scratch,
             compiler_params=pltpu.CompilerParams(vmem_limit_bytes=SUM_VMEM * MIB),
             cost_estimate=pl.CostEstimate(flops=4 * PATCH_DEV * rows * width,
                                           bytes_accessed=12 * PATCH_DEV * rows * width, transcendentals=0),
             name="add_up",
         )(*inputs)
+        finished.append(summed)
         facts = rest if first else facts
         if not last:
             arrived.append(lax.ppermute(extra, "band", [(b, chunk(b, phase)) for b in range(nb)]))
@@ -365,12 +381,12 @@
         for i in range(late - 1):
             extra, terms[i] = lax.optimization_barrier((extra, terms[i]))
         extra = pl.pallas_call(
-            accumulate_kernel, grid=(1,), out_shape=jax.ShapeDtypeStruct(chunk_shape, F32),
-            in_specs=[whole(chunk_shape)] * (1 + late), out_specs=hbm,
+            accumulate_kernel, out_shape=jax.ShapeDtypeStruct(chunk_shape, F32),
+            in_specs=[vmem] * (1 + late), out_specs=hbm,
             scratch_shapes=[pltpu.VMEM(chunk_shape, F32), pltpu.SemaphoreType.DMA((PATCH_DEV,))],
             compiler_params=pltpu.CompilerParams(vmem_limit_bytes=SUM_VMEM * MIB), name="accumulate",
         )(extra, *terms)
-    return (band_buf[None], extra)
+    return (summed[None], extra)
 
 
 def solution(mesh):

time: 48.2 us -> 47.4 us (0.983)
  Pallas kernels: 15.7 us -> 13.7 us
  waiting for transfers between devices: 18.4 us -> 19.5 us
    pallas_call x5, Pallas kernels: 8.27 us -> 6.34 us  [the longest x4 5.47 us: per_device(): pl.pallas_call(functools.partial(sum_kernel, plan, phase), out_shape=outs...]
    ppermute x9, waiting for transfers between devices: 11.8 us -> 13.4 us  [per_device(): lax.ppermute(a, 'sky', [(i, i ^ r) for i in range(sky)])]
    ppermute x3, waiting for transfers between devices: 6.58 us -> 6.09 us  [per_device(): lax.ppermute(extra, 'band', [(b, chunk(b, phase)) for b in range(nb)])]
  transfers between devices with their start and end apart: 12 -> 12, of which waited for: 8 -> 8; matrix products, arithmetic and copies ran while one was open for 0% -> 0% of each run, Pallas kernels for 15% -> 12%
where the time goes in v8:
time: 47.4 us; the launch traced here: 47.2 us
  waiting for transfers between devices  19.5 us (41%)
  Pallas kernels  13.7 us (29%)
  starting transfers between devices  12.2 us (26%)
  local copies, waits for them, and re-layouts  1.05 us (2%)
  between operations  0.71 us (1%)
    ppermute x9, waiting for transfers between devices, per_device(): lax.ppermute(a, 'sky', [(i, i ^ r) for i in range(sky)])  13.4 us
    ppermute x9, starting transfers between devices, per_device(): lax.ppermute(a, 'sky', [(i, i ^ r) for i in range(sky)])  8.23 us
    pallas_call x1, Pallas kernels, per_device(): pl.pallas_call(functools.partial(convolve_kernel, plan), out_shape=out_sh...  7.36 us
    ppermute x3, waiting for transfers between devices, per_device(): lax.ppermute(extra, 'band', [(b, chunk(b, phase)) for b in range(nb)])  6.09 us
    pallas_call x4, Pallas kernels, per_device(): pl.pallas_call(functools.partial(sum_kernel, plan, phase), out_shape=outs...  5.47 us
    ppermute x3, starting transfers between devices, per_device(): lax.ppermute(extra, 'band', [(b, chunk(b, phase)) for b in range(nb)])  3.92 us
    unnamed x6, local copies, waits for them, and re-layouts  1.05 us
  transfers between devices with their start and end apart: 12, of which 8 were waited for; matrix products, arithmetic and copies ran while one was open for 0% of the time, Pallas kernels for 12%

profile of v8, /device:TPU:13, one launch (start us, length us, event | category | flops | bytes accessed | tf_op | source)
XLA Modules:
  0.0 47.2 jit_solution(4785052911782091848)
XLA Ops:
  0.6 7.4 %convolve.1 = (bf16[1,1040,256]{2,1,0:T(8,128)(2,1)}, bf16[1,1040,256]{2,1,0:T(8,128)(2,1)}, bf16[1,272,256]{2,1,0:T(8,128)(2,1)}, bf16[1,272,256]{2,1,0:T(8,128...) custom-call(s32[1,8]{1,0:T(1,128)} %bitcast.7, ...), custom_call_target="tpu_custom_call" | custom-call | flops 2952790016 | bytes 3145728 | tf_op jit(solution)/shard_map/convolve/pallas_call | solution.py:308
  8.0 0.7 %collective-permute-start = (bf16[1,1040,256]{2,1,0:T(8,128)(2,1)}, bf16[1,1040,256]{2,1,0:T(8,128)(2,1)S(1)}, u32[]{:S(2)}, u32[]{:S(2)}) collective-permute-start(bf16[1,1040,256]{2,1,0:T(8,128)(2,1)} %get-tuple-element.31), channel_id=1, source_target_pairs={{0,4},{4,0},{8,12},{12,8},{1,5},{5,1},{9,13},{13,9},{2,6},{6,2},{1... | collective-permute-start | bytes 1597448 | tf_op jit(solution)/shard_map/ppermute | solution.py:325
  8.7 1.2 %collective-permute-start.3 = (bf16[1,272,256]{2,1,0:T(8,128)(2,1)}, bf16[1,272,256]{2,1,0:T(8,128)(2,1)S(1)}, u32[]{:S(2)}, u32[]{:S(2)}) collective-permute-start(bf16[1,272,256]{2,1,0:T(8,128)(2,1)} %get-tuple-element.34), channel_id=1, source_target_pairs={{0,8},{4,12},{8,0},{12,4},{1,9},{5,13},{9,1},{13,5},{2,10},{6,14},... | collective-permute-start | bytes 417800 | tf_op jit(solution)/shard_map/ppermute | solution.py:325
  10.5 1.0 %copy-done = bf16[1,1040,256]{2,1,0:T(8,128)(2,1)S(1)} copy-done((bf16[1,1040,256]{2,1,0:T(8,128)(2,1)S(1)}, bf16[1,1040,256]{2,1,0:T(8,128)(2,1)}, u32[]{:S(2)}) %copy-start) | copy-done | bytes 532504
  11.6 1.3 %collective-permute-start.5 = (bf16[1,256,256]{2,1,0:T(8,128)(2,1)}, bf16[1,256,256]{2,1,0:T(8,128)(2,1)S(1)}, u32[]{:S(2)}, u32[]{:S(2)}) collective-permute-start(bf16[1,256,256]{2,1,0:T(8,128)(2,1)} %get-tuple-element.39), channel_id=1, source_target_pairs={{0,8},{4,12},{8,0},{12,4},{1,9},{5,13},{9,1},{13,5},{2,10},{6,14},... | collective-permute-start | bytes 393224 | tf_op jit(solution)/shard_map/ppermute | solution.py:325
  12.8 0.6 %collective-permute-start.6 = (bf16[1,256,256]{2,1,0:T(8,128)(2,1)}, bf16[1,256,256]{2,1,0:T(8,128)(2,1)S(1)}, u32[]{:S(2)}, u32[]{:S(2)}) collective-permute-start(bf16[1,256,256]{2,1,0:T(8,128)(2,1)} %get-tuple-element.40), channel_id=1, source_target_pairs={{0,12},{4,8},{8,4},{12,0},{1,13},{5,9},{9,5},{13,1},{2,14},{6,10},... | collective-permute-start | bytes 393224 | tf_op jit(solution)/shard_map/ppermute | solution.py:325
  13.4 0.8 %collective-permute-done.3.refs_2_ = bf16[1,272,256]{2,1,0:T(8,128)(2,1)S(1)} collective-permute-done((bf16[1,272,256]{2,1,0:T(8,128)(2,1)}, bf16[1,272,256]{2,1,0:T(8,128)(2,1)S(1)}, u32[]{:S(2)}, u32[]{:S(2)}) %collective-permute-start.3) | collective-permute-done | bytes 139296 | tf_op jit(solution)/shard_map/ppermute | solution.py:325
  14.2 1.2 %collective-permute-start.7 = (bf16[1,256,256]{2,1,0:T(8,128)(2,1)}, bf16[1,256,256]{2,1,0:T(8,128)(2,1)S(1)}, u32[]{:S(2)}, u32[]{:S(2)}) collective-permute-start(bf16[1,256,256]{2,1,0:T(8,128)(2,1)} %get-tuple-element.42), channel_id=1, source_target_pairs={{0,8},{4,12},{8,0},{12,4},{1,9},{5,13},{9,1},{13,5},{2,10},{6,14},... | collective-permute-start | bytes 393224 | tf_op jit(solution)/shard_map/ppermute | solution.py:325
  15.4 2.4 %collective-permute-done.4.refs_3_ = bf16[1,272,256]{2,1,0:T(8,128)(2,1)S(1)} collective-permute-done((bf16[1,272,256]{2,1,0:T(8,128)(2,1)}, bf16[1,272,256]{2,1,0:T(8,128)(2,1)S(1)}, u32[]{:S(2)}, u32[]{:S(2)}) %collective-permute-start.4) | collective-permute-done | bytes 139296 | tf_op jit(solution)/shard_map/ppermute | solution.py:325
  17.8 0.9 %collective-permute-start.8 = (bf16[1,256,256]{2,1,0:T(8,128)(2,1)}, bf16[1,256,256]{2,1,0:T(8,128)(2,1)S(1)}, u32[]{:S(2)}, u32[]{:S(2)}) collective-permute-start(bf16[1,256,256]{2,1,0:T(8,128)(2,1)} %get-tuple-element.43), channel_id=1, source_target_pairs={{0,12},{4,8},{8,4},{12,0},{1,13},{5,9},{9,5},{13,1},{2,14},{6,10},... | collective-permute-start | bytes 393224 | tf_op jit(solution)/shard_map/ppermute | solution.py:325
  18.7 1.5 %add_up.4 = (f32[8,64,256]{2,1,0:T(8,128)S(1)}, bf16[8,64,256]{2,1,0:T(8,128)(2,1)S(1)}, s32[4,128]{1,0:T(4,128)S(1)}, f32[4,128]{1,0:T(4,128)S(1)}) custom-call(bf16[1,1040,256]{2,1,0:T(8,128)(2,1)S(1)} %bring.1.refs_0_, bf16[1,1040,256]{2,1,0:T(8,128)(2,1)S(1)} %collective-permute-done.refs_1_, bf16[1,272,256]{2,1,0:T(8,128)(2,1)S(1)} %collective-permute-done.3.refs_2_, ...), custom_call_target="tpu_custom_call" | custom-call | flops 524288 | bytes 1572864 | tf_op jit(solution)/shard_map/add_up/pallas_call | solution.py:364
  20.2 1.4 %collective-permute-start.9 = (bf16[8,64,256]{2,1,0:T(8,128)(2,1)S(1)}, bf16[8,64,256]{2,1,0:T(8,128)(2,1)S(1)}, u32[]{:S(2)}, u32[]{:S(2)}) collective-permute-start(bf16[8,64,256]{2,1,0:T(8,128)(2,1)S(1)} %get-tuple-element.47), channel_id=1, source_target_pairs={{0,1},{1,2},{2,3},{3,0},{4,5},{5,6},{6,7},{7,4},{8,9},{9,10},{10,1... | collective-permute-start | bytes 786440 | tf_op jit(solution)/shard_map/ppermute | solution.py:378
  21.5 1.9 %collective-permute-done.6.refs_3_ = bf16[1,256,256]{2,1,0:T(8,128)(2,1)S(1)} collective-permute-done((bf16[1,256,256]{2,1,0:T(8,128)(2,1)}, bf16[1,256,256]{2,1,0:T(8,128)(2,1)S(1)}, u32[]{:S(2)}, u32[]{:S(2)}) %collective-permute-start.6) | collective-permute-done | bytes 131104 | tf_op jit(solution)/shard_map/ppermute | solution.py:325
  23.4 0.9 %add_up.5 = (f32[8,64,256]{2,1,0:T(8,128)S(1)}, bf16[8,64,256]{2,1,0:T(8,128)(2,1)S(1)}) custom-call(bf16[1,1040,256]{2,1,0:T(8,128)(2,1)S(1)} %bring.1.refs_0_, bf16[1,1040,256]{2,1,0:T(8,128)(2,1)S(1)} %collective-permute-done.refs_1_, bf16[1,256,256]{2,1,0:T(8,128)(2,1)S(1)} %collective-permute-done.5.refs_2_, ...), custom_call_target="tpu_custom_call" | custom-call | flops 524288 | bytes 1572864 | tf_op jit(solution)/shard_map/add_up/pallas_call | solution.py:364
  24.3 2.4 %collective-permute-start.10 = (bf16[8,64,256]{2,1,0:T(8,128)(2,1)S(1)}, bf16[8,64,256]{2,1,0:T(8,128)(2,1)S(1)}, u32[]{:S(2)}, u32[]{:S(2)}) collective-permute-start(bf16[8,64,256]{2,1,0:T(8,128)(2,1)S(1)} %get-tuple-element.49), channel_id=1, source_target_pairs={{0,2},{1,3},{2,0},{3,1},{4,6},{5,7},{6,4},{7,5},{8,10},{9,11},{10,... | collective-permute-start | bytes 786440 | tf_op jit(solution)/shard_map/ppermute | solution.py:378
  26.7 2.2 %collective-permute-done.8.refs_3_ = bf16[1,256,256]{2,1,0:T(8,128)(2,1)S(1)} collective-permute-done((bf16[1,256,256]{2,1,0:T(8,128)(2,1)}, bf16[1,256,256]{2,1,0:T(8,128)(2,1)S(1)}, u32[]{:S(2)}, u32[]{:S(2)}) %collective-permute-start.8) | collective-permute-done | bytes 131104 | tf_op jit(solution)/shard_map/ppermute | solution.py:325
  28.9 0.9 %add_up.6 = (f32[8,64,256]{2,1,0:T(8,128)S(1)}, bf16[8,64,256]{2,1,0:T(8,128)(2,1)S(1)}) custom-call(bf16[1,1040,256]{2,1,0:T(8,128)(2,1)S(1)} %bring.1.refs_0_, bf16[1,1040,256]{2,1,0:T(8,128)(2,1)S(1)} %collective-permute-done.refs_1_, bf16[1,256,256]{2,1,0:T(8,128)(2,1)S(1)} %collective-permute-done.7.refs_2_, ...), custom_call_target="tpu_custom_call" | custom-call | flops 524288 | bytes 1572864 | tf_op jit(solution)/shard_map/add_up/pallas_call | solution.py:364
  30.0 1.3 %collective-permute-start.1 = (bf16[1,256,256]{2,1,0:T(8,128)(2,1)S(1)}, bf16[1,256,256]{2,1,0:T(8,128)(2,1)S(1)}, u32[]{:S(2)}, u32[]{:S(2)}) collective-permute-start(bf16[1,256,256]{2,1,0:T(8,128)(2,1)S(1)} %copy-done.2), channel_id=1, source_target_pairs={{0,8},{4,12},{8,0},{12,4},{1,9},{5,13},{9,1},{13,5},{2,10},{6,14},... | collective-permute-start | bytes 393224 | tf_op jit(solution)/shard_map/ppermute | solution.py:325
  31.8 3.1 %collective-permute-done.1.refs_2_ = bf16[1,256,256]{2,1,0:T(8,128)(2,1)S(1)} collective-permute-done((bf16[1,256,256]{2,1,0:T(8,128)(2,1)S(1)}, bf16[1,256,256]{2,1,0:T(8,128)(2,1)S(1)}, u32[]{:S(2)}, u32[]{:S(2)}) %collective-permute-start.1) | collective-permute-done | bytes 131104 | tf_op jit(solution)/shard_map/ppermute | solution.py:325
  34.9 3.1 %collective-permute-done.2.refs_3_ = bf16[1,256,256]{2,1,0:T(8,128)(2,1)S(1)} collective-permute-done((bf16[1,256,256]{2,1,0:T(8,128)(2,1)S(1)}, bf16[1,256,256]{2,1,0:T(8,128)(2,1)S(1)}, u32[]{:S(2)}, u32[]{:S(2)}) %collective-permute-start.2) | collective-permute-done | bytes 131104 | tf_op jit(solution)/shard_map/ppermute | solution.py:325
  38.0 2.2 %add_up.7 = (f32[8,256,256]{2,1,0:T(8,128)}, f32[8,64,256]{2,1,0:T(8,128)S(1)}) custom-call(bf16[1,1040,256]{2,1,0:T(8,128)(2,1)S(1)} %bring.1.refs_0_, bf16[1,1040,256]{2,1,0:T(8,128)(2,1)S(1)} %collective-permute-done.refs_1_, bf16[1,256,256]{2,1,0:T(8,128)(2,1)S(1)} %collective-permute-done.1.refs_2_, ...), custom_call_target="tpu_custom_call" | custom-call | flops 524288 | bytes 1572864 | tf_op jit(solution)/shard_map/add_up/pallas_call | solution.py:364
  40.2 3.9 %collective-permute-done.10.refs_2_ = bf16[8,64,256]{2,1,0:T(8,128)(2,1)S(1)} collective-permute-done((bf16[8,64,256]{2,1,0:T(8,128)(2,1)S(1)}, bf16[8,64,256]{2,1,0:T(8,128)(2,1)S(1)}, u32[]{:S(2)}, u32[]{:S(2)}) %collective-permute-start.10) | collective-permute-done | bytes 262176 | tf_op jit(solution)/shard_map/ppermute | solution.py:378
  44.1 2.2 %collective-permute-done.11.refs_3_ = bf16[8,64,256]{2,1,0:T(8,128)(2,1)S(1)} collective-permute-done((bf16[8,64,256]{2,1,0:T(8,128)(2,1)S(1)}, bf16[8,64,256]{2,1,0:T(8,128)(2,1)S(1)}, u32[]{:S(2)}, u32[]{:S(2)}) %collective-permute-start.11) | collective-permute-done | bytes 262176 | tf_op jit(solution)/shard_map/ppermute | solution.py:378
  46.3 0.9 %accumulate.1 = f32[8,64,256]{2,1,0:T(8,128)} custom-call(f32[8,64,256]{2,1,0:T(8,128)S(1)} %get-tuple-element.50.refs_0_, bf16[8,64,256]{2,1,0:T(8,128)(2,1)S(1)} %collective-permute-done.9.refs_1_, bf16[8,64,256]{2,1,0:T(8,128)(2,1)S(1)} %collective-permute-done.10.refs_2_, bf16[8,64,256]{2,1,0:T(8,128)(2,1)S(1)} %collective-permute-done.11.refs_3_), custom_call_target="tpu_custom_call" | custom-call | tf_op jit(solution)/shard_map/accumulate/pallas_call | solution.py:383
  (13 shorter events, 1.3 us)
Async XLA Ops:
  8.0 10.7 %collective-permute-start = (bf16[1,1040,256]{2,1,0:T(8,128)(2,1)}, bf16[1,1040,256]{2,1,0:T(8,128)(2,1)S(1)}, u32[]{:S(2)}, u32[]{:S(2)}) collective-permute-start(bf16[1,1040,256]{2,1,0:T(8,128)(2,1)} %get-tuple-element.31), channel_id=1, source_target_pairs={{0,4},{4,0},{8,12},{12,8},{1,5},{5,1},{9,13},{13,9},{2,6},{6,2},{1... | collective-permute-start | bytes 1597448 | tf_op jit(solution)/shard_map/ppermute | solution.py:325
  8.7 5.5 %collective-permute-start.3 = (bf16[1,272,256]{2,1,0:T(8,128)(2,1)}, bf16[1,272,256]{2,1,0:T(8,128)(2,1)S(1)}, u32[]{:S(2)}, u32[]{:S(2)}) collective-permute-start(bf16[1,272,256]{2,1,0:T(8,128)(2,1)} %get-tuple-element.34), channel_id=1, source_target_pairs={{0,8},{4,12},{8,0},{12,4},{1,9},{5,13},{9,1},{13,5},{2,10},{6,14},... | collective-permute-start | bytes 417800 | tf_op jit(solution)/shard_map/ppermute | solution.py:325
  10.0 7.8 %collective-permute-start.4 = (bf16[1,272,256]{2,1,0:T(8,128)(2,1)}, bf16[1,272,256]{2,1,0:T(8,128)(2,1)S(1)}, u32[]{:S(2)}, u32[]{:S(2)}) collective-permute-start(bf16[1,272,256]{2,1,0:T(8,128)(2,1)} %get-tuple-element.35), channel_id=1, source_target_pairs={{0,12},{4,8},{8,4},{12,0},{1,13},{5,9},{9,5},{13,1},{2,14},{6,10},... | collective-permute-start | bytes 417800 | tf_op jit(solution)/shard_map/ppermute | solution.py:325
  10.4 1.0 %copy-start = (bf16[1,1040,256]{2,1,0:T(8,128)(2,1)S(1)}, bf16[1,1040,256]{2,1,0:T(8,128)(2,1)}, u32[]{:S(2)}) copy-start(bf16[1,1040,256]{2,1,0:T(8,128)(2,1)} %get-tuple-element.28.source) | copy-start | bytes 1597444
  11.5 18.4 %copy-start.2 = (bf16[1,256,256]{2,1,0:T(8,128)(2,1)S(1)}, bf16[1,256,256]{2,1,0:T(8,128)(2,1)}, u32[]{:S(2)}) copy-start(bf16[1,256,256]{2,1,0:T(8,128)(2,1)} %get-tuple-element.32) | copy-start | bytes 393220
  11.5 19.7 %copy-start.1 = (bf16[1,256,256]{2,1,0:T(8,128)(2,1)S(1)}, bf16[1,256,256]{2,1,0:T(8,128)(2,1)}, u32[]{:S(2)}) copy-start(bf16[1,256,256]{2,1,0:T(8,128)(2,1)} %get-tuple-element.33) | copy-start | bytes 393220
  11.6 10.0 %collective-permute-start.5 = (bf16[1,256,256]{2,1,0:T(8,128)(2,1)}, bf16[1,256,256]{2,1,0:T(8,128)(2,1)S(1)}, u32[]{:S(2)}, u32[]{:S(2)}) collective-permute-start(bf16[1,256,256]{2,1,0:T(8,128)(2,1)} %get-tuple-element.39), channel_id=1, source_target_pairs={{0,8},{4,12},{8,0},{12,4},{1,9},{5,13},{9,1},{13,5},{2,10},{6,14},... | collective-permute-start | bytes 393224 | tf_op jit(solution)/shard_map/ppermute | solution.py:325
  12.8 10.6 %collective-permute-start.6 = (bf16[1,256,256]{2,1,0:T(8,128)(2,1)}, bf16[1,256,256]{2,1,0:T(8,128)(2,1)S(1)}, u32[]{:S(2)}, u32[]{:S(2)}) collective-permute-start(bf16[1,256,256]{2,1,0:T(8,128)(2,1)} %get-tuple-element.40), channel_id=1, source_target_pairs={{0,12},{4,8},{8,4},{12,0},{1,13},{5,9},{9,5},{13,1},{2,14},{6,10},... | collective-permute-start | bytes 393224 | tf_op jit(solution)/shard_map/ppermute | solution.py:325
  14.2 12.5 %collective-permute-start.7 = (bf16[1,256,256]{2,1,0:T(8,128)(2,1)}, bf16[1,256,256]{2,1,0:T(8,128)(2,1)S(1)}, u32[]{:S(2)}, u32[]{:S(2)}) collective-permute-start(bf16[1,256,256]{2,1,0:T(8,128)(2,1)} %get-tuple-element.42), channel_id=1, source_target_pairs={{0,8},{4,12},{8,0},{12,4},{1,9},{5,13},{9,1},{13,5},{2,10},{6,14},... | collective-permute-start | bytes 393224 | tf_op jit(solution)/shard_map/ppermute | solution.py:325
  17.8 11.1 %collective-permute-start.8 = (bf16[1,256,256]{2,1,0:T(8,128)(2,1)}, bf16[1,256,256]{2,1,0:T(8,128)(2,1)S(1)}, u32[]{:S(2)}, u32[]{:S(2)}) collective-permute-start(bf16[1,256,256]{2,1,0:T(8,128)(2,1)} %get-tuple-element.43), channel_id=1, source_target_pairs={{0,12},{4,8},{8,4},{12,0},{1,13},{5,9},{9,5},{13,1},{2,14},{6,10},... | collective-permute-start | bytes 393224 | tf_op jit(solution)/shard_map/ppermute | solution.py:325
  20.2 20.0 %collective-permute-start.9 = (bf16[8,64,256]{2,1,0:T(8,128)(2,1)S(1)}, bf16[8,64,256]{2,1,0:T(8,128)(2,1)S(1)}, u32[]{:S(2)}, u32[]{:S(2)}) collective-permute-start(bf16[8,64,256]{2,1,0:T(8,128)(2,1)S(1)} %get-tuple-element.47), channel_id=1, source_target_pairs={{0,1},{1,2},{2,3},{3,0},{4,5},{5,6},{6,7},{7,4},{8,9},{9,10},{10,1... | collective-permute-start | bytes 786440 | tf_op jit(solution)/shard_map/ppermute | solution.py:378
  24.3 19.8 %collective-permute-start.10 = (bf16[8,64,256]{2,1,0:T(8,128)(2,1)S(1)}, bf16[8,64,256]{2,1,0:T(8,128)(2,1)S(1)}, u32[]{:S(2)}, u32[]{:S(2)}) collective-permute-start(bf16[8,64,256]{2,1,0:T(8,128)(2,1)S(1)} %get-tuple-element.49), channel_id=1, source_target_pairs={{0,2},{1,3},{2,0},{3,1},{4,6},{5,7},{6,4},{7,5},{8,10},{9,11},{10,... | collective-permute-start | bytes 786440 | tf_op jit(solution)/shard_map/ppermute | solution.py:378
  29.8 16.5 %collective-permute-start.11 = (bf16[8,64,256]{2,1,0:T(8,128)(2,1)S(1)}, bf16[8,64,256]{2,1,0:T(8,128)(2,1)S(1)}, u32[]{:S(2)}, u32[]{:S(2)}) collective-permute-start(bf16[8,64,256]{2,1,0:T(8,128)(2,1)S(1)} %get-tuple-element.53), channel_id=1, source_target_pairs={{0,3},{1,0},{2,1},{3,2},{4,7},{5,4},{6,5},{7,6},{8,11},{9,8},{10,9... | collective-permute-start | bytes 786440 | tf_op jit(solution)/shard_map/ppermute | solution.py:378
  30.0 4.9 %collective-permute-start.1 = (bf16[1,256,256]{2,1,0:T(8,128)(2,1)S(1)}, bf16[1,256,256]{2,1,0:T(8,128)(2,1)S(1)}, u32[]{:S(2)}, u32[]{:S(2)}) collective-permute-start(bf16[1,256,256]{2,1,0:T(8,128)(2,1)S(1)} %copy-done.2), channel_id=1, source_target_pairs={{0,8},{4,12},{8,0},{12,4},{1,9},{5,13},{9,1},{13,5},{2,10},{6,14},... | collective-permute-start | bytes 393224 | tf_op jit(solution)/shard_map/ppermute | solution.py:325
  31.3 6.7 %collective-permute-start.2 = (bf16[1,256,256]{2,1,0:T(8,128)(2,1)S(1)}, bf16[1,256,256]{2,1,0:T(8,128)(2,1)S(1)}, u32[]{:S(2)}, u32[]{:S(2)}) collective-permute-start(bf16[1,256,256]{2,1,0:T(8,128)(2,1)S(1)} %copy-done.1), channel_id=1, source_target_pairs={{0,12},{4,8},{8,4},{12,0},{1,13},{5,9},{9,5},{13,1},{2,14},{6,10},... | collective-permute-start | bytes 393224 | tf_op jit(solution)/shard_map/ppermute | solution.py:325

commit v9 on v8

--- a/solution.py
+++ b/solution.py
@@ -74,18 +74,21 @@
     tiles = [
         pltpu.make_async_copy(sources[-1].at[s], local[-1].at[s], sems.at[n_in - 1 + s]) for s in range(slots)
     ]
-    for copy in copies + tiles:
+    early, large = copies[:8] + copies[12:], copies[8:12]
+    for copy in early + large + tiles:
         copy.start()
     owner, local_id, valid, visit, inv_var, coef, kx, ky, to_col, to_row, from_col, from_row, tap_col, tap_row, patch = local
-    for copy in copies:
+    for copy in early:
         copy.wait()
     side = patch.shape[1]
     row_waves[...] = dot(tap_row[...], ky[...], ((1,), (1,)))
     col_waves[...] = (dot(kx[...], tap_col[...]) * plan["scale"]).astype(BF16)
     band = lax.axis_index("band")
-    for phase in range(nb):
-        start = pl.multiple_of(plan["chunk"](band, phase) * rows, rows)
-        back[phase * rows : (phase + 1) * rows, :] = from_row[pl.ds(start, rows), :]
+    def place_back():
+        for phase in range(nb):
+            start = pl.multiple_of(plan["chunk"](band, phase) * rows, rows)
+            back[phase * rows : (phase + 1) * rows, :] = from_row[pl.ds(start, rows), :]
+
     heads[...] = jnp.full(heads.shape, -1.0, F32)
     me = lax.axis_index("sky")
     basis = kx.shape[0]
@@ -124,14 +127,18 @@
             for index in range(plan["sky"]):
                 pl.when(box == index)(functools.partial(store, index))
 
+    mixed = [(row_waves[...] * mixing(s)).astype(BF16) for s in range(slots)]
+    all_tables = dot(jnp.concatenate(mixed, axis=0), col_waves[...])
+    for copy in large:
+        copy.wait()
+    place_back()
     for batch in range(0, slots, BATCH):
         group = range(batch, min(batch + BATCH, slots))
         for s in group:
             tiles[s].wait()
         masked = [jnp.where(row_ids < valid[0, s], patch[s], 0.0).astype(BF16) for s in group]
-        mixed = [(row_waves[...] * mixing(s)).astype(BF16) for s in group]
         col = dot(jnp.concatenate(masked, axis=0), to_col[...]).astype(BF16)
-        tables = dot(jnp.concatenate(mixed, axis=0), col_waves[...])
+        tables = all_tables[batch * 2 * sub : (batch + len(group)) * 2 * sub]
         cos, sin = [], []
         for n, s in enumerate(group):
             mine = col[n * side : (n + 1) * side]

time: 47.4 us -> 47.1 us (level)
  the two profiles are of different devices: /device:TPU:13 before, /device:TPU:9 now
where the time goes in v9:
time: 47.1 us; the launch traced here: 46.9 us
  waiting for transfers between devices  19.6 us (42%)
  Pallas kernels  13.4 us (28%)
  starting transfers between devices  12.1 us (26%)
  local copies, waits for them, and re-layouts  1.05 us (2%)
  between operations  0.72 us (2%)
    ppermute x9, waiting for transfers between devices, per_device(): lax.ppermute(a, 'sky', [(i, i ^ r) for i in range(sky)])  13.4 us
    ppermute x9, starting transfers between devices, per_device(): lax.ppermute(a, 'sky', [(i, i ^ r) for i in range(sky)])  8.36 us
    pallas_call x1, Pallas kernels, per_device(): pl.pallas_call(functools.partial(convolve_kernel, plan), out_shape=out_sh...  7.12 us
    ppermute x3, waiting for transfers between devices, per_device(): lax.ppermute(extra, 'band', [(b, chunk(b, phase)) for b in range(nb)])  6.14 us
    pallas_call x4, Pallas kernels, per_device(): pl.pallas_call(functools.partial(sum_kernel, plan, phase), out_shape=outs...  5.4 us
    ppermute x3, starting transfers between devices, per_device(): lax.ppermute(extra, 'band', [(b, chunk(b, phase)) for b in range(nb)])  3.75 us
    unnamed x6, local copies, waits for them, and re-layouts  1.05 us
  transfers between devices with their start and end apart: 12, of which 8 were waited for; matrix products, arithmetic and copies ran while one was open for 0% of the time, Pallas kernels for 12%

profile of v9, /device:TPU:9, one launch (start us, length us, event | category | flops | bytes accessed | tf_op | source)
XLA Modules:
  0.0 46.9 jit_solution(5864221282802323178)
XLA Ops:
  0.6 7.1 %convolve.1 = (bf16[1,1040,256]{2,1,0:T(8,128)(2,1)}, bf16[1,1040,256]{2,1,0:T(8,128)(2,1)}, bf16[1,272,256]{2,1,0:T(8,128)(2,1)}, bf16[1,272,256]{2,1,0:T(8,128...) custom-call(s32[1,8]{1,0:T(1,128)} %bitcast.7, ...), custom_call_target="tpu_custom_call" | custom-call | flops 2952790016 | bytes 3145728 | tf_op jit(solution)/shard_map/convolve/pallas_call | solution.py:315
  7.8 0.7 %collective-permute-start = (bf16[1,1040,256]{2,1,0:T(8,128)(2,1)}, bf16[1,1040,256]{2,1,0:T(8,128)(2,1)S(1)}, u32[]{:S(2)}, u32[]{:S(2)}) collective-permute-start(bf16[1,1040,256]{2,1,0:T(8,128)(2,1)} %get-tuple-element.31), channel_id=1, source_target_pairs={{0,4},{4,0},{8,12},{12,8},{1,5},{5,1},{9,13},{13,9},{2,6},{6,2},{1... | collective-permute-start | bytes 1597448 | tf_op jit(solution)/shard_map/ppermute | solution.py:332
  8.5 1.2 %collective-permute-start.3 = (bf16[1,272,256]{2,1,0:T(8,128)(2,1)}, bf16[1,272,256]{2,1,0:T(8,128)(2,1)S(1)}, u32[]{:S(2)}, u32[]{:S(2)}) collective-permute-start(bf16[1,272,256]{2,1,0:T(8,128)(2,1)} %get-tuple-element.34), channel_id=1, source_target_pairs={{0,8},{4,12},{8,0},{12,4},{1,9},{5,13},{9,1},{13,5},{2,10},{6,14},... | collective-permute-start | bytes 417800 | tf_op jit(solution)/shard_map/ppermute | solution.py:332
  10.2 1.0 %copy-done = bf16[1,1040,256]{2,1,0:T(8,128)(2,1)S(1)} copy-done((bf16[1,1040,256]{2,1,0:T(8,128)(2,1)S(1)}, bf16[1,1040,256]{2,1,0:T(8,128)(2,1)}, u32[]{:S(2)}) %copy-start) | copy-done | bytes 532504
  11.3 1.3 %collective-permute-start.5 = (bf16[1,256,256]{2,1,0:T(8,128)(2,1)}, bf16[1,256,256]{2,1,0:T(8,128)(2,1)S(1)}, u32[]{:S(2)}, u32[]{:S(2)}) collective-permute-start(bf16[1,256,256]{2,1,0:T(8,128)(2,1)} %get-tuple-element.39), channel_id=1, source_target_pairs={{0,8},{4,12},{8,0},{12,4},{1,9},{5,13},{9,1},{13,5},{2,10},{6,14},... | collective-permute-start | bytes 393224 | tf_op jit(solution)/shard_map/ppermute | solution.py:332
  12.6 0.6 %collective-permute-start.6 = (bf16[1,256,256]{2,1,0:T(8,128)(2,1)}, bf16[1,256,256]{2,1,0:T(8,128)(2,1)S(1)}, u32[]{:S(2)}, u32[]{:S(2)}) collective-permute-start(bf16[1,256,256]{2,1,0:T(8,128)(2,1)} %get-tuple-element.40), channel_id=1, source_target_pairs={{0,12},{4,8},{8,4},{12,0},{1,13},{5,9},{9,5},{13,1},{2,14},{6,10},... | collective-permute-start | bytes 393224 | tf_op jit(solution)/shard_map/ppermute | solution.py:332
  13.2 0.8 %collective-permute-done.3.refs_2_ = bf16[1,272,256]{2,1,0:T(8,128)(2,1)S(1)} collective-permute-done((bf16[1,272,256]{2,1,0:T(8,128)(2,1)}, bf16[1,272,256]{2,1,0:T(8,128)(2,1)S(1)}, u32[]{:S(2)}, u32[]{:S(2)}) %collective-permute-start.3) | collective-permute-done | bytes 139296 | tf_op jit(solution)/shard_map/ppermute | solution.py:332
  14.0 1.2 %collective-permute-start.7 = (bf16[1,256,256]{2,1,0:T(8,128)(2,1)}, bf16[1,256,256]{2,1,0:T(8,128)(2,1)S(1)}, u32[]{:S(2)}, u32[]{:S(2)}) collective-permute-start(bf16[1,256,256]{2,1,0:T(8,128)(2,1)} %get-tuple-element.42), channel_id=1, source_target_pairs={{0,8},{4,12},{8,0},{12,4},{1,9},{5,13},{9,1},{13,5},{2,10},{6,14},... | collective-permute-start | bytes 393224 | tf_op jit(solution)/shard_map/ppermute | solution.py:332
  15.2 2.4 %collective-permute-done.4.refs_3_ = bf16[1,272,256]{2,1,0:T(8,128)(2,1)S(1)} collective-permute-done((bf16[1,272,256]{2,1,0:T(8,128)(2,1)}, bf16[1,272,256]{2,1,0:T(8,128)(2,1)S(1)}, u32[]{:S(2)}, u32[]{:S(2)}) %collective-permute-start.4) | collective-permute-done | bytes 139296 | tf_op jit(solution)/shard_map/ppermute | solution.py:332
  17.6 0.9 %collective-permute-start.8 = (bf16[1,256,256]{2,1,0:T(8,128)(2,1)}, bf16[1,256,256]{2,1,0:T(8,128)(2,1)S(1)}, u32[]{:S(2)}, u32[]{:S(2)}) collective-permute-start(bf16[1,256,256]{2,1,0:T(8,128)(2,1)} %get-tuple-element.43), channel_id=1, source_target_pairs={{0,12},{4,8},{8,4},{12,0},{1,13},{5,9},{9,5},{13,1},{2,14},{6,10},... | collective-permute-start | bytes 393224 | tf_op jit(solution)/shard_map/ppermute | solution.py:332
  18.4 1.5 %add_up.4 = (f32[8,64,256]{2,1,0:T(8,128)S(1)}, bf16[8,64,256]{2,1,0:T(8,128)(2,1)S(1)}, s32[4,128]{1,0:T(4,128)S(1)}, f32[4,128]{1,0:T(4,128)S(1)}) custom-call(bf16[1,1040,256]{2,1,0:T(8,128)(2,1)S(1)} %bring.1.refs_0_, bf16[1,1040,256]{2,1,0:T(8,128)(2,1)S(1)} %collective-permute-done.refs_1_, bf16[1,272,256]{2,1,0:T(8,128)(2,1)S(1)} %collective-permute-done.3.refs_2_, ...), custom_call_target="tpu_custom_call" | custom-call | flops 524288 | bytes 1572864 | tf_op jit(solution)/shard_map/add_up/pallas_call | solution.py:371
  19.9 1.4 %collective-permute-start.9 = (bf16[8,64,256]{2,1,0:T(8,128)(2,1)S(1)}, bf16[8,64,256]{2,1,0:T(8,128)(2,1)S(1)}, u32[]{:S(2)}, u32[]{:S(2)}) collective-permute-start(bf16[8,64,256]{2,1,0:T(8,128)(2,1)S(1)} %get-tuple-element.47), channel_id=1, source_target_pairs={{0,1},{1,2},{2,3},{3,0},{4,5},{5,6},{6,7},{7,4},{8,9},{9,10},{10,1... | collective-permute-start | bytes 786440 | tf_op jit(solution)/shard_map/ppermute | solution.py:385
  21.3 1.9 %collective-permute-done.6.refs_3_ = bf16[1,256,256]{2,1,0:T(8,128)(2,1)S(1)} collective-permute-done((bf16[1,256,256]{2,1,0:T(8,128)(2,1)}, bf16[1,256,256]{2,1,0:T(8,128)(2,1)S(1)}, u32[]{:S(2)}, u32[]{:S(2)}) %collective-permute-start.6) | collective-permute-done | bytes 131104 | tf_op jit(solution)/shard_map/ppermute | solution.py:332
  23.2 0.9 %add_up.5 = (f32[8,64,256]{2,1,0:T(8,128)S(1)}, bf16[8,64,256]{2,1,0:T(8,128)(2,1)S(1)}) custom-call(bf16[1,1040,256]{2,1,0:T(8,128)(2,1)S(1)} %bring.1.refs_0_, bf16[1,1040,256]{2,1,0:T(8,128)(2,1)S(1)} %collective-permute-done.refs_1_, bf16[1,256,256]{2,1,0:T(8,128)(2,1)S(1)} %collective-permute-done.5.refs_2_, ...), custom_call_target="tpu_custom_call" | custom-call | flops 524288 | bytes 1572864 | tf_op jit(solution)/shard_map/add_up/pallas_call | solution.py:371
  24.1 2.3 %collective-permute-start.10 = (bf16[8,64,256]{2,1,0:T(8,128)(2,1)S(1)}, bf16[8,64,256]{2,1,0:T(8,128)(2,1)S(1)}, u32[]{:S(2)}, u32[]{:S(2)}) collective-permute-start(bf16[8,64,256]{2,1,0:T(8,128)(2,1)S(1)} %get-tuple-element.49), channel_id=1, source_target_pairs={{0,2},{1,3},{2,0},{3,1},{4,6},{5,7},{6,4},{7,5},{8,10},{9,11},{10,... | collective-permute-start | bytes 786440 | tf_op jit(solution)/shard_map/ppermute | solution.py:385
  26.4 2.2 %collective-permute-done.8.refs_3_ = bf16[1,256,256]{2,1,0:T(8,128)(2,1)S(1)} collective-permute-done((bf16[1,256,256]{2,1,0:T(8,128)(2,1)}, bf16[1,256,256]{2,1,0:T(8,128)(2,1)S(1)}, u32[]{:S(2)}, u32[]{:S(2)}) %collective-permute-start.8) | collective-permute-done | bytes 131104 | tf_op jit(solution)/shard_map/ppermute | solution.py:332
  28.6 0.9 %add_up.6 = (f32[8,64,256]{2,1,0:T(8,128)S(1)}, bf16[8,64,256]{2,1,0:T(8,128)(2,1)S(1)}) custom-call(bf16[1,1040,256]{2,1,0:T(8,128)(2,1)S(1)} %bring.1.refs_0_, bf16[1,1040,256]{2,1,0:T(8,128)(2,1)S(1)} %collective-permute-done.refs_1_, bf16[1,256,256]{2,1,0:T(8,128)(2,1)S(1)} %collective-permute-done.7.refs_2_, ...), custom_call_target="tpu_custom_call" | custom-call | flops 524288 | bytes 1572864 | tf_op jit(solution)/shard_map/add_up/pallas_call | solution.py:371
  29.6 1.4 %collective-permute-start.1 = (bf16[1,256,256]{2,1,0:T(8,128)(2,1)S(1)}, bf16[1,256,256]{2,1,0:T(8,128)(2,1)S(1)}, u32[]{:S(2)}, u32[]{:S(2)}) collective-permute-start(bf16[1,256,256]{2,1,0:T(8,128)(2,1)S(1)} %copy-done.2), channel_id=1, source_target_pairs={{0,8},{4,12},{8,0},{12,4},{1,9},{5,13},{9,1},{13,5},{2,10},{6,14},... | collective-permute-start | bytes 393224 | tf_op jit(solution)/shard_map/ppermute | solution.py:332
  31.6 2.9 %collective-permute-done.1.refs_2_ = bf16[1,256,256]{2,1,0:T(8,128)(2,1)S(1)} collective-permute-done((bf16[1,256,256]{2,1,0:T(8,128)(2,1)S(1)}, bf16[1,256,256]{2,1,0:T(8,128)(2,1)S(1)}, u32[]{:S(2)}, u32[]{:S(2)}) %collective-permute-start.1) | collective-permute-done | bytes 131104 | tf_op jit(solution)/shard_map/ppermute | solution.py:332
  34.5 3.2 %collective-permute-done.2.refs_3_ = bf16[1,256,256]{2,1,0:T(8,128)(2,1)S(1)} collective-permute-done((bf16[1,256,256]{2,1,0:T(8,128)(2,1)S(1)}, bf16[1,256,256]{2,1,0:T(8,128)(2,1)S(1)}, u32[]{:S(2)}, u32[]{:S(2)}) %collective-permute-start.2) | collective-permute-done | bytes 131104 | tf_op jit(solution)/shard_map/ppermute | solution.py:332
  37.7 2.2 %add_up.7 = (f32[8,256,256]{2,1,0:T(8,128)}, f32[8,64,256]{2,1,0:T(8,128)S(1)}) custom-call(bf16[1,1040,256]{2,1,0:T(8,128)(2,1)S(1)} %bring.1.refs_0_, bf16[1,1040,256]{2,1,0:T(8,128)(2,1)S(1)} %collective-permute-done.refs_1_, bf16[1,256,256]{2,1,0:T(8,128)(2,1)S(1)} %collective-permute-done.1.refs_2_, ...), custom_call_target="tpu_custom_call" | custom-call | flops 524288 | bytes 1572864 | tf_op jit(solution)/shard_map/add_up/pallas_call | solution.py:371
  39.9 3.9 %collective-permute-done.10.refs_2_ = bf16[8,64,256]{2,1,0:T(8,128)(2,1)S(1)} collective-permute-done((bf16[8,64,256]{2,1,0:T(8,128)(2,1)S(1)}, bf16[8,64,256]{2,1,0:T(8,128)(2,1)S(1)}, u32[]{:S(2)}, u32[]{:S(2)}) %collective-permute-start.10) | collective-permute-done | bytes 262176 | tf_op jit(solution)/shard_map/ppermute | solution.py:385
  43.8 2.2 %collective-permute-done.11.refs_3_ = bf16[8,64,256]{2,1,0:T(8,128)(2,1)S(1)} collective-permute-done((bf16[8,64,256]{2,1,0:T(8,128)(2,1)S(1)}, bf16[8,64,256]{2,1,0:T(8,128)(2,1)S(1)}, u32[]{:S(2)}, u32[]{:S(2)}) %collective-permute-start.11) | collective-permute-done | bytes 262176 | tf_op jit(solution)/shard_map/ppermute | solution.py:385
  46.0 0.9 %accumulate.1 = f32[8,64,256]{2,1,0:T(8,128)} custom-call(f32[8,64,256]{2,1,0:T(8,128)S(1)} %get-tuple-element.50.refs_0_, bf16[8,64,256]{2,1,0:T(8,128)(2,1)S(1)} %collective-permute-done.9.refs_1_, bf16[8,64,256]{2,1,0:T(8,128)(2,1)S(1)} %collective-permute-done.10.refs_2_, bf16[8,64,256]{2,1,0:T(8,128)(2,1)S(1)} %collective-permute-done.11.refs_3_), custom_call_target="tpu_custom_call" | custom-call | tf_op jit(solution)/shard_map/accumulate/pallas_call | solution.py:390
  (13 shorter events, 1.2 us)
Async XLA Ops:
  7.8 10.7 %collective-permute-start = (bf16[1,1040,256]{2,1,0:T(8,128)(2,1)}, bf16[1,1040,256]{2,1,0:T(8,128)(2,1)S(1)}, u32[]{:S(2)}, u32[]{:S(2)}) collective-permute-start(bf16[1,1040,256]{2,1,0:T(8,128)(2,1)} %get-tuple-element.31), channel_id=1, source_target_pairs={{0,4},{4,0},{8,12},{12,8},{1,5},{5,1},{9,13},{13,9},{2,6},{6,2},{1... | collective-permute-start | bytes 1597448 | tf_op jit(solution)/shard_map/ppermute | solution.py:332
  8.5 5.5 %collective-permute-start.3 = (bf16[1,272,256]{2,1,0:T(8,128)(2,1)}, bf16[1,272,256]{2,1,0:T(8,128)(2,1)S(1)}, u32[]{:S(2)}, u32[]{:S(2)}) collective-permute-start(bf16[1,272,256]{2,1,0:T(8,128)(2,1)} %get-tuple-element.34), channel_id=1, source_target_pairs={{0,8},{4,12},{8,0},{12,4},{1,9},{5,13},{9,1},{13,5},{2,10},{6,14},... | collective-permute-start | bytes 417800 | tf_op jit(solution)/shard_map/ppermute | solution.py:332
  9.7 7.8 %collective-permute-start.4 = (bf16[1,272,256]{2,1,0:T(8,128)(2,1)}, bf16[1,272,256]{2,1,0:T(8,128)(2,1)S(1)}, u32[]{:S(2)}, u32[]{:S(2)}) collective-permute-start(bf16[1,272,256]{2,1,0:T(8,128)(2,1)} %get-tuple-element.35), channel_id=1, source_target_pairs={{0,12},{4,8},{8,4},{12,0},{1,13},{5,9},{9,5},{13,1},{2,14},{6,10},... | collective-permute-start | bytes 417800 | tf_op jit(solution)/shard_map/ppermute | solution.py:332
  10.2 1.0 %copy-start = (bf16[1,1040,256]{2,1,0:T(8,128)(2,1)S(1)}, bf16[1,1040,256]{2,1,0:T(8,128)(2,1)}, u32[]{:S(2)}) copy-start(bf16[1,1040,256]{2,1,0:T(8,128)(2,1)} %get-tuple-element.28.source) | copy-start | bytes 1597444
  11.3 18.3 %copy-start.2 = (bf16[1,256,256]{2,1,0:T(8,128)(2,1)S(1)}, bf16[1,256,256]{2,1,0:T(8,128)(2,1)}, u32[]{:S(2)}) copy-start(bf16[1,256,256]{2,1,0:T(8,128)(2,1)} %get-tuple-element.32) | copy-start | bytes 393220
  11.3 19.7 %copy-start.1 = (bf16[1,256,256]{2,1,0:T(8,128)(2,1)S(1)}, bf16[1,256,256]{2,1,0:T(8,128)(2,1)}, u32[]{:S(2)}) copy-start(bf16[1,256,256]{2,1,0:T(8,128)(2,1)} %get-tuple-element.33) | copy-start | bytes 393220
  11.3 10.0 %collective-permute-start.5 = (bf16[1,256,256]{2,1,0:T(8,128)(2,1)}, bf16[1,256,256]{2,1,0:T(8,128)(2,1)S(1)}, u32[]{:S(2)}, u32[]{:S(2)}) collective-permute-start(bf16[1,256,256]{2,1,0:T(8,128)(2,1)} %get-tuple-element.39), channel_id=1, source_target_pairs={{0,8},{4,12},{8,0},{12,4},{1,9},{5,13},{9,1},{13,5},{2,10},{6,14},... | collective-permute-start | bytes 393224 | tf_op jit(solution)/shard_map/ppermute | solution.py:332
  12.6 10.6 %collective-permute-start.6 = (bf16[1,256,256]{2,1,0:T(8,128)(2,1)}, bf16[1,256,256]{2,1,0:T(8,128)(2,1)S(1)}, u32[]{:S(2)}, u32[]{:S(2)}) collective-permute-start(bf16[1,256,256]{2,1,0:T(8,128)(2,1)} %get-tuple-element.40), channel_id=1, source_target_pairs={{0,12},{4,8},{8,4},{12,0},{1,13},{5,9},{9,5},{13,1},{2,14},{6,10},... | collective-permute-start | bytes 393224 | tf_op jit(solution)/shard_map/ppermute | solution.py:332
  14.0 12.4 %collective-permute-start.7 = (bf16[1,256,256]{2,1,0:T(8,128)(2,1)}, bf16[1,256,256]{2,1,0:T(8,128)(2,1)S(1)}, u32[]{:S(2)}, u32[]{:S(2)}) collective-permute-start(bf16[1,256,256]{2,1,0:T(8,128)(2,1)} %get-tuple-element.42), channel_id=1, source_target_pairs={{0,8},{4,12},{8,0},{12,4},{1,9},{5,13},{9,1},{13,5},{2,10},{6,14},... | collective-permute-start | bytes 393224 | tf_op jit(solution)/shard_map/ppermute | solution.py:332
  17.6 11.1 %collective-permute-start.8 = (bf16[1,256,256]{2,1,0:T(8,128)(2,1)}, bf16[1,256,256]{2,1,0:T(8,128)(2,1)S(1)}, u32[]{:S(2)}, u32[]{:S(2)}) collective-permute-start(bf16[1,256,256]{2,1,0:T(8,128)(2,1)} %get-tuple-element.43), channel_id=1, source_target_pairs={{0,12},{4,8},{8,4},{12,0},{1,13},{5,9},{9,5},{13,1},{2,14},{6,10},... | collective-permute-start | bytes 393224 | tf_op jit(solution)/shard_map/ppermute | solution.py:332
  19.9 19.9 %collective-permute-start.9 = (bf16[8,64,256]{2,1,0:T(8,128)(2,1)S(1)}, bf16[8,64,256]{2,1,0:T(8,128)(2,1)S(1)}, u32[]{:S(2)}, u32[]{:S(2)}) collective-permute-start(bf16[8,64,256]{2,1,0:T(8,128)(2,1)S(1)} %get-tuple-element.47), channel_id=1, source_target_pairs={{0,1},{1,2},{2,3},{3,0},{4,5},{5,6},{6,7},{7,4},{8,9},{9,10},{10,1... | collective-permute-start | bytes 786440 | tf_op jit(solution)/shard_map/ppermute | solution.py:385
  24.1 19.8 %collective-permute-start.10 = (bf16[8,64,256]{2,1,0:T(8,128)(2,1)S(1)}, bf16[8,64,256]{2,1,0:T(8,128)(2,1)S(1)}, u32[]{:S(2)}, u32[]{:S(2)}) collective-permute-start(bf16[8,64,256]{2,1,0:T(8,128)(2,1)S(1)} %get-tuple-element.49), channel_id=1, source_target_pairs={{0,2},{1,3},{2,0},{3,1},{4,6},{5,7},{6,4},{7,5},{8,10},{9,11},{10,... | collective-permute-start | bytes 786440 | tf_op jit(solution)/shard_map/ppermute | solution.py:385
  29.5 16.5 %collective-permute-start.11 = (bf16[8,64,256]{2,1,0:T(8,128)(2,1)S(1)}, bf16[8,64,256]{2,1,0:T(8,128)(2,1)S(1)}, u32[]{:S(2)}, u32[]{:S(2)}) collective-permute-start(bf16[8,64,256]{2,1,0:T(8,128)(2,1)S(1)} %get-tuple-element.53), channel_id=1, source_target_pairs={{0,3},{1,0},{2,1},{3,2},{4,7},{5,4},{6,5},{7,6},{8,11},{9,8},{10,9... | collective-permute-start | bytes 786440 | tf_op jit(solution)/shard_map/ppermute | solution.py:385
  29.6 4.9 %collective-permute-start.1 = (bf16[1,256,256]{2,1,0:T(8,128)(2,1)S(1)}, bf16[1,256,256]{2,1,0:T(8,128)(2,1)S(1)}, u32[]{:S(2)}, u32[]{:S(2)}) collective-permute-start(bf16[1,256,256]{2,1,0:T(8,128)(2,1)S(1)} %copy-done.2), channel_id=1, source_target_pairs={{0,8},{4,12},{8,0},{12,4},{1,9},{5,13},{9,1},{13,5},{2,10},{6,14},... | collective-permute-start | bytes 393224 | tf_op jit(solution)/shard_map/ppermute | solution.py:332
  31.0 6.7 %collective-permute-start.2 = (bf16[1,256,256]{2,1,0:T(8,128)(2,1)S(1)}, bf16[1,256,256]{2,1,0:T(8,128)(2,1)S(1)}, u32[]{:S(2)}, u32[]{:S(2)}) collective-permute-start(bf16[1,256,256]{2,1,0:T(8,128)(2,1)S(1)} %copy-done.1), channel_id=1, source_target_pairs={{0,12},{4,8},{8,4},{12,0},{1,13},{5,9},{9,5},{13,1},{2,14},{6,10},... | collective-permute-start | bytes 393224 | tf_op jit(solution)/shard_map/ppermute | solution.py:332
